TPU v7x, 32 devices: a whole 2x2x4 slice. The times are simulated.
32 devices in a mesh: ctx: 16 (over z, y, x), dp: 2 (over core).
Axes of the slice: x: 2, y: 2, z: 4, core: 2. Of those that a mesh axis runs over, the one named last changes fastest.
Arguments:
- queries: bfloat16 [2, 2048, 1024], P('dp', 'ctx'), may hold values from -45 to 45
- key_rows: bfloat16 [2, 2048, 1024], P('dp', 'ctx'), may hold values from -6 to 6
- value_rows: bfloat16 [2, 2048, 1024], P('dp', 'ctx'), may hold values from -6 to 6
- out_grad: bfloat16 [2, 2048, 1024], P('dp', 'ctx'), may hold values from -6 to 6
- norm_gain: float32 [1024], replicated, may hold values from 0.25 to 1.75
- offsets: int32 [3, 8], replicated, may hold values from 0 to 7, as said below
Outputs:
- attended: bfloat16 [2, 2048, 1024], P('dp', 'ctx')
- query_grad: bfloat16 [2, 2048, 1024], P('dp', 'ctx')
- key_grad: bfloat16 [2, 2048, 1024], P('dp', 'ctx')
- value_grad: bfloat16 [2, 2048, 1024], P('dp', 'ctx')
- gain_grad: float32 [1024], replicated
Inputs may be any that keep to these rules, and one draw needn't show every extreme that they name: `offsets`: row l holds each head's offset at level l + 1, from 0 to that level's rate minus 1 (2, 8, 4); in every row some head has offset 0 and some head the rate minus 1.
All inputs are finite; a program needn't handle non-finite values.
Results may differ from a plain program's by a relative error of at most 0.0085.
Values may be sent and summed in bfloat16 or wider, within the bound.
No kernel may reach another device: no remote copies, remote signals or barrier semaphores. Data moves between devices by JAX's collectives and lax.ppermute only.
A program may use at most 64 MiB of HBM per device.

v0:
```python
import math

import jax
import jax.numpy as jnp
from jax import lax
from jax.sharding import PartitionSpec as P

H = 8
HD = 128
SPAN_A = 2
RATE_A = 1
SPAN_B = 4
RATE_B = 2
SPAN_C = 16
RATE_C = 8


EPSILON = 1e-05


def partner(value, axis, apart):
    mask = 2**apart
    pairs = [(source, source ^ mask) for source in range(lax.axis_size(axis))]
    return lax.ppermute(value, axis, pairs)


def head_mask(stride, chosen):
    return (jnp.arange(stride, dtype=jnp.int32)[None, :] == chosen[:, None]).reshape(
        chosen.shape[0], 1, stride, 1
    )


def pick_rows(tensor, stride, chosen):
    if chosen is None:
        return tensor
    grouped = tensor.reshape(tensor.shape[0], tensor.shape[1] // stride, stride, tensor.shape[2])
    return jnp.sum(
        jnp.where(head_mask(stride, chosen), grouped, jnp.zeros((), tensor.dtype)), axis=2
    )


def widen_rows(tensor, stride, chosen, filler):
    if chosen is None:
        return tensor
    widened = jnp.where(head_mask(stride, chosen), tensor[:, :, None, :], filler)
    return widened.reshape(tensor.shape[0], tensor.shape[1] * stride, tensor.shape[2])


def low_side(my_index, bit_number):
    return my_index // (1 << bit_number) % 2 == 0


def attach(mine, other, my_index, bit_number):
    return jnp.where(
        low_side(my_index, bit_number),
        jnp.concatenate([mine, other], axis=0),
        jnp.concatenate([other, mine], axis=0),
    )


def collect(blocks, level_bits, my_index):
    blocks = list(blocks)
    for level_id in range(len(blocks)):
        for bit_number in level_bits[level_id]:
            arrived = partner(blocks[level_id], "ctx", bit_number)
            blocks[level_id] = attach(blocks[level_id], arrived, my_index, bit_number)
    return blocks


def halves(buffer, my_index, bit_number):
    half_size = buffer.shape[0] // 2
    lower_half = buffer[:half_size]
    upper_half = buffer[half_size:]
    on_low = low_side(my_index, bit_number)
    return (
        jnp.where(on_low, lower_half, upper_half),
        jnp.where(on_low, upper_half, lower_half).astype(jnp.bfloat16),
    )


def release(buffers, level_bits, my_index):
    buffers = list(buffers)
    for level_id in range(len(buffers)):
        for bit_number in level_bits[level_id][::-1]:
            kept_half, sent_half = halves(buffers[level_id], my_index, bit_number)
            arrived = partner(sent_half, "ctx", bit_number)
            buffers[level_id] = kept_half + arrived.astype(jnp.float32)
    return [buffer[0] for buffer in buffers]


def flat_keys(block):
    members = block.shape[0]
    heads = block.shape[2]
    rows = block.shape[3]
    width = block.shape[4]
    arranged = jnp.transpose(block, (1, 2, 0, 3, 4))
    return arranged.reshape(2, heads, members * rows, width)


def shards(queries, key_rows, value_rows, out_grad, norm_gain, offsets):
    tokens_here = queries.shape[1]
    model_width = queries.shape[2]
    scale = HD ** (-0.5)
    ctx_count = lax.axis_size("ctx")
    my_index = lax.axis_index("ctx")
    plan = [
        (SPAN_A, RATE_A, None),
        (SPAN_B, RATE_B, offsets[0]),
        (SPAN_C, RATE_C, offsets[1]),
        (ctx_count // 2, ctx_count // 4, offsets[2]),
    ]
    top_bits = max((span_size.bit_length() - 1 for span_size, stride, chosen in plan))
    sequence = list(range(top_bits))
    level_bits = [
        [bit_number for bit_number in sequence if bit_number < span_size.bit_length() - 1]
        for span_size, stride, chosen in plan
    ]
    query_heads = jnp.transpose(queries[0].reshape(tokens_here, H, HD), (1, 0, 2))
    key_heads = jnp.transpose(key_rows[0].reshape(tokens_here, H, HD), (1, 0, 2))
    value_heads = jnp.transpose(value_rows[0].reshape(tokens_here, H, HD), (1, 0, 2))
    blocks = [
        jnp.stack([pick_rows(key_heads, stride, chosen), pick_rows(value_heads, stride, chosen)])[
            None
        ]
        for span_size, stride, chosen in plan
    ]
    blocks = collect(blocks, level_bits, my_index)
    members = [block.shape[0] for block in blocks]
    flats = [flat_keys(block) for block in blocks]
    maxima = []
    totals = []
    weighted = []
    for level_id, (span_size, stride, chosen) in enumerate(plan):
        act_q = pick_rows(query_heads, stride, chosen)
        scores = (
            jnp.einsum(
                "hqd,hkd->hqk", act_q, flats[level_id][0], preferred_element_type=jnp.float32
            )
            * scale
        )
        level_max = jnp.max(scores, axis=-1)
        weights = jnp.exp(scores - level_max[..., None])
        level_total = jnp.sum(weights, axis=-1)
        level_sum = jnp.einsum(
            "hqk,hkd->hqd",
            weights.astype(jnp.bfloat16),
            flats[level_id][1],
            preferred_element_type=jnp.float32,
        )
        maxima.append(widen_rows(level_max[..., None], stride, chosen, -jnp.inf)[..., 0])
        totals.append(widen_rows(level_total[..., None], stride, chosen, 0.0)[..., 0])
        weighted.append(widen_rows(level_sum, stride, chosen, 0.0))
    maxima = jnp.stack(maxima)
    top_max = jnp.max(maxima, axis=0)
    factors = jnp.exp(maxima - top_max[None])
    total = jnp.sum(factors * jnp.stack(totals), axis=0)
    mixed = jnp.sum(factors[..., None] * jnp.stack(weighted), axis=0) / total[..., None]
    attn = jnp.transpose(mixed, (1, 0, 2)).reshape(tokens_here, model_width).astype(jnp.bfloat16)
    log_total = top_max + jnp.log(total)
    features = attn.astype(jnp.float32)
    centered = features - jnp.mean(features, axis=-1, keepdims=True)
    inverse = lax.rsqrt(jnp.mean(centered * centered, axis=-1, keepdims=True) + EPSILON)
    normed = centered * inverse
    attended = (normed * norm_gain).astype(jnp.bfloat16)
    upstream = out_grad[0].astype(jnp.float32)
    scaled = upstream * norm_gain
    attn_grad = (
        inverse
        * (
            scaled
            - jnp.mean(scaled, axis=-1, keepdims=True)
            - normed * jnp.mean(scaled * normed, axis=-1, keepdims=True)
        )
    ).astype(jnp.bfloat16)
    gain_part = jnp.sum(upstream * normed, axis=0)
    gain_sum = lax.psum(gain_part, ("ctx", "dp"))
    gain_grad = gain_sum / math.sqrt(lax.axis_size("ctx") * lax.axis_size("dp") * tokens_here)
    correction = jnp.sum(
        (attn_grad.astype(jnp.float32) * features).reshape(tokens_here, H, HD), axis=-1
    ).T
    grad_heads = jnp.transpose(attn_grad.reshape(tokens_here, H, HD), (1, 0, 2))
    query_grad = jnp.zeros((H, tokens_here, HD), jnp.float32)
    buffers = []
    for level_id, (span_size, stride, chosen) in enumerate(plan):
        act_q = pick_rows(query_heads, stride, chosen)
        act_g = pick_rows(grad_heads, stride, chosen)
        act_log = pick_rows(log_total[..., None], stride, chosen)[..., 0]
        act_corr = pick_rows(correction[..., None], stride, chosen)[..., 0]
        key_block = flats[level_id][0]
        value_block = flats[level_id][1]
        scores = (
            jnp.einsum("hqd,hkd->hqk", act_q, key_block, preferred_element_type=jnp.float32) * scale
        )
        probs = jnp.exp(scores - act_log[..., None])
        value_part = jnp.einsum(
            "hqk,hqd->hkd", probs.astype(jnp.bfloat16), act_g, preferred_element_type=jnp.float32
        )
        prob_grad = jnp.einsum(
            "hqd,hkd->hqk", act_g, value_block, preferred_element_type=jnp.float32
        )
        score_grad = (probs * (prob_grad - act_corr[..., None])).astype(jnp.bfloat16)
        query_part = (
            jnp.einsum("hqk,hkd->hqd", score_grad, key_block, preferred_element_type=jnp.float32)
            * scale
        )
        query_grad = query_grad + widen_rows(query_part, stride, chosen, 0.0)
        key_part = (
            jnp.einsum("hqk,hqd->hkd", score_grad, act_q, preferred_element_type=jnp.float32)
            * scale
        )
        both_parts = jnp.stack([key_part, value_part]).reshape(
            2, H, members[level_id], key_part.shape[1] // members[level_id], HD
        )
        buffers.append(jnp.transpose(both_parts, (2, 0, 1, 3, 4)))
    owned = release(buffers, level_bits, my_index)
    key_grad = jnp.zeros((H, tokens_here, HD), jnp.float32)
    value_grad = jnp.zeros((H, tokens_here, HD), jnp.float32)
    for level_id, (span_size, stride, chosen) in enumerate(plan):
        key_grad = key_grad + widen_rows(owned[level_id][0], stride, chosen, 0.0)
        value_grad = value_grad + widen_rows(owned[level_id][1], stride, chosen, 0.0)

    def rows_out(tensor):
        return (
            jnp.transpose(tensor, (1, 0, 2))
            .reshape(tokens_here, model_width)
            .astype(jnp.bfloat16)[None]
        )

    return (
        attended[None],
        rows_out(query_grad),
        rows_out(key_grad),
        rows_out(value_grad),
        gain_grad,
    )


def solution(mesh):
    return jax.shard_map(
        shards,
        mesh=mesh,
        in_specs=(
            P("dp", "ctx", None),
            P("dp", "ctx", None),
            P("dp", "ctx", None),
            P("dp", "ctx", None),
            P(),
            P(),
        ),
        out_specs=(
            P("dp", "ctx", None),
            P("dp", "ctx", None),
            P("dp", "ctx", None),
            P("dp", "ctx", None),
            P(),
        ),
        check_vma=False,
    )
```

profile of v0, /device:TPU:0, one launch (start us, length us, event | category | flops | bytes accessed | tf_op | source)
XLA Modules:
  0.0 198.3 jit_solution(14141206604714049037)
XLA Ops:
  4.8 1.8 select_reduce_fusion.3
  6.6 3.0 %collective-permute-start.7 = (bf16[1,2,8,32,128]{4,3,0,2,1:T(8,128)(2,1)S(1)}, bf16[1,2,8,32,128]{4,3,0,2,1:T(8,128)(2,1)S(1)}, u32[]{:S(2)}, u32[]{:S(2)}) collective-permute-start(bf16[1,2,8,32,128]{4,3,0,2,1:T(8,128)(2,1)S(1)} %maximum_bitcast_fusion.6), channel_id=1, source_target_pairs={{0,2},{2,0},{4,6},{6,4},{8,10},{10,8},{12,14},{14,12},{16,18},{18,... | collective-permute-start | bytes 393224 | tf_op jit(solution)/shard_map/ppermute | solution.py:24
  9.7 1.2 fusion.65
  11.1 2.2 %fusion.58 = (bf16[8,64,128]{2,1,0:T(8,128)(2,1)S(1)}, bf16[8,64,128]{2,1,0:T(8,128)(2,1)S(1)}, bf16[8,64,128]{2,1,0:T(8,128)(2,1)S(1)}) fusion(bf16[8,64,2,128]{3,2,1,0:T(2,128)(2,1)S(1)} %bitcast.317, pred[8,2]{1,0:T(8,128)(4,1)S(1)} %copy.100, bf16[8,64,2,128]{3,2,1,0:T(2,128)(2,1)S(1)} %bitcast.321, bf16[8,64,2,128]{3,2,1,0:T(2,128)(2,1)S(1)} %bitcast.319), kind=kLoop, calls=%fused_computation.119 | loop fusion | flops 589824 | bytes 1179664 | tf_op jit(solution)/shard_map/reduce_sum | solution.py:37
  13.3 2.1 %collective-permute-start.1 = (bf16[1,2,8,64,128]{4,3,0,2,1:T(8,128)(2,1)S(1)}, bf16[1,2,8,64,128]{4,3,0,2,1:T(8,128)(2,1)}, u32[]{:S(2)}, u32[]{:S(2)}) collective-permute-start(bf16[1,2,8,64,128]{4,3,0,2,1:T(8,128)(2,1)S(1)} %maximum_bitcast_fusion.5), channel_id=1, source_target_pairs={{0,2},{2,0},{4,6},{6,4},{8,10},{10,8},{12,14},{14,12},{16,18},{18,... | collective-permute-start | bytes 786440 | tf_op jit(solution)/shard_map/ppermute | solution.py:24
  15.6 2.1 %collective-permute-start.4 = (bf16[2,2,8,16,128]{4,3,0,2,1:T(8,128)(2,1)S(1)}, bf16[2,2,8,16,128]{4,3,0,2,1:T(8,128)(2,1)S(1)}, u32[]{:S(2)}, u32[]{:S(2)}) collective-permute-start(bf16[2,2,8,16,128]{4,3,0,2,1:T(8,128)(2,1)S(1)} %maximum_select_fusion.9), channel_id=1, source_target_pairs={{0,4},{2,6},{4,0},{6,2},{8,12},{10,14},{12,8},{14,10},{16,20},{18,... | collective-permute-start | bytes 393224 | tf_op jit(solution)/shard_map/ppermute | solution.py:24
  18.0 4.0 %collective-permute-done.4 = bf16[2,2,8,16,128]{4,3,0,2,1:T(8,128)(2,1)S(1)} collective-permute-done((bf16[2,2,8,16,128]{4,3,0,2,1:T(8,128)(2,1)S(1)}, bf16[2,2,8,16,128]{4,3,0,2,1:T(8,128)(2,1)S(1)}, u32[]{:S(2)}, u32[]{:S(2)}) %collective-permute-start.4) | collective-permute-done | bytes 131104 | tf_op jit(solution)/shard_map/ppermute | solution.py:24
  22.1 2.1 %collective-permute-start.5 = (bf16[4,2,8,16,128]{4,3,0,2,1:T(8,128)(2,1)S(1)}, bf16[4,2,8,16,128]{4,3,0,2,1:T(8,128)(2,1)}, u32[]{:S(2)}, u32[]{:S(2)}) collective-permute-start(bf16[4,2,8,16,128]{4,3,0,2,1:T(8,128)(2,1)S(1)} %maximum_select_fusion.7), channel_id=1, source_target_pairs={{0,8},{2,10},{4,12},{6,14},{8,0},{10,2},{12,4},{14,6},{16,24},{18,... | collective-permute-start | bytes 786440 | tf_op jit(solution)/shard_map/ppermute | solution.py:24
  28.9 1.7 collective-permute-start.2
  31.8 1.9 maximum_select_fusion.5
  33.7 2.6 %collective-permute-start.6 = (bf16[8,2,8,16,128]{4,3,0,2,1:T(8,128)(2,1)}, bf16[8,2,8,16,128]{4,3,0,2,1:T(8,128)(2,1)}, u32[]{:S(2)}, u32[]{:S(2)}) collective-permute-start(bf16[8,2,8,16,128]{4,3,0,2,1:T(8,128)(2,1)} %maximum_select_fusion.5), channel_id=1, source_target_pairs={{0,16},{2,18},{4,20},{6,22},{8,24},{10,26},{12,28},{14,30},{16,0},... | collective-permute-start | bytes 1572872 | tf_op jit(solution)/shard_map/ppermute | solution.py:24
  40.2 1.3 fusion.15
  43.2 1.5 copy.122
  45.4 1.5 copy.110
  49.8 2.0 %collective-permute-done.9 = bf16[4,2,8,32,128]{4,3,0,2,1:T(8,128)(2,1)} collective-permute-done((bf16[4,2,8,32,128]{4,3,0,2,1:T(8,128)(2,1)}, bf16[4,2,8,32,128]{4,3,0,2,1:T(8,128)(2,1)}, u32[]{:S(2)}, u32[]{:S(2)}) %collective-permute-start.9) | collective-permute-done | bytes 524320 | tf_op jit(solution)/shard_map/ppermute | solution.py:24
  51.8 1.7 fusion.17
  56.7 1.3 fusion.77
  59.1 1.7 fusion.16
  64.1 2.0 %fusion = f32[8,128,128]{2,1,0:T(8,128)S(1)} fusion(f32[1,8,128,128]{3,2,1,0:T(8,128)} %broadcast_select_fusion.4, f32[1,8,128,128]{3,2,1,0:T(8,128)S(1)} %bitcast_select_fusion, f32[1,8,128,128]{3,2,1,0:T(8,128)} %broadcast_select_fusion.5, f32[1,8,128,128]{3,2,1,0:T(8,128)} %convolution_bitcast_fusion, f32[4,8,128]{2,1,0:T(8,128)S(1)} %get-tuple-element.43), kind=kLoop, calls=%fused_computation.1 | loop fusion | flops 2490368 | bytes 2637824 | tf_op jit(solution)/shard_map/reduce_sum | solution.py:157
  70.5 1.9 fusion.26
  72.4 2.1 %fusion.62 = (bf16[8,16,128]{2,1,0:T(8,128)(2,1)}, bf16[128,8,128]{2,0,1:T(8,128)(2,1)S(1)}) fusion(pred[8,8]{1,0:T(8,128)(4,1)} %copy-done.78, f32[128]{0:T(128)S(1)} %broadcast_multiply_fusion.1, f32[128]{0:T(128)S(1)} %broadcast_multiply_fusion.3, bf16[128,8,128]{2,0,1:T(8,128)(2,1)S(1)} %get-tuple-element.41, f32[128]{0:T(128)S(1)} %broadcast_multiply_fusion.2, ...), kind=kLoop, calls=%fused_computation.129 | loop fusion | flops 1425408 | bytes 1087552 | tf_op jit(solution)/shard_map/reduce_sum | solution.py:37
  76.3 2.3 %fusion.3 = bf16[8,128,256]{1,2,0:T(8,128)(2,1)} fusion(bf16[8,256,128]{2,1,0:T(8,128)(2,1)} %bitcast.307, f32[8,128,256]{1,2,0:T(8,128)S(1)} %get-tuple-element.83, f32[8,128]{1,0:T(8,128)S(1)} %bitcast.369, f32[8,128]{1,0:T(8,128)} %get-tuple-element.67, bf16[128,8,128]{2,0,1:T(8,128)(2,1)S(1)} %get-tuple-element.39), kind=kOutput, calls=%fused_computation.14 | convolution fusion | flops 68157440 | bytes 2367488 | tf_op jit(solution)/shard_map/hqd,hkd->hqk/dot_general | solution.py:198
  78.6 2.0 %fusion.27 = f32[8,256,128]{2,1,0:T(8,128)} fusion(f32[8,128,256]{1,2,0:T(8,128)S(1)} %get-tuple-element.83, f32[8,128]{1,0:T(8,128)} %get-tuple-element.67, bf16[128,8,128]{2,0,1:T(8,128)(2,1)S(1)} %get-tuple-element.39), kind=kOutput, calls=%fused_computation.65 | convolution fusion | flops 67633152 | bytes 2363392 | tf_op jit(solution)/shard_map/hqk,hqd->hkd/dot_general | solution.py:195
  81.5 1.5 fusion.75
  83.5 2.2 %convolution_multiply_fusion = f32[8,256,128]{2,1,0:T(8,128)} fusion(bf16[8,32,256]{2,1,0:T(8,128)(2,1)S(1)} %fusion.11, bf16[8,32,128]{2,1,0:T(8,128)(2,1)} %get-tuple-element.31), kind=kOutput, calls=%fused_computation.6 | convolution fusion | flops 17039360 | bytes 1245184 | tf_op jit(solution)/shard_map/hqk,hqd->hkd/dot_general | solution.py:208
  86.0 1.5 fusion.84
  88.0 1.4 convolution_multiply_fusion.1
  90.7 1.6 fusion.54
  92.8 1.3 convolution_multiply_fusion.4
  99.7 1.5 fusion.9
  102.1 1.3 copy.155
  103.4 1.4 copy.154
  104.8 1.5 maximum_bitcast_fusion
  106.5 1.5 collective-permute-start.10
  113.2 1.4 copy-done
  116.0 41.8 %psum.7 = f32[1024]{0:T(1024)S(1)} all-reduce(f32[1024]{0:T(1024)S(1)} %copy-done.73), channel_id=1, replica_groups=mesh['ctx'=16,'dp'=2] {'ctx','dp'}, use_global_device_ids=true, to_apply=%region_34.35 | all-reduce | flops 1024 | bytes 8192 | tf_op jit(solution)/shard_map/psum | solution.py:176
  159.3 2.1 %convert_add_fusion = f32[4,2,8,32,128]{4,3,0,2,1:T(8,128)S(1)} fusion(bf16[4,2,8,32,128]{4,3,0,2,1:T(8,128)(2,1)} %collective-permute-done.17, f32[8,2,8,32,128]{4,3,0,2,1:T(8,128)} %copy-done.4, pred[]{:T(512)S(6)} %eq.70), kind=kLoop, calls=%fused_computation.44 | loop fusion | flops 786432 | bytes 3670017 | tf_op jit(solution)/shard_map/add | solution.py:87
  161.5 2.3 %collective-permute-start.18 = (bf16[2,2,8,32,128]{4,3,0,2,1:T(8,128)(2,1)S(1)}, bf16[2,2,8,32,128]{4,3,0,2,1:T(8,128)(2,1)S(1)}, u32[]{:S(2)}, u32[]{:S(2)}) collective-permute-start(bf16[2,2,8,32,128]{4,3,0,2,1:T(8,128)(2,1)S(1)} %select_convert_fusion.4), channel_id=1, source_target_pairs={{0,4},{2,6},{4,0},{6,2},{8,12},{10,14},{12,8},{14,10},{16,20},{18,... | collective-permute-start | bytes 786440 | tf_op jit(solution)/shard_map/ppermute | solution.py:24
  163.8 1.3 convert_add_fusion.1
  165.2 1.3 collective-permute-start.14
  166.4 1.4 convert_add_fusion.2
  167.9 1.6 collective-permute-start.12
  173.5 2.5 %collective-permute-done.12 = bf16[1,2,8,64,128]{4,3,0,2,1:T(8,128)(2,1)S(1)} collective-permute-done((bf16[1,2,8,64,128]{4,3,0,2,1:T(8,128)(2,1)S(1)}, bf16[1,2,8,64,128]{4,3,0,2,1:T(8,128)(2,1)S(1)}, u32[]{:S(2)}, u32[]{:S(2)}) %collective-permute-start.12) | collective-permute-done | bytes 262176 | tf_op jit(solution)/shard_map/ppermute | solution.py:24
  179.3 1.2 copy.157
  188.4 2.0 %copy.163 = f32[8,128,128]{1,2,0:T(8,128)} copy(f32[8,128,128]{2,1,0:T(8,128)} %broadcast_bitcast_fusion) | data formatting | bytes 1048576 | tf_op jit(solution)/shard_map/jit(_where)/broadcast_in_dim | solution.py:45
  191.3 2.1 %copy.158 = f32[8,128,128]{1,2,0:T(8,128)} copy(f32[8,128,128]{2,1,0:T(8,128)} %broadcast_bitcast_fusion.1) | data formatting | bytes 1048576 | tf_op jit(solution)/shard_map/jit(_where)/broadcast_in_dim | solution.py:45
  193.4 2.3 %fusion.34 = (bf16[8,128,128]{1,2,0:T(8,128)(2,1)S(1)}, bf16[8,128,128]{1,2,0:T(8,128)(2,1)}) fusion(f32[1,2,8,128,128]{3,4,2,1,0:T(8,128)S(1)} %convert_add_fusion.3, f32[8,128,128]{1,2,0:T(8,128)S(1)} %copy.165, f32[8,128,128]{1,2,0:T(8,128)} %copy.163, f32[8,128,128]{1,2,0:T(8,128)S(1)} %copy.162, pred[8,128]{1,0:T(8,128)(4,1)S(1)} %copy-done.66, ...), kind=kLoop, calls=%fused_computation.72 | loop fusion | flops 1835008 | bytes 4721664 | tf_op jit(solution)/shard_map/convert_element_type | solution.py:226
  195.7 1.8 copy.167
  (372 shorter events, 68.2 us)
Async XLA Ops:
  2.5 21.7 %copy-start.86 = (pred[8,4]{0,1:T(4,128)(4,1)}, pred[8,4]{0,1:T(4,128)(4,1)S(1)}, u32[]{:S(2)}) copy-start(pred[8,4]{0,1:T(4,128)(4,1)S(1)} %iota_compare_fusion.1) | copy-start | bytes 100
  6.6 11.1 %copy-start.32 = (bf16[1,128,1024]{2,1,0:T(8,128)(2,1)S(1)}, bf16[1,128,1024]{2,1,0:T(8,128)(2,1)}, u32[]{:S(2)}) copy-start(bf16[1,128,1024]{2,1,0:T(8,128)(2,1)} %param.9) | copy-start | bytes 786436
  6.6 11.3 %collective-permute-start.7 = (bf16[1,2,8,32,128]{4,3,0,2,1:T(8,128)(2,1)S(1)}, bf16[1,2,8,32,128]{4,3,0,2,1:T(8,128)(2,1)S(1)}, u32[]{:S(2)}, u32[]{:S(2)}) collective-permute-start(bf16[1,2,8,32,128]{4,3,0,2,1:T(8,128)(2,1)S(1)} %maximum_bitcast_fusion.6), channel_id=1, source_target_pairs={{0,2},{2,0},{4,6},{6,4},{8,10},{10,8},{12,14},{14,12},{16,18},{18,... | collective-permute-start | bytes 393224 | tf_op jit(solution)/shard_map/ppermute | solution.py:24
  9.7 8.1 %copy-start.78 = (pred[8,8]{1,0:T(8,128)(4,1)}, pred[8,8]{1,0:T(8,128)(4,1)S(1)}, u32[]{:S(2)}) copy-start(pred[8,8]{1,0:T(8,128)(4,1)S(1)} %iota_compare_fusion) | copy-start | bytes 196
  10.9 4.6 %collective-permute-start.3 = (bf16[1,2,8,16,128]{4,3,0,2,1:T(8,128)(2,1)S(1)}, bf16[1,2,8,16,128]{4,3,0,2,1:T(8,128)(2,1)S(1)}, u32[]{:S(2)}, u32[]{:S(2)}) collective-permute-start(bf16[1,2,8,16,128]{4,3,0,2,1:T(8,128)(2,1)S(1)} %maximum_bitcast_fusion.7), channel_id=1, source_target_pairs={{0,2},{2,0},{4,6},{6,4},{8,10},{10,8},{12,14},{14,12},{16,18},{18,... | collective-permute-start | bytes 196616 | tf_op jit(solution)/shard_map/ppermute | solution.py:24
  11.0 31.5 %copy-start.84 = (pred[8,2]{0,1:T(4,128)(4,1)}, pred[8,2]{0,1:T(4,128)(4,1)S(1)}, u32[]{:S(2)}) copy-start(pred[8,2]{0,1:T(4,128)(4,1)S(1)} %iota_compare_fusion.2) | copy-start | bytes 52
  11.1 6.7 %copy-start.91 = (pred[8,2]{1,0:T(8,128)(4,1)}, pred[8,2]{1,0:T(8,128)(4,1)S(1)}, u32[]{:S(2)}) copy-start(pred[8,2]{1,0:T(8,128)(4,1)S(1)} %copy.100) | copy-start | bytes 52
  13.3 28.4 %copy-start.30 = (bf16[8,64,128]{2,1,0:T(8,128)(2,1)}, bf16[8,64,128]{2,1,0:T(8,128)(2,1)S(1)}, u32[]{:S(2)}) copy-start(bf16[8,64,128]{2,1,0:T(8,128)(2,1)S(1)} %get-tuple-element.25) | copy-start | bytes 393220
  13.3 14.4 %collective-permute-start.1 = (bf16[1,2,8,64,128]{4,3,0,2,1:T(8,128)(2,1)S(1)}, bf16[1,2,8,64,128]{4,3,0,2,1:T(8,128)(2,1)}, u32[]{:S(2)}, u32[]{:S(2)}) collective-permute-start(bf16[1,2,8,64,128]{4,3,0,2,1:T(8,128)(2,1)S(1)} %maximum_bitcast_fusion.5), channel_id=1, source_target_pairs={{0,2},{2,0},{4,6},{6,4},{8,10},{10,8},{12,14},{14,12},{16,18},{18,... | collective-permute-start | bytes 786440 | tf_op jit(solution)/shard_map/ppermute | solution.py:24
  15.5 20.8 %collective-permute-start = (bf16[1,2,8,128,128]{4,3,0,2,1:T(8,128)(2,1)S(1)}, bf16[1,2,8,128,128]{4,3,0,2,1:T(8,128)(2,1)S(1)}, u32[]{:S(2)}, u32[]{:S(2)}) collective-permute-start(bf16[1,2,8,128,128]{4,3,0,2,1:T(8,128)(2,1)S(1)} %maximum_bitcast_fusion.4), channel_id=1, source_target_pairs={{0,2},{2,0},{4,6},{6,4},{8,10},{10,8},{12,14},{14,12},{16,18},{18,... | collective-permute-start | bytes 1572872 | tf_op jit(solution)/shard_map/ppermute | solution.py:24
  15.6 6.4 %collective-permute-start.4 = (bf16[2,2,8,16,128]{4,3,0,2,1:T(8,128)(2,1)S(1)}, bf16[2,2,8,16,128]{4,3,0,2,1:T(8,128)(2,1)S(1)}, u32[]{:S(2)}, u32[]{:S(2)}) collective-permute-start(bf16[2,2,8,16,128]{4,3,0,2,1:T(8,128)(2,1)S(1)} %maximum_select_fusion.9), channel_id=1, source_target_pairs={{0,4},{2,6},{4,0},{6,2},{8,12},{10,14},{12,8},{14,10},{16,20},{18,... | collective-permute-start | bytes 393224 | tf_op jit(solution)/shard_map/ppermute | solution.py:24
  17.9 13.5 %copy-start.74 = (pred[8,8]{0,1:T(8,128)(4,1)}, pred[8,8]{0,1:T(8,128)(4,1)S(1)}, u32[]{:S(2)}) copy-start(pred[8,8]{0,1:T(8,128)(4,1)S(1)} %copy.102) | copy-start | bytes 196
  17.9 12.6 %collective-permute-start.8 = (bf16[2,2,8,32,128]{4,3,0,2,1:T(8,128)(2,1)S(1)}, bf16[2,2,8,32,128]{4,3,0,2,1:T(8,128)(2,1)S(1)}, u32[]{:S(2)}, u32[]{:S(2)}) collective-permute-start(bf16[2,2,8,32,128]{4,3,0,2,1:T(8,128)(2,1)S(1)} %maximum_select_fusion.8), channel_id=1, source_target_pairs={{0,4},{2,6},{4,0},{6,2},{8,12},{10,14},{12,8},{14,10},{16,20},{18,... | collective-permute-start | bytes 786440 | tf_op jit(solution)/shard_map/ppermute | solution.py:24
  22.1 9.8 %collective-permute-start.5 = (bf16[4,2,8,16,128]{4,3,0,2,1:T(8,128)(2,1)S(1)}, bf16[4,2,8,16,128]{4,3,0,2,1:T(8,128)(2,1)}, u32[]{:S(2)}, u32[]{:S(2)}) collective-permute-start(bf16[4,2,8,16,128]{4,3,0,2,1:T(8,128)(2,1)S(1)} %maximum_select_fusion.7), channel_id=1, source_target_pairs={{0,8},{2,10},{4,12},{6,14},{8,0},{10,2},{12,4},{14,6},{16,24},{18,... | collective-permute-start | bytes 786440 | tf_op jit(solution)/shard_map/ppermute | solution.py:24
  26.2 22.6 %copy-start.69 = (pred[8,128]{1,0:T(8,128)(4,1)}, pred[8,128]{1,0:T(8,128)(4,1)S(1)}, u32[]{:S(2)}) copy-start(pred[8,128]{1,0:T(8,128)(4,1)S(1)} %copy.109) | copy-start | bytes 3076
  27.1 9.2 %copy-start.55 = (pred[8,16,8]{0,2,1:T(8,128)(4,1)}, pred[8,16,8]{0,2,1:T(8,128)(4,1)S(1)}, u32[]{:S(2)}) copy-start(pred[8,16,8]{0,2,1:T(8,128)(4,1)S(1)} %broadcast_in_dim.539) | copy-start | bytes 3076
  28.9 11.4 %collective-permute-start.2 = (bf16[2,2,8,64,128]{4,3,0,2,1:T(8,128)(2,1)S(1)}, bf16[2,2,8,64,128]{4,3,0,2,1:T(8,128)(2,1)}, u32[]{:S(2)}, u32[]{:S(2)}) collective-permute-start(bf16[2,2,8,64,128]{4,3,0,2,1:T(8,128)(2,1)S(1)} %maximum_select_fusion.4), channel_id=1, source_target_pairs={{0,4},{2,6},{4,0},{6,2},{8,12},{10,14},{12,8},{14,10},{16,20},{18,... | collective-permute-start | bytes 1572872 | tf_op jit(solution)/shard_map/ppermute | solution.py:24
  31.4 20.4 %collective-permute-start.9 = (bf16[4,2,8,32,128]{4,3,0,2,1:T(8,128)(2,1)}, bf16[4,2,8,32,128]{4,3,0,2,1:T(8,128)(2,1)}, u32[]{:S(2)}, u32[]{:S(2)}) collective-permute-start(bf16[4,2,8,32,128]{4,3,0,2,1:T(8,128)(2,1)} %maximum_select_fusion.6), channel_id=1, source_target_pairs={{0,8},{2,10},{4,12},{6,14},{8,0},{10,2},{12,4},{14,6},{16,24},{18,... | collective-permute-start | bytes 1572872 | tf_op jit(solution)/shard_map/ppermute | solution.py:24
  33.7 25.4 %collective-permute-start.6 = (bf16[8,2,8,16,128]{4,3,0,2,1:T(8,128)(2,1)}, bf16[8,2,8,16,128]{4,3,0,2,1:T(8,128)(2,1)}, u32[]{:S(2)}, u32[]{:S(2)}) collective-permute-start(bf16[8,2,8,16,128]{4,3,0,2,1:T(8,128)(2,1)} %maximum_select_fusion.5), channel_id=1, source_target_pairs={{0,16},{2,18},{4,20},{6,22},{8,24},{10,26},{12,28},{14,30},{16,0},... | collective-permute-start | bytes 1572872 | tf_op jit(solution)/shard_map/ppermute | solution.py:24
  41.6 7.1 %copy-start.5 = (bf16[1,8,4,64,128]{4,3,2,1,0:T(8,128)(2,1)}, bf16[1,8,4,64,128]{4,3,2,1,0:T(8,128)(2,1)S(1)}, u32[]{:S(2)}) copy-start(bf16[1,8,4,64,128]{4,3,2,1,0:T(8,128)(2,1)S(1)} %get-tuple-element.49) | copy-start | bytes 1572868
  41.6 7.1 %copy-start.15 = (bf16[1,8,4,64,128]{4,3,2,1,0:T(8,128)(2,1)}, bf16[1,8,4,64,128]{4,3,2,1,0:T(8,128)(2,1)S(1)}, u32[]{:S(2)}) copy-start(bf16[1,8,4,64,128]{4,3,2,1,0:T(8,128)(2,1)S(1)} %get-tuple-element.48) | copy-start | bytes 1572868
  42.1 7.6 %copy-start.43 = (f32[8,64]{0,1:T(8,128)}, f32[8,64]{0,1:T(8,128)S(1)}, u32[]{:S(2)}) copy-start(f32[8,64]{0,1:T(8,128)S(1)} %copy.101) | copy-start | bytes 6148
  43.2 10.3 %copy-start.34 = (f32[8,64,2]{0,2,1:T(2,128)}, f32[8,64,2]{0,2,1:T(2,128)S(1)}, u32[]{:S(2)}) copy-start(f32[8,64,2]{0,2,1:T(2,128)S(1)} %get-tuple-element.72) | copy-start | bytes 12292
  54.4 4.7 %copy-start.7 = (bf16[1,8,8,32,128]{4,3,2,1,0:T(8,128)(2,1)}, bf16[1,8,8,32,128]{4,3,2,1,0:T(8,128)(2,1)S(1)}, u32[]{:S(2)}) copy-start(bf16[1,8,8,32,128]{4,3,2,1,0:T(8,128)(2,1)S(1)} %get-tuple-element.53) | copy-start | bytes 1572868
  61.1 5.0 %copy-start.12 = (bf16[1,8,16,16,128]{4,3,2,1,0:T(8,128)(2,1)}, bf16[1,8,16,16,128]{4,3,2,1,0:T(8,128)(2,1)S(1)}, u32[]{:S(2)}) copy-start(bf16[1,8,16,16,128]{4,3,2,1,0:T(8,128)(2,1)S(1)} %get-tuple-element.50) | copy-start | bytes 1572868
  64.1 6.4 %copy-start.33 = (bf16[1,128,1024]{2,1,0:T(8,128)(2,1)S(1)}, bf16[1,128,1024]{2,1,0:T(8,128)(2,1)}, u32[]{:S(2)}) copy-start(bf16[1,128,1024]{2,1,0:T(8,128)(2,1)} %param.9) | copy-start | bytes 786436
  76.2 4.8 %copy-start.58 = (f32[8,16]{0,1:T(8,128)S(1)}, f32[8,16]{0,1:T(8,128)}, u32[]{:S(2)}) copy-start(f32[8,16]{0,1:T(8,128)} %copy-done.57) | copy-start | bytes 1540
  76.2 4.9 %copy-start.35 = (f32[8,64,2]{0,2,1:T(2,128)S(1)}, f32[8,64,2]{0,2,1:T(2,128)}, u32[]{:S(2)}) copy-start(f32[8,64,2]{0,2,1:T(2,128)} %copy-done.34) | copy-start | bytes 12292
  76.2 4.9 %copy-start.37 = (f32[8,128]{0,1:T(8,128)S(1)}, f32[8,128]{0,1:T(8,128)}, u32[]{:S(2)}) copy-start(f32[8,128]{0,1:T(8,128)} %copy.131) | copy-start | bytes 12292
  76.2 4.9 %copy-start.39 = (f32[8,128]{0,1:T(8,128)S(1)}, f32[8,128]{0,1:T(8,128)}, u32[]{:S(2)}) copy-start(f32[8,128]{0,1:T(8,128)} %copy.135) | copy-start | bytes 12292
  76.2 4.9 %copy-start.41 = (f32[8,128]{0,1:T(8,128)S(1)}, f32[8,128]{0,1:T(8,128)}, u32[]{:S(2)}) copy-start(f32[8,128]{0,1:T(8,128)} %copy.137) | copy-start | bytes 12292
  76.2 4.9 %copy-start.56 = (pred[8,16,8]{0,2,1:T(8,128)(4,1)S(1)}, pred[8,16,8]{0,2,1:T(8,128)(4,1)}, u32[]{:S(2)}) copy-start(pred[8,16,8]{0,2,1:T(8,128)(4,1)} %copy-done.55) | copy-start | bytes 3076
  76.3 4.9 %copy-start.88 = (pred[8,4]{0,1:T(4,128)(4,1)S(1)}, pred[8,4]{0,1:T(4,128)(4,1)}, u32[]{:S(2)}) copy-start(pred[8,4]{0,1:T(4,128)(4,1)} %copy-done.86) | copy-start | bytes 100
  106.5 63.0 %collective-permute-start.10 = (bf16[1,2,8,128,128]{3,4,2,1,0:T(8,128)(2,1)S(1)}, bf16[1,2,8,128,128]{3,4,2,1,0:T(8,128)(2,1)}, u32[]{:S(2)}, u32[]{:S(2)}) collective-permute-start(bf16[1,2,8,128,128]{3,4,2,1,0:T(8,128)(2,1)S(1)} %select_convert_fusion.3), channel_id=1, source_target_pairs={{0,2},{2,0},{4,6},{6,4},{8,10},{10,8},{12,14},{14,12},{16,18},{18,... | collective-permute-start | bytes 1572872 | tf_op jit(solution)/shard_map/ppermute | solution.py:24
  109.2 50.1 %collective-permute-start.17 = (bf16[4,2,8,32,128]{4,3,0,2,1:T(8,128)(2,1)}, bf16[4,2,8,32,128]{4,3,0,2,1:T(8,128)(2,1)}, u32[]{:S(2)}, u32[]{:S(2)}) collective-permute-start(bf16[4,2,8,32,128]{4,3,0,2,1:T(8,128)(2,1)} %select_convert_fusion), channel_id=1, source_target_pairs={{0,8},{2,10},{4,12},{6,14},{8,0},{10,2},{12,4},{14,6},{16,24},{18,... | collective-permute-start | bytes 1572872 | tf_op jit(solution)/shard_map/ppermute | solution.py:24
  111.6 52.2 %collective-permute-start.13 = (bf16[8,2,8,16,128]{4,3,0,2,1:T(8,128)(2,1)}, bf16[8,2,8,16,128]{4,3,0,2,1:T(8,128)(2,1)}, u32[]{:S(2)}, u32[]{:S(2)}) collective-permute-start(bf16[8,2,8,16,128]{4,3,0,2,1:T(8,128)(2,1)} %select_convert_fusion.1), channel_id=1, source_target_pairs={{0,16},{2,18},{4,20},{6,22},{8,24},{10,26},{12,28},{14,30},{16,0},... | collective-permute-start | bytes 1572872 | tf_op jit(solution)/shard_map/ppermute | solution.py:24
  113.0 45.5 %copy-start.27 = (f32[1,128,1024]{2,1,0:T(8,128)S(1)}, f32[1,128,1024]{2,1,0:T(8,128)}, u32[]{:S(2)}) copy-start(f32[1,128,1024]{2,1,0:T(8,128)} %reshape.1123) | copy-start | bytes 1572868
  113.0 45.5 %copy-start.64 = (f32[1024]{0:T(1024)S(1)}, f32[1024]{0:T(1024)}, u32[]{:S(2)}) copy-start(f32[1024]{0:T(1024)} %param.10) | copy-start | bytes 12292
  113.0 45.5 %copy-start.81 = (f32[128]{0:T(128)S(1)}, f32[128]{0:T(128)}, u32[]{:S(2)}) copy-start(f32[128]{0:T(128)} %copy-done.80) | copy-start | bytes 1540
  113.0 45.5 %copy-start.83 = (f32[128]{0:T(128)S(1)}, f32[128]{0:T(128)}, u32[]{:S(2)}) copy-start(f32[128]{0:T(128)} %copy-done.82) | copy-start | bytes 1540
  115.5 50.9 %collective-permute-start.11 = (bf16[2,2,8,64,128]{4,3,0,2,1:T(8,128)(2,1)}, bf16[2,2,8,64,128]{4,3,0,2,1:T(8,128)(2,1)}, u32[]{:S(2)}, u32[]{:S(2)}) collective-permute-start(bf16[2,2,8,64,128]{4,3,0,2,1:T(8,128)(2,1)} %select_convert_fusion.2), channel_id=1, source_target_pairs={{0,4},{2,6},{4,0},{6,2},{8,12},{10,14},{12,8},{14,10},{16,20},{18,... | collective-permute-start | bytes 1572872 | tf_op jit(solution)/shard_map/ppermute | solution.py:24
  161.5 5.0 %copy-start.1 = (f32[4,2,8,64,128]{4,3,0,2,1:T(8,128)S(1)}, f32[4,2,8,64,128]{4,3,0,2,1:T(8,128)}, u32[]{:S(2)}) copy-start(f32[4,2,8,64,128]{4,3,0,2,1:T(8,128)} %copy-done) | copy-start | bytes 6291460
  161.5 9.2 %collective-permute-start.18 = (bf16[2,2,8,32,128]{4,3,0,2,1:T(8,128)(2,1)S(1)}, bf16[2,2,8,32,128]{4,3,0,2,1:T(8,128)(2,1)S(1)}, u32[]{:S(2)}, u32[]{:S(2)}) collective-permute-start(bf16[2,2,8,32,128]{4,3,0,2,1:T(8,128)(2,1)S(1)} %select_convert_fusion.4), channel_id=1, source_target_pairs={{0,4},{2,6},{4,0},{6,2},{8,12},{10,14},{12,8},{14,10},{16,20},{18,... | collective-permute-start | bytes 786440 | tf_op jit(solution)/shard_map/ppermute | solution.py:24
  165.2 7.0 %collective-permute-start.14 = (bf16[4,2,8,16,128]{4,3,0,2,1:T(8,128)(2,1)S(1)}, bf16[4,2,8,16,128]{4,3,0,2,1:T(8,128)(2,1)S(1)}, u32[]{:S(2)}, u32[]{:S(2)}) collective-permute-start(bf16[4,2,8,16,128]{4,3,0,2,1:T(8,128)(2,1)S(1)} %select_convert_fusion.5), channel_id=1, source_target_pairs={{0,8},{2,10},{4,12},{6,14},{8,0},{10,2},{12,4},{14,6},{16,24},{18,... | collective-permute-start | bytes 786440 | tf_op jit(solution)/shard_map/ppermute | solution.py:24
  167.9 8.2 %collective-permute-start.12 = (bf16[1,2,8,64,128]{4,3,0,2,1:T(8,128)(2,1)S(1)}, bf16[1,2,8,64,128]{4,3,0,2,1:T(8,128)(2,1)S(1)}, u32[]{:S(2)}, u32[]{:S(2)}) collective-permute-start(bf16[1,2,8,64,128]{4,3,0,2,1:T(8,128)(2,1)S(1)} %select_convert_fusion.6), channel_id=1, source_target_pairs={{0,2},{2,0},{4,6},{6,4},{8,10},{10,8},{12,14},{14,12},{16,18},{18,... | collective-permute-start | bytes 786440 | tf_op jit(solution)/shard_map/ppermute | solution.py:24
  171.5 11.8 %collective-permute-start.19 = (bf16[1,2,8,32,128]{4,3,0,2,1:T(8,128)(2,1)}, bf16[1,2,8,32,128]{4,3,0,2,1:T(8,128)(2,1)S(1)}, u32[]{:S(2)}, u32[]{:S(2)}) collective-permute-start(bf16[1,2,8,32,128]{4,3,0,2,1:T(8,128)(2,1)} %select_convert_fusion.7), channel_id=1, source_target_pairs={{0,2},{2,0},{4,6},{6,4},{8,10},{10,8},{12,14},{14,12},{16,18},{18,... | collective-permute-start | bytes 393224 | tf_op jit(solution)/shard_map/ppermute | solution.py:24
  173.0 7.5 %collective-permute-start.15 = (bf16[2,2,8,16,128]{4,3,0,2,1:T(8,128)(2,1)}, bf16[2,2,8,16,128]{4,3,0,2,1:T(8,128)(2,1)}, u32[]{:S(2)}, u32[]{:S(2)}) collective-permute-start(bf16[2,2,8,16,128]{4,3,0,2,1:T(8,128)(2,1)} %select_convert_fusion.8), channel_id=1, source_target_pairs={{0,4},{2,6},{4,0},{6,2},{8,12},{10,14},{12,8},{14,10},{16,20},{18,... | collective-permute-start | bytes 393224 | tf_op jit(solution)/shard_map/ppermute | solution.py:24
  182.1 4.6 %collective-permute-start.16 = (bf16[1,2,8,16,128]{4,3,0,2,1:T(8,128)(2,1)}, bf16[1,2,8,16,128]{4,3,0,2,1:T(8,128)(2,1)}, u32[]{:S(2)}, u32[]{:S(2)}) collective-permute-start(bf16[1,2,8,16,128]{4,3,0,2,1:T(8,128)(2,1)} %select_convert_fusion.9), channel_id=1, source_target_pairs={{0,2},{2,0},{4,6},{6,4},{8,10},{10,8},{12,14},{14,12},{16,18},{18,... | collective-permute-start | bytes 196616 | tf_op jit(solution)/shard_map/ppermute | solution.py:24
  (65 other events, 205.0 us)
where the time goes:
time: 200 us; the launch traced here: 198 us
  local copies, waits for them, and re-layouts  51.5 us (26%)
  other arithmetic  48.4 us (24%)
  blocking collectives  41.8 us (21%)
  starting transfers between devices  23.6 us (12%)
  matrix products  21.3 us (11%)
  waiting for transfers between devices  9.67 us (5%)
  between operations  2.08 us (1%)
    psum x1, blocking collectives, shards(): gain_sum = lax.psum(gain_part, ('ctx', 'dp'))  41.8 us
    ppermute x20, starting transfers between devices, partner(): return lax.ppermute(value, axis, pairs)  23.6 us
    broadcast_in_dim x45, local copies, waits for them, and re-layouts, widen_rows(): jnp.where(head_mask(stride, chosen), tensor[:, :, None, :], filler)  21.7 us
    unnamed x193, local copies, waits for them, and re-layouts  13.5 us
    ppermute x20, waiting for transfers between devices, partner(): return lax.ppermute(value, axis, pairs)  9.67 us
    reduce_sum x9, other arithmetic, pick_rows(): jnp.sum(jnp.where(head_mask(stride, chosen), grouped, jnp.zeros((), tenso...  9.19 us
    add x10, other arithmetic, release(): buffers[level_id] = kept_half + arrived.astype(jnp.float32)  8.16 us
    dot_general x4, matrix products, shards(): jnp.einsum('hqk,hqd->hkd', probs.astype(jnp.bfloat16), act_g, preferred_e...  6.53 us
  transfers between devices with their start and end apart: 20, of which 5 were waited for; matrix products, arithmetic and copies ran while one was open for 27% of the time, Pallas kernels for 0%

commit v1 on v0

v1 whole, which is shorter than its diff:
```python
import functools
import math

import jax
import jax.numpy as jnp
from jax import lax
from jax.experimental import pallas as pl
from jax.experimental.pallas import tpu as pltpu
from jax.sharding import PartitionSpec as P

SPAN_A = 2
RATE_A = 1
SPAN_B = 4
RATE_B = 2
SPAN_C = 16
RATE_C = 8

EPSILON = 1e-05
LOG2E = math.log2(math.e)
TILE = 16
F32 = jnp.float32
BF16 = jnp.bfloat16

NT = (((1,), (1,)), ((), ()))
TN = (((0,), (0,)), ((), ()))
NN = (((1,), (0,)), ((), ()))


def dot(left, right, dims):
    return lax.dot_general(left, right, dims, preferred_element_type=F32)


def row_order(tokens, rate, transposed):
    short = tokens // rate
    placed = lax.broadcasted_iota(jnp.int32, (tokens, tokens), 1 if transposed else 0)
    source = lax.broadcasted_iota(jnp.int32, (tokens, tokens), 0 if transposed else 1)
    return (source == (placed % short) * rate + placed // short).astype(BF16)


def split_kernel(rate, q_ref, k_ref, v_ref, g_ref, out_ref):
    group, _, tokens, hd = out_ref.shape
    order = row_order(tokens, rate, False)
    for t, ref in enumerate((q_ref, k_ref, v_ref, g_ref)):
        moved = dot(order, ref[0], NN).astype(BF16)
        for h in range(group):
            out_ref[h, t] = moved[:, h * hd : (h + 1) * hd]


class Level:
    def __init__(self, index, span, rate, top_rate, fold, group):
        self.index = index
        self.rate = rate
        self.count = top_rate // rate
        self.crossing = span > group
        self.bits = span.bit_length() - group.bit_length()
        self.pieces = min(span, group) // fold
        self.segments = 1 if self.crossing else group // span

    def starts(self, offs_ref):
        first = 0 if self.index == 0 else offs_ref[self.index - 1]
        return [first + self.rate * i for i in range(self.count)]

    def places(self, offs_ref, segment):
        low = segment * self.pieces
        return [(nb, b) for b in self.starts(offs_ref) for nb in range(low, low + self.pieces)]


def gather(read, places):
    return jnp.concatenate([read(nb, b) for nb, b in places], axis=0)


def scores_of(query, key, scale):
    return dot(query, key, NT) * scale


def forward(query, key, value, scale):
    scores = scores_of(query, key, scale)
    top = jnp.max(scores, axis=-1, keepdims=True)
    weights = jnp.exp2(scores - top)
    total = jnp.sum(weights, axis=-1, keepdims=True)
    mixed = dot(weights.astype(BF16), value, NN) / total
    return mixed, jnp.broadcast_to(top + jnp.log2(total), mixed.shape)


def merge(mixed, lse, more, more_lse):
    top = jnp.maximum(lse, more_lse)
    left, right = jnp.exp2(lse - top), jnp.exp2(more_lse - top)
    total = left + right
    return (mixed * left + more * right) / total, top + jnp.log2(total)


def merge_into(o_ref, lse_ref, places, more, more_lse):
    mixed, lse = merge(
        gather(lambda nb, b: o_ref[nb, b], places),
        gather(lambda nb, b: lse_ref[nb, b], places),
        more,
        more_lse,
    )
    put(o_ref, places, mixed)
    put(lse_ref, places, lse)


def put(ref, places, rows):
    size = ref.shape[-2]
    for i, (nb, b) in enumerate(places):
        ref[nb, b] = rows[i * size : (i + 1) * size]


def add(ref, places, rows):
    size = ref.shape[-2]
    for i, (nb, b) in enumerate(places):
        ref[nb, b] += rows[i * size : (i + 1) * size]


def local_kernel(levels, scale, offs_ref, x_ref, o_ref, lse_ref):
    for level in levels:
        for segment in range(level.segments):
            places = level.places(offs_ref, segment)
            query, key, value = (gather(lambda nb, b, t=t: x_ref[nb, t, b], places) for t in range(3))
            mixed, lse = forward(query, key, value, scale)
            if level.index == 0:
                put(o_ref, places, mixed)
                put(lse_ref, places, lse)
            else:
                merge_into(o_ref, lse_ref, places, mixed, lse)


def crossing_keys(level, places, x_ref, other_ref, t):
    found = [x_ref[nb, t, b] for nb, b in places]
    for e in range(other_ref.shape[0]):
        for i in range(level.count):
            found += [other_ref[e, nb, t - 1, i] for nb in range(level.pieces)]
    return jnp.concatenate(found, axis=0)


def stats_kernel(levels, scale, offs_ref, x_ref, o_in, lse_in, gain_ref, *refs):
    others, (attn_ref, lse_ref, stats_ref, o_ref) = refs[: len(levels)], refs[len(levels) :]
    pieces, rate, size, hd = o_ref.shape
    o_ref[...] = o_in[...]
    lse_ref[...] = lse_in[...]
    for level, other_ref in zip(levels, others):
        places = level.places(offs_ref, 0)
        query = gather(lambda nb, b: x_ref[nb, 0, b], places)
        key = crossing_keys(level, places, x_ref, other_ref, 1)
        value = crossing_keys(level, places, x_ref, other_ref, 2)
        merge_into(o_ref, lse_ref, places, *forward(query, key, value, scale))
    chunks = pieces * rate * size // hd
    per = chunks // pieces
    lane = lax.broadcasted_iota(jnp.int32, (hd, hd), 1)
    table = jnp.zeros((hd, hd), F32)
    for nb in range(pieces):
        attn_ref[nb] = o_ref[nb].astype(BF16)
        attn_all = attn_ref[nb].reshape(rate * size, hd).astype(F32)
        grad_all = x_ref[nb, 3].reshape(rate * size, hd).astype(F32)
        for part in range(per):
            attn = attn_all[part * hd : (part + 1) * hd]
            scaled = grad_all[part * hd : (part + 1) * hd] * gain_ref[...]
            total = jnp.sum(attn, axis=-1, keepdims=True)
            away = attn - total * (1.0 / hd)
            sums = (
                total,
                jnp.sum(away * away, axis=-1, keepdims=True),
                jnp.sum(scaled, axis=-1, keepdims=True),
                jnp.sum(scaled * away, axis=-1, keepdims=True),
            )
            for i, column in enumerate(sums):
                table = jnp.where(lane == i * chunks + nb * per + part, column, table)
    turned = table.T[: 4 * chunks]
    for peer in range(stats_ref.shape[0]):
        stats_ref[peer] = turned


def norm_kernel(levels, scale, score_scale, offs_ref, x_ref, attn_ref, lse_ref, gain_ref, stats_ref, *refs):
    count = len(levels)
    others, refs = refs[:count], refs[count:]
    attended_ref, grad_ref, delta_ref, gsum_ref = refs[:4]
    own_refs, sent_refs = refs[4 : 4 + count], refs[4 + count :]
    pieces, rate, size, hd = attn_ref.shape
    chunks = pieces * rate * size // hd
    per = chunks // pieces
    heads = stats_ref.shape[0]
    width = heads * hd
    sums, squares, scaleds, products = (
        [stats_ref[h, i * chunks : (i + 1) * chunks, :] for h in range(heads)] for i in range(4)
    )
    mean = functools.reduce(jnp.add, sums) * (1.0 / width)
    apart = [total * (1.0 / hd) - mean for total in sums]
    variance = functools.reduce(
        jnp.add, [square + hd * a * a for square, a in zip(squares, apart)]
    ) * (1.0 / width)
    inverse = lax.rsqrt(variance + EPSILON)
    first = functools.reduce(jnp.add, scaleds) * (1.0 / width)
    second = (
        functools.reduce(jnp.add, [p + a * s for p, a, s in zip(products, apart, scaleds)])
        * (1.0 / width)
        * inverse
    )
    table = jnp.concatenate(
        [mean, inverse, first, second, jnp.zeros((hd - 4 * chunks, hd), F32)], axis=0
    ).T
    gsum = jnp.zeros((1, hd), F32)
    for nb in range(pieces):
        attn_all = attn_ref[nb].reshape(rate * size, hd).astype(F32)
        grad_all = x_ref[nb, 3].reshape(rate * size, hd).astype(F32)
        attended, grads, deltas = [], [], []
        for part in range(per):
            chunk = nb * per + part
            mean_c, inv_c, first_c, second_c = (
                table[:, i * chunks + chunk : i * chunks + chunk + 1] for i in range(4)
            )
            attn = attn_all[part * hd : (part + 1) * hd]
            upstream = grad_all[part * hd : (part + 1) * hd]
            normed = (attn - mean_c) * inv_c
            attended.append((normed * gain_ref[...]).astype(BF16))
            grad = (inv_c * (upstream * gain_ref[...] - first_c - normed * second_c)).astype(BF16)
            grads.append(grad)
            delta = jnp.sum(grad.astype(F32) * attn, axis=-1, keepdims=True)
            deltas.append(jnp.broadcast_to(delta, attn.shape))
            gsum = gsum + jnp.sum(upstream * normed, axis=0, keepdims=True)
        shape = (rate, size, hd)
        attended_ref[nb] = jnp.concatenate(attended, axis=0).reshape(shape)
        grad_ref[nb] = jnp.concatenate(grads, axis=0).reshape(shape)
        delta_ref[nb] = jnp.concatenate(deltas, axis=0).reshape(shape)
    gsum_ref[...] = gsum
    for level, other_ref, own_ref, sent_ref in zip(levels, others, own_refs, sent_refs):
        places = level.places(offs_ref, 0)
        query = gather(lambda nb, b: x_ref[nb, 0, b], places)
        key = crossing_keys(level, places, x_ref, other_ref, 1)
        value = crossing_keys(level, places, x_ref, other_ref, 2)
        parts = backward(
            query,
            key,
            value,
            gather(lambda nb, b: grad_ref[nb, b], places),
            gather(lambda nb, b: lse_ref[nb, b], places),
            gather(lambda nb, b: delta_ref[nb, b], places),
            scale,
            score_scale,
        )
        own = len(places) * size
        steps = [(i, nb) for i in range(level.count) for nb in range(level.pieces)]
        for t, part in enumerate(parts):
            for j, (i, nb) in enumerate(steps):
                own_ref[t, nb, i] = part[j * size : (j + 1) * size]
                if t > 0:
                    for e in range(sent_ref.shape[0]):
                        low = (e + 1) * own + j * size
                        sent_ref[e, nb, t - 1, i] = part[low : low + size].astype(sent_ref.dtype)


def backward(query, key, value, grad, lse, delta, scale, score_scale):
    wide = key.shape[0] // lse.shape[1]
    spread = lambda column: jnp.concatenate([column] * wide, axis=1)
    probs = jnp.exp2(scores_of(query, key, score_scale) - spread(lse))
    prob_grad = dot(grad, value, NT)
    score_grad = (probs * (prob_grad - spread(delta))).astype(BF16)
    return (
        dot(score_grad, key, NN) * scale,
        dot(score_grad, query, TN) * scale,
        dot(probs.astype(BF16), grad, TN),
    )


def grads_kernel(levels, crossing, scale, score_scale, offs_ref, x_ref, attended_ref, grad_ref, lse_ref, delta_ref, *refs):
    own_refs, (out_ref, kv_ref, dq_ref) = refs[: len(crossing)], refs[len(crossing) :]
    accumulators = (dq_ref, kv_ref.at[0], kv_ref.at[1])
    for level in levels:
        for segment in range(level.segments):
            places = level.places(offs_ref, segment)
            query, key, value = (gather(lambda nb, b, t=t: x_ref[nb, t, b], places) for t in range(3))
            parts = backward(
                query,
                key,
                value,
                gather(lambda nb, b: grad_ref[nb, b], places),
                gather(lambda nb, b: lse_ref[nb, b], places),
                gather(lambda nb, b: delta_ref[nb, b], places),
                scale,
                score_scale,
            )
            for ref, part in zip(accumulators, parts):
                (put if level.index == 0 else add)(ref, places, part)
    for level, own_ref in zip(crossing, own_refs):
        starts = level.starts(offs_ref)
        for t, ref in enumerate(accumulators):
            for i, b in enumerate(starts):
                for nb in range(level.pieces):
                    ref[nb, b] += own_ref[t, nb, i]
    out_ref[:, 0] = dq_ref[...].astype(BF16)
    out_ref[:, 1] = attended_ref[...]


def pack_kernel(crossing, fold, offs_ref, main_ref, kv_in, gsum_ref, *refs):
    arrived_refs, (out_ref, kv_ref) = refs[: len(crossing)], refs[len(crossing) :]
    pieces, _, rate, size, hd = main_ref.shape
    rows = rate * size
    kv_ref[...] = kv_in[...]
    for level, arrived_ref in zip(crossing, arrived_refs):
        for i, b in enumerate(level.starts(offs_ref)):
            for nb in range(level.pieces):
                for t in range(2):
                    kv_ref[t, nb, b] += arrived_ref[nb, t, i].astype(F32)
    total = jnp.broadcast_to(gsum_ref[...], (TILE, hd))
    high = total.astype(BF16).astype(F32)
    middle = (total - high).astype(BF16).astype(F32)
    low = total - high - middle
    row = lax.broadcasted_iota(jnp.int32, (TILE, hd), 0)
    coded = jnp.where(row == 0, high, jnp.where(row == 1, middle, jnp.where(row == 2, low, 0.0)))
    for nb in range(pieces):
        for t in range(2):
            out_ref[nb, t * rows : (t + 1) * rows] = main_ref[nb, t].reshape(rows, hd)
            out_ref[nb, (t + 2) * rows : (t + 3) * rows] = (
                kv_ref[t, nb].reshape(rows, hd).astype(BF16)
            )
        for f in range(fold):
            out_ref[nb, 4 * rows + f * TILE : 4 * rows + (f + 1) * TILE] = coded.astype(BF16)


def join_kernel(rate, factor, in_ref, dq_ref, attended_ref, dk_ref, dv_ref, gain_ref):
    group = in_ref.shape[0]
    hd = in_ref.shape[2]
    tokens = dq_ref.shape[1]
    order = row_order(tokens, rate, True)
    for t, ref in enumerate((dq_ref, attended_ref, dk_ref, dv_ref)):
        for h in range(group):
            moved = dot(order, in_ref[h, t * tokens : (t + 1) * tokens, :], NN)
            ref[0, :, h * hd : (h + 1) * hd] = moved.astype(BF16)
    for h in range(group):
        coded = in_ref[h, 4 * tokens : 4 * tokens + TILE, :].astype(F32)
        gain_ref[:, h * hd : (h + 1) * hd] = jnp.sum(coded, axis=0, keepdims=True) * factor


SMEM = pl.BlockSpec(memory_space=pltpu.SMEM)
VMEM = pl.BlockSpec(memory_space=pltpu.VMEM)


def call(body, name, inputs, outputs, scratch=(), flops=0, limit=24):
    shapes = [jax.ShapeDtypeStruct(*output) for output in outputs]
    moved = sum(x.size * x.dtype.itemsize for x in list(inputs) + shapes)
    return pl.pallas_call(
        body,
        name=name,
        in_specs=[SMEM if x.dtype == jnp.int32 else VMEM for x in inputs],
        out_specs=[VMEM] * len(shapes),
        out_shape=shapes,
        scratch_shapes=[pltpu.VMEM(*each) for each in scratch],
        cost_estimate=pl.CostEstimate(flops=flops, bytes_accessed=moved, transcendentals=0),
        compiler_params=pltpu.CompilerParams(vmem_limit_bytes=limit * 1024 * 1024),
    )(*inputs)


def flip(value, axis, bit):
    pairs = [(source, source ^ (1 << bit)) for source in range(lax.axis_size(axis))]
    return lax.ppermute(value, axis, pairs)


def shards(queries, key_rows, value_rows, out_grad, norm_gain, offsets):
    tokens, width = queries.shape[1:]
    group = offsets.shape[1]
    hd = width // group
    ctx_count = lax.axis_size("ctx")
    dp_count = lax.axis_size("dp")
    scale = hd ** (-0.5)
    score_scale = scale * LOG2E
    spans = [
        (SPAN_A, RATE_A),
        (SPAN_B, RATE_B),
        (SPAN_C, RATE_C),
        (ctx_count // 2, ctx_count // 4),
    ]
    rate = max(r for _, r in spans)
    short = tokens // rate
    fold = max(1, TILE // short)
    size = short * fold
    pieces = group // fold
    levels = [Level(i, span, r, rate, fold, group) for i, (span, r) in enumerate(spans)]
    local = [level for level in levels if not level.crossing]
    crossing = [level for level in levels if level.crossing]
    groups = [list(range(low, low + group)) for low in range(0, ctx_count, group)]
    low_bit = group.bit_length() - 1

    def exchange(value):
        return lax.all_to_all(value, "ctx", 0, 0, tiled=True, axis_index_groups=groups)

    head = lax.axis_index("ctx") % group
    offs = lax.dynamic_slice(offsets, (0, head), (offsets.shape[0], 1))[:, 0]
    gain = lax.dynamic_slice(norm_gain, (head * hd,), (hd,))[None]

    (sent,) = call(
        functools.partial(split_kernel, rate),
        "split",
        [queries, key_rows, value_rows, out_grad],
        [((group, 4, tokens, hd), BF16)],
    )
    x = exchange(sent)
    if fold > 1:
        x = x.reshape(pieces, fold, 4, rate, short, hd).transpose(0, 2, 3, 1, 4, 5)
    x = x.reshape(pieces, 4, rate, size, hd)

    others = []
    for level in crossing:
        own = jnp.concatenate(
            [
                lax.dynamic_slice(x, (0, 1, b, 0, 0), (pieces, 2, 1, size, hd))
                for b in level.starts(offs)
            ],
            axis=2,
        )
        blocks = [own]
        for bit in range(level.bits):
            blocks += [flip(block, "ctx", low_bit + bit) for block in blocks]
        others.append(jnp.stack(blocks[1:]))

    state = (pieces, rate, size, hd)
    o, lse = call(
        functools.partial(local_kernel, local, score_scale),
        "local_forward",
        [offs, x],
        [(state, F32), (state, F32)],
        flops=10**8,
    )
    chunks = group * tokens // hd
    attn, lse, stats = call(
        functools.partial(stats_kernel, crossing, score_scale),
        "crossing_forward",
        [offs, x, o, lse, gain] + others,
        [(state, BF16), (state, F32), ((group, 4 * chunks, hd), F32)],
        scratch=[(state, F32)],
    )
    stats = exchange(stats)
    outs = [(state, BF16), (state, BF16), (state, F32), ((1, hd), F32)]
    outs += [((3, pieces, level.count, size, hd), F32) for level in crossing]
    sent_types = [BF16 if level.bits == 1 else F32 for level in crossing]
    outs += [(other.shape, kind) for other, kind in zip(others, sent_types)]
    attended, grad, delta, gsum, *rest = call(
        functools.partial(norm_kernel, crossing, scale, score_scale),
        "norm_and_crossing",
        [offs, x, attn, lse, gain, stats] + others,
        outs,
    )
    owns, parts = rest[: len(crossing)], rest[len(crossing) :]

    arrived = []
    for level, part in zip(crossing, parts):
        blocks = [None] + [part[e] for e in range(part.shape[0])]
        for bit in reversed(range(level.bits)):
            half = 1 << bit
            came = [flip(block.astype(BF16), "ctx", low_bit + bit) for block in blocks[half:]]
            blocks = [
                c if b is None else b.astype(F32) + c.astype(F32)
                for b, c in zip(blocks[:half], came)
            ]
        arrived.append(blocks[0])
    for axis, count, first in (("dp", dp_count, 0), ("ctx", ctx_count, low_bit)):
        for bit in range(first, count.bit_length() - 1):
            gsum = gsum + flip(gsum, axis, bit)

    main, kv = call(
        functools.partial(grads_kernel, local, crossing, scale, score_scale),
        "local_backward",
        [offs, x, attended, grad, lse, delta] + owns,
        [((pieces, 2, rate, size, hd), BF16), ((2,) + state, F32)],
        scratch=[(state, F32)],
        flops=3 * 10**8,
    )
    tail = TILE * fold
    (packed,) = call(
        functools.partial(pack_kernel, crossing, fold),
        "pack",
        [offs, main, kv, gsum] + arrived,
        [((pieces, 4 * rate * size + tail, hd), BF16)],
        scratch=[((2,) + state, F32)],
    )
    if fold > 1:
        rows = packed[:, : 4 * rate * size].reshape(pieces, 4, rate, fold, short, hd)
        rows = rows.transpose(0, 3, 1, 2, 4, 5).reshape(group, 4 * tokens, hd)
        packed = jnp.concatenate([rows, packed[:, 4 * rate * size :].reshape(group, TILE, hd)], 1)
    back = exchange(packed)
    factor = 1.0 / math.sqrt(ctx_count * dp_count * tokens)
    row = ((1, tokens, width), BF16)
    dq, attended, dk, dv, gain_grad = call(
        functools.partial(join_kernel, rate, factor),
        "join",
        [back],
        [row, row, row, row, ((1, width), F32)],
    )
    return attended, dq, dk, dv, gain_grad[0]


def solution(mesh):
    rows = P("dp", "ctx", None)
    return jax.shard_map(
        shards,
        mesh=mesh,
        in_specs=(rows, rows, rows, rows, P(), P()),
        out_specs=(rows, rows, rows, rows, P()),
        check_vma=False,
    )
```

time: 200 us -> 74 us (0.37)
  other arithmetic: 48.4 us -> 0.01 us
  local copies, waits for them, and re-layouts: 51.5 us -> 4.59 us
  matrix products: 21.3 us -> 0 us
  blocking collectives: 41.8 us -> 26.1 us
  Pallas kernels: 0 us -> 12.2 us
  starting transfers between devices: 23.6 us -> 12 us
  waiting for transfers between devices: 9.67 us -> 16.1 us
    psum x1 -> x0, blocking collectives: 41.8 us -> none  [shards(): gain_sum = lax.psum(gain_part, ('ctx', 'dp'))]
    all_to_all x0 -> x2, blocking collectives: none -> 26.1 us  [exchange(): lax.all_to_all(value, 'ctx', 0, 0, tiled=True, axis_index_groups=groups)]
    broadcast_in_dim x45 -> x1, local copies, waits for them, and re-layouts: 21.7 us -> 0.07 us  [shards(): gain = lax.dynamic_slice(norm_gain, (head * hd,), (hd,))[None]]
    dot_general x24 -> x0, matrix products: 21.3 us -> none  [the longest x4 6.53 us: shards(): jnp.einsum('hqk,hqd->hkd', probs.astype(jnp.bfloat16), act_g, preferred_e...]
    ppermute x20 -> x4, starting transfers between devices: 23.6 us -> 5.64 us  [flip(): return lax.ppermute(value, axis, pairs)]
    reduce_sum x19 -> x0, other arithmetic: 15.1 us -> none  [the longest x9 9.19 us: pick_rows(): jnp.sum(jnp.where(head_mask(stride, chosen), grouped, jnp.zeros((), tenso...]
    pallas_call x0 -> x7, Pallas kernels: none -> 12.2 us  [call(): pl.pallas_call(body, name=name, in_specs=[SMEM if x.dtype == jnp.int32 el...]
    all_to_all x0 -> x1, waiting for transfers between devices: none -> 12 us  [exchange(): lax.all_to_all(value, 'ctx', 0, 0, tiled=True, axis_index_groups=groups)]
  transfers between devices with their start and end apart: 20 -> 5, of which waited for: 5 -> 4; matrix products, arithmetic and copies ran while one was open for 27% -> 1% of each run, Pallas kernels for 0% -> 7%
where the time goes in v1:
time: 74 us; the launch traced here: 73.6 us
  blocking collectives  26.1 us (35%)
  waiting for transfers between devices  16.1 us (22%)
  Pallas kernels  12.2 us (16%)
  starting transfers between devices  12 us (16%)
  local copies, waits for them, and re-layouts  4.59 us (6%)
  between operations  2.65 us (4%)
    all_to_all x2, blocking collectives, exchange(): lax.all_to_all(value, 'ctx', 0, 0, tiled=True, axis_index_groups=groups)  26.1 us
    pallas_call x7, Pallas kernels, call(): pl.pallas_call(body, name=name, in_specs=[SMEM if x.dtype == jnp.int32 el...  12.2 us
    all_to_all x1, waiting for transfers between devices, exchange(): lax.all_to_all(value, 'ctx', 0, 0, tiled=True, axis_index_groups=groups)  12 us
    all_to_all x1, starting transfers between devices, exchange(): lax.all_to_all(value, 'ctx', 0, 0, tiled=True, axis_index_groups=groups)  6.32 us
    ppermute x4, starting transfers between devices, flip(): return lax.ppermute(value, axis, pairs)  5.64 us
    ppermute x4, waiting for transfers between devices, flip(): return lax.ppermute(value, axis, pairs)  4.1 us
    unnamed x12, local copies, waits for them, and re-layouts  3.81 us
  transfers between devices with their start and end apart: 5, of which 4 were waited for; matrix products, arithmetic and copies ran while one was open for 1% of the time, Pallas kernels for 7%

profile of v1, /device:TPU:0, one launch (start us, length us, event | category | flops | bytes accessed | tf_op | source)
XLA Modules:
  0.0 73.6 jit_solution(17014916730901892166)
XLA Ops:
  0.6 0.0 copy-start
  0.6 0.0 copy-start.1
  0.7 0.9 %copy-done.1 = bf16[1,128,1024]{2,1,0:T(8,128)(2,1)S(1)} copy-done((bf16[1,128,1024]{2,1,0:T(8,128)(2,1)S(1)}, bf16[1,128,1024]{2,1,0:T(8,128)(2,1)}, u32[]{:S(2)}) %copy-start.1) | copy-done | bytes 262168
  1.6 0.0 copy-start.2
  1.6 0.9 %copy-done.2 = bf16[1,128,1024]{2,1,0:T(8,128)(2,1)S(1)} copy-done((bf16[1,128,1024]{2,1,0:T(8,128)(2,1)S(1)}, bf16[1,128,1024]{2,1,0:T(8,128)(2,1)}, u32[]{:S(2)}) %copy-start.2) | copy-done | bytes 262168
  2.6 0.0 copy-start.3
  2.6 0.9 %copy-done.3 = bf16[1,128,1024]{2,1,0:T(8,128)(2,1)S(1)} copy-done((bf16[1,128,1024]{2,1,0:T(8,128)(2,1)S(1)}, bf16[1,128,1024]{2,1,0:T(8,128)(2,1)}, u32[]{:S(2)}) %copy-start.3) | copy-done | bytes 262168
  3.5 0.0 copy-start.4
  3.5 0.9 %copy-done.4 = bf16[1,128,1024]{2,1,0:T(8,128)(2,1)S(1)} copy-done((bf16[1,128,1024]{2,1,0:T(8,128)(2,1)S(1)}, bf16[1,128,1024]{2,1,0:T(8,128)(2,1)}, u32[]{:S(2)}) %copy-start.4) | copy-done | bytes 262168
  4.5 1.4 %split.1 = bf16[8,4,128,128]{3,2,1,0:T(8,128)(2,1)} custom-call(bf16[1,128,1024]{2,1,0:T(8,128)(2,1)S(1)} %copy-done.1, bf16[1,128,1024]{2,1,0:T(8,128)(2,1)S(1)} %copy-done.2, bf16[1,128,1024]{2,1,0:T(8,128)(2,1)S(1)} %copy-done.3, bf16[1,128,1024]{2,1,0:T(8,128)(2,1)S(1)} %copy-done.4), custom_call_target="tpu_custom_call" | custom-call | bytes 2097152 | tf_op jit(solution)/shard_map/split/pallas_call | solution.py:340
  5.9 0.0 copy-start.5
  5.9 6.3 %all-to-all-start = ((bf16[8,4,128,128]{3,2,1,0:T(8,128)(2,1)}), bf16[8,4,128,128]{3,2,1,0:T(8,128)(2,1)S(1)}, u32[]{:S(2)}, u32[]{:S(2)}) async-start(bf16[8,4,128,128]{3,2,1,0:T(8,128)(2,1)} %split.1), calls=%async_computation | async-start | bytes 2097152 | tf_op jit(solution)/shard_map/all_to_all | solution.py:383
  12.2 0.0 copy-done.5
  12.2 0.2 fusion
  12.4 0.5 slice.4
  14.8 12.0 %all-to-all-done = bf16[8,4,128,128]{3,2,1,0:T(8,128)(2,1)S(1)} async-done(((bf16[8,4,128,128]{3,2,1,0:T(8,128)(2,1)}), bf16[8,4,128,128]{3,2,1,0:T(8,128)(2,1)S(1)}, u32[]{:S(2)}, u32[]{:S(2)}) %all-to-all-start) | async-done | bytes 1048608 | tf_op jit(solution)/shard_map/all_to_all | solution.py:383
  26.9 2.7 %collective-permute-start = (bf16[8,2,1,16,128]{4,3,2,1,0:T(8,128)(2,1)S(1)}, bf16[8,2,1,16,128]{4,3,2,1,0:T(8,128)(2,1)S(1)}, u32[]{:S(2)}, u32[]{:S(2)}) collective-permute-start(bf16[8,2,1,16,128]{4,3,2,1,0:T(8,128)(2,1)S(1)} %constant_dynamic-slice_fusion), channel_id=1, source_target_pairs={{0,16},{2,18},{4,20},{6,22},{8,24},{10,26},{12,28},{14,30},{16,0},... | collective-permute-start | bytes 196616 | tf_op jit(solution)/shard_map/ppermute | solution.py:354
  29.5 0.0 copy-done
  29.5 0.1 dynamic-slice_bitcast_fusion.gain_ref
  29.6 1.9 %local_forward.1 = (f32[8,8,16,128]{3,2,1,0:T(8,128)S(1)}, f32[8,8,16,128]{3,2,1,0:T(8,128)S(1)}) custom-call(s32[3]{0:T(128)S(1)} %get-tuple-element.41.offs_ref, bf16[8,4,8,16,128]{4,3,2,1,0:T(8,128)(2,1)S(1)} %bitcast.10), custom_call_target="tpu_custom_call" | custom-call | flops 100000000 | bytes 2097164 | tf_op jit(solution)/shard_map/local_forward/pallas_call | solution.py:340
  31.5 1.8 %collective-permute-done = bf16[8,2,1,16,128]{4,3,2,1,0:T(8,128)(2,1)S(1)} collective-permute-done((bf16[8,2,1,16,128]{4,3,2,1,0:T(8,128)(2,1)S(1)}, bf16[8,2,1,16,128]{4,3,2,1,0:T(8,128)(2,1)S(1)}, u32[]{:S(2)}, u32[]{:S(2)}) %collective-permute-start) | collective-permute-done | bytes 65568 | tf_op jit(solution)/shard_map/ppermute | solution.py:354
  33.3 1.5 %crossing_forward.1 = (bf16[8,8,16,128]{3,2,1,0:T(8,128)(2,1)S(1)}, f32[8,8,16,128]{3,2,1,0:T(8,128)S(1)}, f32[8,32,128]{2,1,0:T(8,128)S(1)}) custom-call(s32[3]{0:T(128)S(1)} %get-tuple-element.41.offs_ref, bf16[8,4,8,16,128]{4,3,2,1,0:T(8,128)(2,1)S(1)} %bitcast.11, f32[8,8,16,128]{3,2,1,0:T(8,128)S(1)} %get-tuple-element.23.o_in, ...), custom_call_target="tpu_custom_call" | custom-call | bytes 3080716 | tf_op jit(solution)/shard_map/crossing_forward/pallas_call | solution.py:340
  34.8 8.5 %all_to_all.15.stats_ref = f32[8,32,128]{2,1,0:T(8,128)S(1)} all-to-all(f32[8,32,128]{2,1,0:T(8,128)S(1)} %get-tuple-element.27), channel_id=1, replica_groups={{0,2,4,6,8,10,12,14},{16,18,20,22,24,26,28,30},{1,3,5,7,9,11,13,15},{17..., dimensions={0} | all-to-all | bytes 262144 | tf_op jit(solution)/shard_map/all_to_all | solution.py:383
  43.3 2.3 %norm_and_crossing.1 = (bf16[8,8,16,128]{3,2,1,0:T(8,128)(2,1)S(1)}, bf16[8,8,16,128]{3,2,1,0:T(8,128)(2,1)S(1)}, f32[8,8,16,128]{3,2,1,0:T(8,128)S(1)}, f32[1,1...) custom-call(s32[3]{0:T(128)S(1)} %get-tuple-element.41.offs_ref, ...), custom_call_target="tpu_custom_call" | custom-call | bytes 3343372 | tf_op jit(solution)/shard_map/norm_and_crossing/pallas_call | solution.py:340
  45.6 2.8 %collective-permute-start.3 = (bf16[8,2,1,16,128]{4,3,2,1,0:T(8,128)(2,1)S(1)}, bf16[8,2,1,16,128]{4,3,2,1,0:T(8,128)(2,1)S(1)}, u32[]{:S(2)}, u32[]{:S(2)}) collective-permute-start(bf16[8,2,1,16,128]{4,3,2,1,0:T(8,128)(2,1)S(1)} %bitcast.16), channel_id=1, source_target_pairs={{0,16},{2,18},{4,20},{6,22},{8,24},{10,26},{12,28},{14,30},{16,0},... | collective-permute-start | bytes 196616 | tf_op jit(solution)/shard_map/ppermute | solution.py:354
  48.5 0.0 collective-permute-start.1
  48.5 1.1 %collective-permute-done.1 = f32[1,128]{1,0:T(1,128)S(1)} collective-permute-done((f32[1,128]{1,0:T(1,128)S(1)}, f32[1,128]{1,0:T(1,128)S(1)}, u32[]{:S(2)}, u32[]{:S(2)}) %collective-permute-start.1) | collective-permute-done | bytes 544 | tf_op jit(solution)/shard_map/ppermute | solution.py:354
  49.6 0.1 collective-permute-start.2
  49.7 3.1 %local_backward.1 = (bf16[8,2,8,16,128]{4,3,2,1,0:T(8,128)(2,1)S(1)}, f32[2,8,8,16,128]{4,3,2,1,0:T(8,128)S(1)}) custom-call(s32[3]{0:T(128)S(1)} %get-tuple-element.41.offs_ref, bf16[8,4,8,16,128]{4,3,2,1,0:T(8,128)(2,1)S(1)} %bitcast.13, bf16[8,8,16,128]{3,2,1,0:T(8,128)(2,1)S(1)} %get-tuple-element.28.attended_ref, ...), custom_call_target="tpu_custom_call" | custom-call | flops 300000000 | bytes 4390924 | tf_op jit(solution)/shard_map/local_backward/pallas_call | solution.py:340
  52.8 1.2 %collective-permute-done.2 = f32[1,128]{1,0:T(1,128)S(1)} collective-permute-done((f32[1,128]{1,0:T(1,128)S(1)}, f32[1,128]{1,0:T(1,128)S(1)}, u32[]{:S(2)}, u32[]{:S(2)}) %collective-permute-start.2) | collective-permute-done | bytes 544 | tf_op jit(solution)/shard_map/ppermute | solution.py:354
  54.0 0.0 collective-permute-done.3.refs_0_
  54.0 0.7 pack.1
  54.7 17.6 %all_to_all.16.in_ref = bf16[8,528,128]{2,1,0:T(8,128)(2,1)S(1)} all-to-all(bf16[8,528,128]{2,1,0:T(8,128)(2,1)S(1)} %pack.1), channel_id=1, replica_groups={{0,2,4,6,8,10,12,14},{16,18,20,22,24,26,28,30},{1,3,5,7,9,11,13,15},{17..., dimensions={0} | all-to-all | bytes 2162688 | tf_op jit(solution)/shard_map/all_to_all | solution.py:383
  72.3 1.3 %join.1 = (bf16[1,128,1024]{2,1,0:T(8,128)(2,1)}, bf16[1,128,1024]{2,1,0:T(8,128)(2,1)}, bf16[1,128,1024]{2,1,0:T(8,128)(2,1)}, bf16[1,128,1024]{2,1,0:T(8,128)(2,1)}, f32[1,1024]{1,0:T(1,128)}) custom-call(bf16[8,528,128]{2,1,0:T(8,128)(2,1)S(1)} %all_to_all.16.in_ref), custom_call_target="tpu_custom_call" | custom-call | bytes 2134016 | tf_op jit(solution)/shard_map/join/pallas_call | solution.py:340
  (3 shorter events, 0.0 us)
Async XLA Ops:
  0.6 28.9 %copy-start = (f32[1024]{0:T(1024)S(1)}, f32[1024]{0:T(1024)}, u32[]{:S(2)}) copy-start(f32[1024]{0:T(1024)} %param.10) | copy-start | bytes 12292
  0.6 1.0 %copy-start.1 = (bf16[1,128,1024]{2,1,0:T(8,128)(2,1)S(1)}, bf16[1,128,1024]{2,1,0:T(8,128)(2,1)}, u32[]{:S(2)}) copy-start(bf16[1,128,1024]{2,1,0:T(8,128)(2,1)} %q_ref.1) | copy-start | bytes 786436
  1.6 0.9 %copy-start.2 = (bf16[1,128,1024]{2,1,0:T(8,128)(2,1)S(1)}, bf16[1,128,1024]{2,1,0:T(8,128)(2,1)}, u32[]{:S(2)}) copy-start(bf16[1,128,1024]{2,1,0:T(8,128)(2,1)} %k_ref.1) | copy-start | bytes 786436
  2.6 0.9 %copy-start.3 = (bf16[1,128,1024]{2,1,0:T(8,128)(2,1)S(1)}, bf16[1,128,1024]{2,1,0:T(8,128)(2,1)}, u32[]{:S(2)}) copy-start(bf16[1,128,1024]{2,1,0:T(8,128)(2,1)} %v_ref.1) | copy-start | bytes 786436
  3.5 0.9 %copy-start.4 = (bf16[1,128,1024]{2,1,0:T(8,128)(2,1)S(1)}, bf16[1,128,1024]{2,1,0:T(8,128)(2,1)}, u32[]{:S(2)}) copy-start(bf16[1,128,1024]{2,1,0:T(8,128)(2,1)} %g_ref.1) | copy-start | bytes 786436
  5.9 6.3 %copy-start.5 = (s32[3,8]{1,0:T(4,128)S(1)}, s32[3,8]{1,0:T(4,128)}, u32[]{:S(2)}) copy-start(s32[3,8]{1,0:T(4,128)} %param.11) | copy-start | bytes 292
  5.9 21.0 %all-to-all-start = ((bf16[8,4,128,128]{3,2,1,0:T(8,128)(2,1)}), bf16[8,4,128,128]{3,2,1,0:T(8,128)(2,1)S(1)}, u32[]{:S(2)}, u32[]{:S(2)}) async-start(bf16[8,4,128,128]{3,2,1,0:T(8,128)(2,1)} %split.1), calls=%async_computation | async-start | bytes 2097152 | tf_op jit(solution)/shard_map/all_to_all | solution.py:383
  26.9 6.4 %collective-permute-start = (bf16[8,2,1,16,128]{4,3,2,1,0:T(8,128)(2,1)S(1)}, bf16[8,2,1,16,128]{4,3,2,1,0:T(8,128)(2,1)S(1)}, u32[]{:S(2)}, u32[]{:S(2)}) collective-permute-start(bf16[8,2,1,16,128]{4,3,2,1,0:T(8,128)(2,1)S(1)} %constant_dynamic-slice_fusion), channel_id=1, source_target_pairs={{0,16},{2,18},{4,20},{6,22},{8,24},{10,26},{12,28},{14,30},{16,0},... | collective-permute-start | bytes 196616 | tf_op jit(solution)/shard_map/ppermute | solution.py:354
  45.6 8.4 %collective-permute-start.3 = (bf16[8,2,1,16,128]{4,3,2,1,0:T(8,128)(2,1)S(1)}, bf16[8,2,1,16,128]{4,3,2,1,0:T(8,128)(2,1)S(1)}, u32[]{:S(2)}, u32[]{:S(2)}) collective-permute-start(bf16[8,2,1,16,128]{4,3,2,1,0:T(8,128)(2,1)S(1)} %bitcast.16), channel_id=1, source_target_pairs={{0,16},{2,18},{4,20},{6,22},{8,24},{10,26},{12,28},{14,30},{16,0},... | collective-permute-start | bytes 196616 | tf_op jit(solution)/shard_map/ppermute | solution.py:354
  48.5 1.1 %collective-permute-start.1 = (f32[1,128]{1,0:T(1,128)S(1)}, f32[1,128]{1,0:T(1,128)S(1)}, u32[]{:S(2)}, u32[]{:S(2)}) collective-permute-start(f32[1,128]{1,0:T(1,128)S(1)} %get-tuple-element.34), channel_id=1, source_target_pairs={{0,1},{1,0},{2,3},{3,2},{4,5},{5,4},{6,7},{7,6},{8,9},{9,8},{10,11... | collective-permute-start | bytes 1544 | tf_op jit(solution)/shard_map/ppermute | solution.py:354
  49.6 4.4 %collective-permute-start.2 = (f32[1,128]{1,0:T(1,128)S(1)}, f32[1,128]{1,0:T(1,128)S(1)}, u32[]{:S(2)}, u32[]{:S(2)}) collective-permute-start(f32[1,128]{1,0:T(1,128)S(1)} %add.23), channel_id=1, source_target_pairs={{0,16},{2,18},{4,20},{6,22},{8,24},{10,26},{12,28},{14,30},{16,0},... | collective-permute-start | bytes 1544 | tf_op jit(solution)/shard_map/ppermute | solution.py:354

commit v2 on v1

v2 whole, which is shorter than its diff:
```python
import functools
import math

import jax
import jax.numpy as jnp
from jax import lax
from jax.experimental import pallas as pl
from jax.experimental.pallas import tpu as pltpu
from jax.sharding import PartitionSpec as P

SPAN_A = 2
RATE_A = 1
SPAN_B = 4
RATE_B = 2
SPAN_C = 16
RATE_C = 8

EPSILON = 1e-05
LOG2E = math.log2(math.e)
TILE = 16
STAGED = 4
F32 = jnp.float32
BF16 = jnp.bfloat16

NT = (((1,), (1,)), ((), ()))
TN = (((0,), (0,)), ((), ()))
NN = (((1,), (0,)), ((), ()))


def dot(left, right, dims):
    return lax.dot_general(left, right, dims, preferred_element_type=F32)


def two_parts(value):
    high = value.astype(BF16)
    return jnp.concatenate([high, (value - high.astype(F32)).astype(BF16)], axis=1)


def row_order(tokens, rate, transposed):
    short = tokens // rate
    placed = lax.broadcasted_iota(jnp.int32, (tokens, tokens), 1 if transposed else 0)
    source = lax.broadcasted_iota(jnp.int32, (tokens, tokens), 0 if transposed else 1)
    return (source == (placed % short) * rate + placed // short).astype(BF16)


def split_kernel(rate, q_ref, k_ref, v_ref, g_ref, out_ref):
    group, _, tokens, hd = out_ref.shape
    order = row_order(tokens, rate, False)
    for t, ref in enumerate((q_ref, k_ref, v_ref, g_ref)):
        moved = dot(order, ref[0], NN).astype(BF16)
        for h in range(group):
            out_ref[h, t] = moved[:, h * hd : (h + 1) * hd]


class Level:
    def __init__(self, index, span, rate, top_rate, fold, group):
        self.index = index
        self.rate = rate
        self.count = top_rate // rate
        self.crossing = span > group
        self.bits = span.bit_length() - group.bit_length()
        self.pieces = min(span, group) // fold
        self.segments = 1 if self.crossing else group // span

    def starts(self, offs):
        first = 0 if self.index == 0 else offs[self.index - 1, 0]
        return [first + self.rate * i for i in range(self.count)]

    def places(self, offs_ref, segment):
        low = segment * self.pieces
        return [(nb, b) for b in self.starts(offs_ref) for nb in range(low, low + self.pieces)]


def gather(read, places):
    return jnp.concatenate([read(nb, b) for nb, b in places], axis=0)


def scores_of(query, key, scale):
    return dot(query, key, NT) * scale


def forward(query, key, value, scale):
    hd = value.shape[1]
    scores = scores_of(query, key, scale)
    top = jnp.max(scores, axis=-1, keepdims=True)
    weights = jnp.exp2(scores - top).astype(BF16)
    both = dot(weights, jnp.concatenate([value, jnp.ones_like(value)], axis=1), NN)
    mixed, total = both[:, :hd], both[:, hd:]
    return mixed / total, top + jnp.log2(total)


def merge(mixed, lse, more, more_lse):
    top = jnp.maximum(lse, more_lse)
    left, right = jnp.exp2(lse - top), jnp.exp2(more_lse - top)
    total = left + right
    return (mixed * left + more * right) / total, top + jnp.log2(total)


def merge_into(o_ref, lse_ref, places, more, more_lse):
    mixed, lse = merge(
        gather(lambda nb, b: o_ref[nb, b], places),
        gather(lambda nb, b: lse_ref[nb, b], places),
        more,
        more_lse,
    )
    put(o_ref, places, mixed)
    put(lse_ref, places, lse)


def put(ref, places, rows):
    size = ref.shape[-2]
    for i, (nb, b) in enumerate(places):
        ref[nb, b] = rows[i * size : (i + 1) * size]


def add(ref, places, rows):
    size = ref.shape[-2]
    for i, (nb, b) in enumerate(places):
        ref[nb, b] += rows[i * size : (i + 1) * size]


def crossing_keys(places, x_ref, other_ref, t):
    found = [x_ref[nb, t, b] for nb, b in places]
    others, pieces, _, count = other_ref.shape[:4]
    found += [
        other_ref[e, nb, t - 1, i]
        for e in range(others)
        for i in range(count)
        for nb in range(pieces)
    ]
    return jnp.concatenate(found, axis=0)


def all_blocks(levels, offs_ref, x_ref, others):
    crossing = 0
    for level in levels:
        if level.crossing:
            other_ref = others[crossing]
            crossing += 1
        for segment in range(level.segments):
            places = level.places(offs_ref, segment)
            query = gather(lambda nb, b: x_ref[nb, 0, b], places)
            if level.crossing:
                key, value = (crossing_keys(places, x_ref, other_ref, t) for t in (1, 2))
            else:
                key, value = (gather(lambda nb, b, t=t: x_ref[nb, t, b], places) for t in (1, 2))
            yield level, places, query, key, value


def row_sums(attn, grad, gain):
    hd = attn.shape[-1]
    attn = attn.astype(BF16).astype(F32)
    scaled = grad.astype(F32) * gain
    total = jnp.sum(attn, axis=-1, keepdims=True)
    away = attn - total * (1.0 / hd)
    return (
        total,
        jnp.sum(away * away, axis=-1, keepdims=True),
        jnp.sum(scaled, axis=-1, keepdims=True),
        jnp.sum(scaled * away, axis=-1, keepdims=True),
    )


def forward_kernel(levels, scale, offs_ref, gain_ref, x_ref, o_ref, lse_ref, table_ref):
    pieces, rate, size, hd = o_ref.shape
    for level, places, query, key, value in all_blocks(levels, offs_ref, x_ref, ()):
        mixed, lse = forward(query, key, value, scale)
        if level.index == 0:
            put(o_ref, places, mixed)
            put(lse_ref, places, lse)
        else:
            merge_into(o_ref, lse_ref, places, mixed, lse)
    per = rate * size // hd
    chunks = pieces * per
    lane = lax.broadcasted_iota(jnp.int32, (hd, hd), 1)
    table = jnp.zeros((hd, hd), F32)
    for nb in range(pieces):
        attn = o_ref[nb].reshape(rate * size, hd)
        grad = x_ref[nb, 3].reshape(rate * size, hd)
        for part in range(per):
            rows = slice(part * hd, (part + 1) * hd)
            for i, column in enumerate(row_sums(attn[rows], grad[rows], gain_ref[...])):
                table = jnp.where(lane == i * chunks + nb * per + part, column, table)
    table_ref[...] = table


def crossing_forward_kernel(levels, scale, offs_ref, gain_ref, x_ref, o_in, lse_in, table_ref, *refs):
    others, (attn_ref, lse_ref, stats_ref, o_ref, sums_ref) = refs[:-5], refs[-5:]
    pieces, rate, size, hd = o_ref.shape
    per = rate * size // hd
    chunks = pieces * per
    lane = lax.broadcasted_iota(jnp.int32, (size, hd), 1)
    o_ref[...] = o_in[...]
    lse_ref[...] = lse_in[...]
    sums_ref[...] = table_ref[...]
    for level, places, query, key, value in all_blocks(levels, offs_ref, x_ref, others):
        merge_into(o_ref, lse_ref, places, *forward(query, key, value, scale))
        sums = row_sums(
            gather(lambda nb, b: o_ref[nb, b], places),
            gather(lambda nb, b: x_ref[nb, 3, b], places),
            gain_ref[...],
        )
        for j, (nb, b) in enumerate(places):
            chunk = nb * per + b * size // hd
            rows = pl.ds(pl.multiple_of(b * size % hd, size), size)
            table = sums_ref[rows, :]
            for i, column in enumerate(sums):
                table = jnp.where(lane == i * chunks + chunk, column[j * size : (j + 1) * size], table)
            sums_ref[rows, :] = table
    attn_ref[...] = o_ref[...].astype(BF16)
    turned = sums_ref[...].T[: 4 * chunks]
    for peer in range(stats_ref.shape[0]):
        stats_ref[peer] = turned


def norm_kernel(heads, levels, scale, score_scale, offs_ref, x_ref, attn_ref, lse_ref, gain_ref, stats_ref, *refs):
    count = len(levels)
    others, refs = refs[:count], refs[count:]
    attended_ref, grad_ref, delta_ref, gsum_ref = refs[:4]
    own_refs, sent_refs = refs[4 : 4 + count], refs[4 + count :]
    pieces, rate, size, hd = attn_ref.shape
    chunks = pieces * rate * size // hd
    per = chunks // pieces
    width = heads * hd
    sums, squares, scaleds, products = (
        [stats_ref[h, i * chunks : (i + 1) * chunks, :] for h in range(heads)] for i in range(4)
    )
    mean = functools.reduce(jnp.add, sums) * (1.0 / width)
    apart = [total * (1.0 / hd) - mean for total in sums]
    variance = functools.reduce(
        jnp.add, [square + hd * a * a for square, a in zip(squares, apart)]
    ) * (1.0 / width)
    inverse = lax.rsqrt(variance + EPSILON)
    first = functools.reduce(jnp.add, scaleds) * (1.0 / width)
    second = (
        functools.reduce(jnp.add, [p + a * s for p, a, s in zip(products, apart, scaleds)])
        * (1.0 / width)
        * inverse
    )
    table = jnp.concatenate(
        [mean, inverse, first, second, jnp.zeros((hd - 4 * chunks, hd), F32)], axis=0
    )
    table = two_parts(table.T)
    lane = lax.broadcasted_iota(jnp.int32, (hd, 2 * hd), 1) % chunks
    picker = lax.broadcasted_iota(jnp.int32, (2 * hd, 4 * hd), 0) % hd // chunks
    picker = (picker == lax.broadcasted_iota(jnp.int32, (2 * hd, 4 * hd), 1) // hd).astype(BF16)
    picked = [jnp.where(lane == chunk, table, jnp.zeros_like(table)) for chunk in range(chunks)]
    columns = dot(jnp.concatenate(picked, axis=0), picker, NN)
    gsum = jnp.zeros((1, hd), F32)
    products = []
    shape = (rate, size, hd)
    for nb in range(pieces):
        attn_all = attn_ref[nb].reshape(rate * size, hd).astype(F32)
        grad_all = x_ref[nb, 3].reshape(rate * size, hd).astype(F32)
        attended, grads = [], []
        for part in range(per):
            chunk = nb * per + part
            mean_c, inv_c, first_c, second_c = (
                columns[chunk * hd : (chunk + 1) * hd, i * hd : (i + 1) * hd] for i in range(4)
            )
            attn = attn_all[part * hd : (part + 1) * hd]
            upstream = grad_all[part * hd : (part + 1) * hd]
            normed = (attn - mean_c) * inv_c
            attended.append((normed * gain_ref[...]).astype(BF16))
            grad = (inv_c * (upstream * gain_ref[...] - first_c - normed * second_c)).astype(BF16)
            grads.append(grad)
            products.append(two_parts(grad.astype(F32) * attn))
            gsum = gsum + jnp.sum(upstream * normed, axis=0, keepdims=True)
        attended_ref[nb] = jnp.concatenate(attended, axis=0).reshape(shape)
        grad_ref[nb] = jnp.concatenate(grads, axis=0).reshape(shape)
    ones = jnp.ones((2 * hd, hd), BF16)
    deltas = dot(jnp.concatenate(products, axis=0), ones, NN)
    for nb in range(pieces):
        delta_ref[nb] = deltas[nb * rate * size : (nb + 1) * rate * size].reshape(shape)
    gsum_ref[...] = gsum
    blocks = list(all_blocks(levels, offs_ref, x_ref, others))
    results = backward(blocks, grad_ref, lse_ref, delta_ref, scale, score_scale)
    for i, parts in enumerate(results):
        own = parts[0].shape[0]
        others_count, pieces, _, steps, size, _ = sent_refs[i].shape
        for t, part in enumerate(parts):
            own_refs[i][t] = part[:own]
            if t > 0:
                low = own
                for e in range(others_count):
                    for step in range(steps):
                        for nb in range(pieces):
                            rows = part[low : low + size].astype(sent_refs[i].dtype)
                            sent_refs[i][e, nb, t - 1, step] = rows
                            low += size


def backward(blocks, grad_ref, lse_ref, delta_ref, scale, score_scale):
    def wide(ref, places, key):
        column = gather(lambda nb, b: ref[nb, b], places)
        return jnp.concatenate([column] * (key.shape[0] // column.shape[1]), axis=1)

    grads = [gather(lambda nb, b: grad_ref[nb, b], places) for _, places, _, _, _ in blocks]
    scores = [scores_of(query, key, score_scale) for _, _, query, key, _ in blocks]
    prob_grads = [dot(grad, block[4], NT) for grad, block in zip(grads, blocks)]
    probs = [
        jnp.exp2(score - wide(lse_ref, places, key))
        for score, (_, places, _, key, _) in zip(scores, blocks)
    ]
    score_grads = [
        (prob * (prob_grad - wide(delta_ref, places, key))).astype(BF16)
        for prob, prob_grad, (_, places, _, key, _) in zip(probs, prob_grads, blocks)
    ]
    queries = [dot(each, block[3], NN) * scale for each, block in zip(score_grads, blocks)]
    keys = [dot(each, block[2], TN) * scale for each, block in zip(score_grads, blocks)]
    values = [dot(prob.astype(BF16), grad, TN) for prob, grad in zip(probs, grads)]
    return list(zip(queries, keys, values))


def local_kernel(levels, crossing, scale, score_scale, offs_ref, x_ref, attended_ref, grad_ref, lse_ref, delta_ref, *refs):
    own_refs, (out_ref, kv_ref, dq_ref) = refs[: len(crossing)], refs[len(crossing) :]
    accumulators = (dq_ref, kv_ref.at[0], kv_ref.at[1])
    blocks = list(all_blocks(levels, offs_ref, x_ref, ()))
    for low in range(0, len(blocks), STAGED):
        some = blocks[low : low + STAGED]
        results = backward(some, grad_ref, lse_ref, delta_ref, scale, score_scale)
        for i, ref in enumerate(accumulators):
            for (level, places, *_), parts in zip(some, results):
                (put if level.index == 0 else add)(ref, places, parts[i])
    for level, own_ref in zip(crossing, own_refs):
        places = level.places(offs_ref, 0)
        for t, ref in enumerate(accumulators):
            add(ref, places, own_ref[t])
    out_ref[:, 0] = dq_ref[...].astype(BF16)
    out_ref[:, 1] = attended_ref[...]


def pack_kernel(crossing, fold, offs_ref, main_ref, kv_in, gsum_ref, *refs):
    arrived_refs, (out_ref, kv_ref) = refs[: len(crossing)], refs[len(crossing) :]
    pieces, _, rate, size, hd = main_ref.shape
    rows = rate * size
    kv_ref[...] = kv_in[...]
    for level, arrived_ref in zip(crossing, arrived_refs):
        for i, b in enumerate(level.starts(offs_ref)):
            for nb in range(level.pieces):
                for t in range(2):
                    kv_ref[t, nb, b] += arrived_ref[nb, t, i].astype(F32)
    total = jnp.broadcast_to(gsum_ref[...], (TILE, hd))
    high = total.astype(BF16).astype(F32)
    middle = (total - high).astype(BF16).astype(F32)
    low = total - high - middle
    row = lax.broadcasted_iota(jnp.int32, (TILE, hd), 0)
    coded = jnp.where(row == 0, high, jnp.where(row == 1, middle, jnp.where(row == 2, low, 0.0)))
    for nb in range(pieces):
        for t in range(2):
            out_ref[nb, t * rows : (t + 1) * rows] = main_ref[nb, t].reshape(rows, hd)
            out_ref[nb, (t + 2) * rows : (t + 3) * rows] = (
                kv_ref[t, nb].reshape(rows, hd).astype(BF16)
            )
        for f in range(fold):
            out_ref[nb, 4 * rows + f * TILE : 4 * rows + (f + 1) * TILE] = coded.astype(BF16)


def join_kernel(rate, factor, in_ref, dq_ref, attended_ref, dk_ref, dv_ref, gain_ref):
    group, _, hd = in_ref.shape
    tokens = dq_ref.shape[1]
    order = row_order(tokens, rate, True)
    for t, ref in enumerate((dq_ref, attended_ref, dk_ref, dv_ref)):
        for h in range(group):
            moved = dot(order, in_ref[h, t * tokens : (t + 1) * tokens, :], NN)
            ref[0, :, h * hd : (h + 1) * hd] = moved.astype(BF16)
    for h in range(group):
        coded = in_ref[h, 4 * tokens : 4 * tokens + TILE, :].astype(F32)
        gain_ref[:, h * hd : (h + 1) * hd] = jnp.sum(coded, axis=0, keepdims=True) * factor


VMEM = pl.BlockSpec(memory_space=pltpu.VMEM)


def call(body, name, inputs, outputs, scratch=(), flops=0, limit=24):
    shapes = [jax.ShapeDtypeStruct(*output) for output in outputs]
    moved = sum(x.size * x.dtype.itemsize for x in list(inputs) + shapes)
    return list(pl.pallas_call(
        body,
        name=name,
        in_specs=[VMEM] * len(inputs),
        out_specs=[VMEM] * len(shapes),
        out_shape=shapes,
        scratch_shapes=[pltpu.VMEM(*each) for each in scratch],
        cost_estimate=pl.CostEstimate(flops=flops, bytes_accessed=moved, transcendentals=0),
        compiler_params=pltpu.CompilerParams(vmem_limit_bytes=limit * 1024 * 1024),
    )(*inputs))


def flip(value, axis, bit):
    pairs = [(source, source ^ (1 << bit)) for source in range(lax.axis_size(axis))]
    return lax.ppermute(value, axis, pairs)


def shards(queries, key_rows, value_rows, out_grad, norm_gain, offsets):
    tokens, width = queries.shape[1:]
    group = offsets.shape[1]
    hd = width // group
    ctx_count = lax.axis_size("ctx")
    dp_count = lax.axis_size("dp")
    scale = hd ** (-0.5)
    score_scale = scale * LOG2E
    spans = [
        (SPAN_A, RATE_A),
        (SPAN_B, RATE_B),
        (SPAN_C, RATE_C),
        (ctx_count // 2, ctx_count // 4),
    ]
    rate = max(r for _, r in spans)
    short = tokens // rate
    fold = max(1, TILE // short)
    size = short * fold
    pieces = group // fold
    levels = [Level(i, span, r, rate, fold, group) for i, (span, r) in enumerate(spans)]
    local = [level for level in levels if not level.crossing]
    crossing = [level for level in levels if level.crossing]
    groups = [list(range(low, low + group)) for low in range(0, ctx_count, group)]
    low_bit = group.bit_length() - 1

    def exchange(value):
        return lax.all_to_all(value, "ctx", 0, 0, tiled=True, axis_index_groups=groups)

    head = lax.axis_index("ctx") % group
    offs = lax.dynamic_slice(offsets, (0, head), (offsets.shape[0], 1))
    offs_rows = jnp.broadcast_to(offs, (offsets.shape[0], hd))
    gain = lax.dynamic_slice(norm_gain, (head * hd,), (hd,))[None]

    (sent,) = call(
        functools.partial(split_kernel, rate),
        "split",
        [queries, key_rows, value_rows, out_grad],
        [((group, 4, tokens, hd), BF16)],
        limit=60,
    )
    x = exchange(sent)
    if fold > 1:
        x = x.reshape(pieces, fold, 4, rate, short, hd).transpose(0, 2, 3, 1, 4, 5)
    x = x.reshape(pieces, 4, rate, size, hd)

    others = []
    for level in crossing:
        own = [
            lax.dynamic_slice(x, (0, 1, b, 0, 0), (pieces, 2, 1, size, hd))
            for b in level.starts(offs)
        ]
        blocks = [jnp.concatenate(own, axis=2)]
        for bit in range(level.bits):
            blocks += [flip(block, "ctx", low_bit + bit) for block in blocks]
        others.append(jnp.stack(blocks[1:]))

    state = (pieces, rate, size, hd)
    chunks = group * tokens // hd
    o, lse, table = call(
        functools.partial(forward_kernel, local, score_scale),
        "local_forward",
        [offs_rows, gain, x],
        [(state, F32), (state, F32), ((hd, hd), F32)],
        flops=10**8,
    )
    attn, lse, stats = call(
        functools.partial(crossing_forward_kernel, crossing, score_scale),
        "crossing_forward",
        [offs_rows, gain, x, o, lse, table] + others,
        [(state, BF16), (state, F32), ((group, 4 * chunks, hd), F32)],
        scratch=[(state, F32), ((hd, hd), F32)],
    )
    stats = exchange(stats)
    outs = [(state, BF16), (state, BF16), (state, F32), ((1, hd), F32)]
    outs += [((3, pieces * level.count * size, hd), F32) for level in crossing]
    sent_types = [BF16 if level.bits == 1 else F32 for level in crossing]
    outs += [(other.shape, kind) for other, kind in zip(others, sent_types)]
    attended, grad, delta, gsum, *rest = call(
        functools.partial(norm_kernel, group, crossing, scale, score_scale),
        "norm_and_crossing",
        [offs_rows, x, attn, lse, gain, stats] + others,
        outs,
        flops=10**7,
    )
    owns, parts = rest[: len(crossing)], rest[len(crossing) :]

    arrived = []
    for level, part in zip(crossing, parts):
        partial = [None] + [part[e] for e in range(part.shape[0])]
        for bit in reversed(range(level.bits)):
            half = 1 << bit
            came = [flip(block.astype(BF16), "ctx", low_bit + bit) for block in partial[half:]]
            partial = [
                c if b is None else b.astype(F32) + c.astype(F32)
                for b, c in zip(partial[:half], came)
            ]
        arrived.append(partial[0])
    for axis, count, first in (("dp", dp_count, 0), ("ctx", ctx_count, low_bit)):
        for bit in range(first, count.bit_length() - 1):
            gsum = gsum + flip(gsum, axis, bit)

    main, kv = call(
        functools.partial(local_kernel, local, crossing, scale, score_scale),
        "local_backward",
        [offs_rows, x, attended, grad, lse, delta] + owns,
        [((pieces, 2, rate, size, hd), BF16), ((2,) + state, F32)],
        scratch=[(state, F32)],
        flops=3 * 10**8,
    )
    (packed,) = call(
        functools.partial(pack_kernel, crossing, fold),
        "pack",
        [offs_rows, main, kv, gsum] + arrived,
        [((pieces, 4 * rate * size + TILE * fold, hd), BF16)],
        scratch=[((2,) + state, F32)],
    )
    if fold > 1:
        rows = packed[:, : 4 * rate * size].reshape(pieces, 4, rate, fold, short, hd)
        rows = rows.transpose(0, 3, 1, 2, 4, 5).reshape(group, 4 * tokens, hd)
        packed = jnp.concatenate([rows, packed[:, 4 * rate * size :].reshape(group, TILE, hd)], 1)
    back = exchange(packed)
    factor = 1.0 / math.sqrt(ctx_count * dp_count * tokens)
    row = ((1, tokens, width), BF16)
    dq, attended, dk, dv, gain_grad = call(
        functools.partial(join_kernel, rate, factor),
        "join",
        [back],
        [row, row, row, row, ((1, width), F32)],
    )
    return attended, dq, dk, dv, gain_grad[0]


def solution(mesh):
    rows = P("dp", "ctx", None)
    return jax.shard_map(
        shards,
        mesh=mesh,
        in_specs=(rows, rows, rows, rows, P(), P()),
        out_specs=(rows, rows, rows, rows, P()),
        check_vma=False,
    )
```

time: 74 us -> 68.8 us (0.930)
  local copies, waits for them, and re-layouts: 4.59 us -> 0.87 us
  Pallas kernels: 12.2 us -> 9.05 us
  waiting for transfers between devices: 16.1 us -> 17.9 us
    unnamed x12 -> x4, local copies, waits for them, and re-layouts: 3.81 us -> 0.01 us
    pallas_call x7, Pallas kernels: 12.2 us -> 9.05 us  [call(): pl.pallas_call(body, name=name, in_specs=[VMEM] * len(inputs), out_specs=...]
    ppermute x4, waiting for transfers between devices: 4.1 us -> 5.88 us  [flip(): return lax.ppermute(value, axis, pairs)]
  transfers between devices with their start and end apart: 5 -> 5, of which waited for: 4 -> 4; matrix products, arithmetic and copies ran while one was open for 1% -> 1% of each run, Pallas kernels for 7% -> 5%
where the time goes in v2:
time: 68.8 us; the launch traced here: 68.5 us
  blocking collectives  26.1 us (38%)
  waiting for transfers between devices  17.9 us (26%)
  starting transfers between devices  12 us (17%)
  Pallas kernels  9.05 us (13%)
  between operations  2.64 us (4%)
  local copies, waits for them, and re-layouts  0.87 us (1%)
    all_to_all x2, blocking collectives, exchange(): lax.all_to_all(value, 'ctx', 0, 0, tiled=True, axis_index_groups=groups)  26.1 us
    all_to_all x1, waiting for transfers between devices, exchange(): lax.all_to_all(value, 'ctx', 0, 0, tiled=True, axis_index_groups=groups)  12 us
    pallas_call x7, Pallas kernels, call(): pl.pallas_call(body, name=name, in_specs=[VMEM] * len(inputs), out_specs=...  9.05 us
    all_to_all x1, starting transfers between devices, exchange(): lax.all_to_all(value, 'ctx', 0, 0, tiled=True, axis_index_groups=groups)  6.32 us
    ppermute x4, waiting for transfers between devices, flip(): return lax.ppermute(value, axis, pairs)  5.88 us
    ppermute x4, starting transfers between devices, flip(): return lax.ppermute(value, axis, pairs)  5.64 us
  transfers between devices with their start and end apart: 5, of which 4 were waited for; matrix products, arithmetic and copies ran while one was open for 1% of the time, Pallas kernels for 5%

profile of v2, /device:TPU:0, one launch (start us, length us, event | category | flops | bytes accessed | tf_op | source)
XLA Modules:
  0.0 68.5 jit_solution(12402200625535162760)
XLA Ops:
  0.6 0.0 copy-start
  0.6 2.6 %split.1 = bf16[8,4,128,128]{3,2,1,0:T(8,128)(2,1)} custom-call(bf16[1,128,1024]{2,1,0:T(8,128)(2,1)} %q_ref.1, bf16[1,128,1024]{2,1,0:T(8,128)(2,1)} %k_ref.1, bf16[1,128,1024]{2,1,0:T(8,128)(2,1)} %v_ref.1, bf16[1,128,1024]{2,1,0:T(8,128)(2,1)} %g_ref.1), custom_call_target="tpu_custom_call" | custom-call | bytes 2097152 | tf_op jit(solution)/shard_map/split/pallas_call | solution.py:378
  3.2 0.0 copy-start.1
  3.2 6.3 %all-to-all-start = ((bf16[8,4,128,128]{3,2,1,0:T(8,128)(2,1)}), bf16[8,4,128,128]{3,2,1,0:T(8,128)(2,1)S(1)}, u32[]{:S(2)}, u32[]{:S(2)}) async-start(bf16[8,4,128,128]{3,2,1,0:T(8,128)(2,1)} %split.1), calls=%async_computation | async-start | bytes 2097152 | tf_op jit(solution)/shard_map/all_to_all | solution.py:421
  9.6 0.0 copy-done.1
  9.6 0.2 fusion
  9.7 0.5 slice.3
  12.2 12.0 %all-to-all-done = bf16[8,4,128,128]{3,2,1,0:T(8,128)(2,1)S(1)} async-done(((bf16[8,4,128,128]{3,2,1,0:T(8,128)(2,1)}), bf16[8,4,128,128]{3,2,1,0:T(8,128)(2,1)S(1)}, u32[]{:S(2)}, u32[]{:S(2)}) %all-to-all-start) | async-done | bytes 1048608 | tf_op jit(solution)/shard_map/all_to_all | solution.py:421
  24.2 2.7 %collective-permute-start = (bf16[8,2,1,16,128]{4,3,2,1,0:T(8,128)(2,1)S(1)}, bf16[8,2,1,16,128]{4,3,2,1,0:T(8,128)(2,1)S(1)}, u32[]{:S(2)}, u32[]{:S(2)}) collective-permute-start(bf16[8,2,1,16,128]{4,3,2,1,0:T(8,128)(2,1)S(1)} %constant_dynamic-slice_fusion), channel_id=1, source_target_pairs={{0,16},{2,18},{4,20},{6,22},{8,24},{10,26},{12,28},{14,30},{16,0},... | collective-permute-start | bytes 196616 | tf_op jit(solution)/shard_map/ppermute | solution.py:392
  26.9 0.0 copy-done
  26.9 0.1 dynamic-slice_bitcast_fusion.gain_ref
  27.0 0.1 broadcast_in_dim.11.offs_ref
  27.0 1.5 %local_forward.1 = (f32[8,8,16,128]{3,2,1,0:T(8,128)S(1)}, f32[8,8,16,128]{3,2,1,0:T(8,128)S(1)}, f32[128,128]{1,0:T(8,128)S(1)}) custom-call(s32[3,128]{1,0:T(4,128)S(1)} %broadcast_in_dim.11.offs_ref, f32[1,128]{1,0:T(1,128)S(1)} %dynamic-slice_bitcast_fusion.gain_ref, bf16[8,4,8,16,128]{4,3,2,1,0:T(8,128)(2,1)S(1)} %bitcast.10), custom_call_target="tpu_custom_call" | custom-call | flops 100000000 | bytes 2164736 | tf_op jit(solution)/shard_map/local_forward/pallas_call | solution.py:378
  28.6 2.0 %collective-permute-done = bf16[8,2,1,16,128]{4,3,2,1,0:T(8,128)(2,1)S(1)} collective-permute-done((bf16[8,2,1,16,128]{4,3,2,1,0:T(8,128)(2,1)S(1)}, bf16[8,2,1,16,128]{4,3,2,1,0:T(8,128)(2,1)S(1)}, u32[]{:S(2)}, u32[]{:S(2)}) %collective-permute-start) | collective-permute-done | bytes 65568 | tf_op jit(solution)/shard_map/ppermute | solution.py:392
  30.6 0.7 %crossing_forward.1 = (bf16[8,8,16,128]{3,2,1,0:T(8,128)(2,1)S(1)}, f32[8,8,16,128]{3,2,1,0:T(8,128)S(1)}, f32[8,32,128]{2,1,0:T(8,128)S(1)}) custom-call(s32[3,128]{1,0:T(4,128)S(1)} %broadcast_in_dim.11.offs_ref, f32[1,128]{1,0:T(1,128)S(1)} %dynamic-slice_bitcast_fusion.gain_ref, bf16[8,4,8,16,128]{4,3,2,1,0:T(8,128)(2,1)S(1)} %bitcast.11, ...), custom_call_target="tpu_custom_call" | custom-call | bytes 3147776 | tf_op jit(solution)/shard_map/crossing_forward/pallas_call | solution.py:378
  31.3 8.5 %all_to_all.15.stats_ref = f32[8,32,128]{2,1,0:T(8,128)S(1)} all-to-all(f32[8,32,128]{2,1,0:T(8,128)S(1)} %get-tuple-element.29), channel_id=1, replica_groups={{0,2,4,6,8,10,12,14},{16,18,20,22,24,26,28,30},{1,3,5,7,9,11,13,15},{17..., dimensions={0} | all-to-all | bytes 262144 | tf_op jit(solution)/shard_map/all_to_all | solution.py:421
  39.8 1.2 %norm_and_crossing.1 = (bf16[8,8,16,128]{3,2,1,0:T(8,128)(2,1)S(1)}, bf16[8,8,16,128]{3,2,1,0:T(8,128)(2,1)S(1)}, f32[8,8,16,128]{3,2,1,0:T(8,128)S(1)}, f32[1,1...) custom-call(s32[3,128]{1,0:T(4,128)S(1)} %broadcast_in_dim.11.offs_ref, ...), custom_call_target="tpu_custom_call" | custom-call | flops 10000000 | bytes 3344896 | tf_op jit(solution)/shard_map/norm_and_crossing/pallas_call | solution.py:378
  41.0 2.8 %collective-permute-start.3 = (bf16[8,2,1,16,128]{4,3,2,1,0:T(8,128)(2,1)S(1)}, bf16[8,2,1,16,128]{4,3,2,1,0:T(8,128)(2,1)S(1)}, u32[]{:S(2)}, u32[]{:S(2)}) collective-permute-start(bf16[8,2,1,16,128]{4,3,2,1,0:T(8,128)(2,1)S(1)} %bitcast.16), channel_id=1, source_target_pairs={{0,16},{2,18},{4,20},{6,22},{8,24},{10,26},{12,28},{14,30},{16,0},... | collective-permute-start | bytes 196616 | tf_op jit(solution)/shard_map/ppermute | solution.py:392
  43.9 0.0 collective-permute-start.1
  43.9 1.1 %collective-permute-done.1 = f32[1,128]{1,0:T(1,128)S(1)} collective-permute-done((f32[1,128]{1,0:T(1,128)S(1)}, f32[1,128]{1,0:T(1,128)S(1)}, u32[]{:S(2)}, u32[]{:S(2)}) %collective-permute-start.1) | collective-permute-done | bytes 544 | tf_op jit(solution)/shard_map/ppermute | solution.py:392
  45.0 0.1 collective-permute-start.2
  45.1 1.6 %local_backward.1 = (bf16[8,2,8,16,128]{4,3,2,1,0:T(8,128)(2,1)S(1)}, f32[2,8,8,16,128]{4,3,2,1,0:T(8,128)S(1)}) custom-call(s32[3,128]{1,0:T(4,128)S(1)} %broadcast_in_dim.11.offs_ref, bf16[8,4,8,16,128]{4,3,2,1,0:T(8,128)(2,1)S(1)} %bitcast.13, bf16[8,8,16,128]{3,2,1,0:T(8,128)(2,1)S(1)} %get-tuple-element.30.attended_ref, ...), custom_call_target="tpu_custom_call" | custom-call | flops 300000000 | bytes 4392448 | tf_op jit(solution)/shard_map/local_backward/pallas_call | solution.py:378
  46.7 2.7 %collective-permute-done.2 = f32[1,128]{1,0:T(1,128)S(1)} collective-permute-done((f32[1,128]{1,0:T(1,128)S(1)}, f32[1,128]{1,0:T(1,128)S(1)}, u32[]{:S(2)}, u32[]{:S(2)}) %collective-permute-start.2) | collective-permute-done | bytes 544 | tf_op jit(solution)/shard_map/ppermute | solution.py:392
  49.4 0.0 collective-permute-done.3.refs_0_
  49.4 0.2 pack.1
  49.6 17.6 %all_to_all.16.in_ref = bf16[8,528,128]{2,1,0:T(8,128)(2,1)S(1)} all-to-all(bf16[8,528,128]{2,1,0:T(8,128)(2,1)S(1)} %pack.1), channel_id=1, replica_groups={{0,2,4,6,8,10,12,14},{16,18,20,22,24,26,28,30},{1,3,5,7,9,11,13,15},{17..., dimensions={0} | all-to-all | bytes 2162688 | tf_op jit(solution)/shard_map/all_to_all | solution.py:421
  67.2 1.3 %join.1 = (bf16[1,128,1024]{2,1,0:T(8,128)(2,1)}, bf16[1,128,1024]{2,1,0:T(8,128)(2,1)}, bf16[1,128,1024]{2,1,0:T(8,128)(2,1)}, bf16[1,128,1024]{2,1,0:T(8,128)(2,1)}, f32[1,1024]{1,0:T(1,128)}) custom-call(bf16[8,528,128]{2,1,0:T(8,128)(2,1)S(1)} %all_to_all.16.in_ref), custom_call_target="tpu_custom_call" | custom-call | bytes 2134016 | tf_op jit(solution)/shard_map/join/pallas_call | solution.py:378
  (3 shorter events, 0.0 us)
Async XLA Ops:
  0.6 26.3 %copy-start = (f32[1024]{0:T(1024)S(1)}, f32[1024]{0:T(1024)}, u32[]{:S(2)}) copy-start(f32[1024]{0:T(1024)} %param.10) | copy-start | bytes 12292
  3.2 6.3 %copy-start.1 = (s32[3,8]{1,0:T(4,128)S(1)}, s32[3,8]{1,0:T(4,128)}, u32[]{:S(2)}) copy-start(s32[3,8]{1,0:T(4,128)} %param.11) | copy-start | bytes 292
  3.2 21.0 %all-to-all-start = ((bf16[8,4,128,128]{3,2,1,0:T(8,128)(2,1)}), bf16[8,4,128,128]{3,2,1,0:T(8,128)(2,1)S(1)}, u32[]{:S(2)}, u32[]{:S(2)}) async-start(bf16[8,4,128,128]{3,2,1,0:T(8,128)(2,1)} %split.1), calls=%async_computation | async-start | bytes 2097152 | tf_op jit(solution)/shard_map/all_to_all | solution.py:421
  24.2 6.4 %collective-permute-start = (bf16[8,2,1,16,128]{4,3,2,1,0:T(8,128)(2,1)S(1)}, bf16[8,2,1,16,128]{4,3,2,1,0:T(8,128)(2,1)S(1)}, u32[]{:S(2)}, u32[]{:S(2)}) collective-permute-start(bf16[8,2,1,16,128]{4,3,2,1,0:T(8,128)(2,1)S(1)} %constant_dynamic-slice_fusion), channel_id=1, source_target_pairs={{0,16},{2,18},{4,20},{6,22},{8,24},{10,26},{12,28},{14,30},{16,0},... | collective-permute-start | bytes 196616 | tf_op jit(solution)/shard_map/ppermute | solution.py:392
  41.0 8.4 %collective-permute-start.3 = (bf16[8,2,1,16,128]{4,3,2,1,0:T(8,128)(2,1)S(1)}, bf16[8,2,1,16,128]{4,3,2,1,0:T(8,128)(2,1)S(1)}, u32[]{:S(2)}, u32[]{:S(2)}) collective-permute-start(bf16[8,2,1,16,128]{4,3,2,1,0:T(8,128)(2,1)S(1)} %bitcast.16), channel_id=1, source_target_pairs={{0,16},{2,18},{4,20},{6,22},{8,24},{10,26},{12,28},{14,30},{16,0},... | collective-permute-start | bytes 196616 | tf_op jit(solution)/shard_map/ppermute | solution.py:392
  43.9 1.1 %collective-permute-start.1 = (f32[1,128]{1,0:T(1,128)S(1)}, f32[1,128]{1,0:T(1,128)S(1)}, u32[]{:S(2)}, u32[]{:S(2)}) collective-permute-start(f32[1,128]{1,0:T(1,128)S(1)} %get-tuple-element.36), channel_id=1, source_target_pairs={{0,1},{1,0},{2,3},{3,2},{4,5},{5,4},{6,7},{7,6},{8,9},{9,8},{10,11... | collective-permute-start | bytes 1544 | tf_op jit(solution)/shard_map/ppermute | solution.py:392
  45.0 4.4 %collective-permute-start.2 = (f32[1,128]{1,0:T(1,128)S(1)}, f32[1,128]{1,0:T(1,128)S(1)}, u32[]{:S(2)}, u32[]{:S(2)}) collective-permute-start(f32[1,128]{1,0:T(1,128)S(1)} %add.23), channel_id=1, source_target_pairs={{0,16},{2,18},{4,20},{6,22},{8,24},{10,26},{12,28},{14,30},{16,0},... | collective-permute-start | bytes 1544 | tf_op jit(solution)/shard_map/ppermute | solution.py:392

commit v3 on v2

--- a/solution.py
+++ b/solution.py
@@ -34,6 +34,16 @@
 def two_parts(value):
     high = value.astype(BF16)
     return jnp.concatenate([high, (value - high.astype(F32)).astype(BF16)], axis=1)
+
+
+def three_parts(row):
+    total = jnp.broadcast_to(row, (TILE, row.shape[1]))
+    high = total.astype(BF16).astype(F32)
+    middle = (total - high).astype(BF16).astype(F32)
+    low = total - high - middle
+    place = lax.broadcasted_iota(jnp.int32, total.shape, 0)
+    parts = jnp.where(place == 0, high, jnp.where(place == 1, middle, low))
+    return jnp.where(place < 3, parts, 0.0).astype(BF16)
 
 
 def row_order(tokens, rate, transposed):
@@ -277,17 +287,19 @@
     results = backward(blocks, grad_ref, lse_ref, delta_ref, scale, score_scale)
     for i, parts in enumerate(results):
         own = parts[0].shape[0]
-        others_count, pieces, _, steps, size, _ = sent_refs[i].shape
+        level, coded = levels[i], three_parts(gsum)
+        steps = level.count
         for t, part in enumerate(parts):
             own_refs[i][t] = part[:own]
             if t > 0:
                 low = own
-                for e in range(others_count):
+                for e in range(sent_refs[i].shape[0]):
                     for step in range(steps):
-                        for nb in range(pieces):
+                        for nb in range(level.pieces):
                             rows = part[low : low + size].astype(sent_refs[i].dtype)
-                            sent_refs[i][e, nb, t - 1, step] = rows
+                            sent_refs[i][e, (nb * 2 + t - 1) * steps + step] = rows
                             low += size
+                    sent_refs[i][e, 2 * steps * level.pieces] = coded.astype(sent_refs[i].dtype)
 
 
 def backward(blocks, grad_ref, lse_ref, delta_ref, scale, score_scale):
@@ -330,8 +342,8 @@
     out_ref[:, 1] = attended_ref[...]
 
 
-def pack_kernel(crossing, fold, offs_ref, main_ref, kv_in, gsum_ref, *refs):
-    arrived_refs, (out_ref, kv_ref) = refs[: len(crossing)], refs[len(crossing) :]
+def pack_kernel(crossing, fold, sums, offs_ref, main_ref, kv_in, *refs):
+    gsum_refs, arrived_refs, (out_ref, kv_ref) = refs[:sums], refs[sums:-2], refs[-2:]
     pieces, _, rate, size, hd = main_ref.shape
     rows = rate * size
     kv_ref[...] = kv_in[...]
@@ -339,13 +351,13 @@
         for i, b in enumerate(level.starts(offs_ref)):
             for nb in range(level.pieces):
                 for t in range(2):
-                    kv_ref[t, nb, b] += arrived_ref[nb, t, i].astype(F32)
-    total = jnp.broadcast_to(gsum_ref[...], (TILE, hd))
-    high = total.astype(BF16).astype(F32)
-    middle = (total - high).astype(BF16).astype(F32)
-    low = total - high - middle
-    row = lax.broadcasted_iota(jnp.int32, (TILE, hd), 0)
-    coded = jnp.where(row == 0, high, jnp.where(row == 1, middle, jnp.where(row == 2, low, 0.0)))
+                    block = (nb * 2 + t) * level.count + i
+                    kv_ref[t, nb, b] += arrived_ref[block].astype(F32)
+    total = functools.reduce(jnp.add, [ref[...] for ref in gsum_refs])
+    if sums > 1:
+        other = arrived_refs[0][arrived_refs[0].shape[0] - 1]
+        total = total + jnp.sum(other.astype(F32), axis=0, keepdims=True)
+    coded = three_parts(total)
     for nb in range(pieces):
         for t in range(2):
             out_ref[nb, t * rows : (t + 1) * rows] = main_ref[nb, t].reshape(rows, hd)
@@ -353,7 +365,7 @@
                 kv_ref[t, nb].reshape(rows, hd).astype(BF16)
             )
         for f in range(fold):
-            out_ref[nb, 4 * rows + f * TILE : 4 * rows + (f + 1) * TILE] = coded.astype(BF16)
+            out_ref[nb, 4 * rows + f * TILE : 4 * rows + (f + 1) * TILE] = coded
 
 
 def join_kernel(rate, factor, in_ref, dq_ref, attended_ref, dk_ref, dv_ref, gain_ref):
@@ -390,6 +402,14 @@
 def flip(value, axis, bit):
     pairs = [(source, source ^ (1 << bit)) for source in range(lax.axis_size(axis))]
     return lax.ppermute(value, axis, pairs)
+
+
+def cross(value):
+    ctx_count, dp_count = lax.axis_size("ctx"), lax.axis_size("dp")
+    count = ctx_count * dp_count
+    far = ctx_count // 2 * dp_count + dp_count // 2
+    pairs = [(source, source ^ far) for source in range(count)]
+    return lax.ppermute(value, ("ctx", "dp"), pairs)
 
 
 def shards(queries, key_rows, value_rows, out_grad, norm_gain, offsets):
@@ -468,7 +488,10 @@
     outs = [(state, BF16), (state, BF16), (state, F32), ((1, hd), F32)]
     outs += [((3, pieces * level.count * size, hd), F32) for level in crossing]
     sent_types = [BF16 if level.bits == 1 else F32 for level in crossing]
-    outs += [(other.shape, kind) for other, kind in zip(others, sent_types)]
+    outs += [
+        ((other.shape[0], 2 * level.pieces * level.count + 1, size, hd), kind)
+        for level, other, kind in zip(crossing, others, sent_types)
+    ]
     attended, grad, delta, gsum, *rest = call(
         functools.partial(norm_kernel, group, crossing, scale, score_scale),
         "norm_and_crossing",
@@ -489,9 +512,14 @@
                 for b, c in zip(partial[:half], came)
             ]
         arrived.append(partial[0])
-    for axis, count, first in (("dp", dp_count, 0), ("ctx", ctx_count, low_bit)):
-        for bit in range(first, count.bit_length() - 1):
-            gsum = gsum + flip(gsum, axis, bit)
+    alone = ctx_count == 2 * group and dp_count == 2 and size == TILE and len(crossing) == 1
+    gsums = [gsum]
+    if alone:
+        gsums += [flip(gsum, "dp", 0), cross(gsum)]
+    else:
+        for axis, count, first in (("dp", dp_count, 0), ("ctx", ctx_count, low_bit)):
+            for bit in range(first, count.bit_length() - 1):
+                gsums = [gsums[0] + flip(gsums[0], axis, bit)]
 
     main, kv = call(
         functools.partial(local_kernel, local, crossing, scale, score_scale),
@@ -502,9 +530,9 @@
         flops=3 * 10**8,
     )
     (packed,) = call(
-        functools.partial(pack_kernel, crossing, fold),
+        functools.partial(pack_kernel, crossing, fold, len(gsums)),
         "pack",
-        [offs_rows, main, kv, gsum] + arrived,
+        [offs_rows, main, kv] + gsums + arrived,
         [((pieces, 4 * rate * size + TILE * fold, hd), BF16)],
         scratch=[((2,) + state, F32)],
     )

time: 68.8 us -> 67.5 us (0.981)
  waiting for transfers between devices: 17.9 us -> 16.1 us
    ppermute x4 -> x3, waiting for transfers between devices: 5.88 us -> 2.03 us  [flip(): return lax.ppermute(value, axis, pairs)]
    ppermute x0 -> x1, waiting for transfers between devices: none -> 2.04 us  [cross(): return lax.ppermute(value, ('ctx', 'dp'), pairs)]
    ppermute x4 -> x3, starting transfers between devices: 5.64 us -> 5.75 us  [flip(): return lax.ppermute(value, axis, pairs)]
  transfers between devices with their start and end apart: 5 -> 5, of which waited for: 4 -> 3; matrix products, arithmetic and copies ran while one was open for 1% -> 1% of each run, Pallas kernels for 5% -> 5%
where the time goes in v3:
time: 67.5 us; the launch traced here: 67.2 us
  blocking collectives  26.5 us (39%)
  waiting for transfers between devices  16.1 us (24%)
  starting transfers between devices  12.1 us (18%)
  Pallas kernels  9.04 us (13%)
  between operations  2.64 us (4%)
  local copies, waits for them, and re-layouts  0.87 us (1%)
    all_to_all x2, blocking collectives, exchange(): lax.all_to_all(value, 'ctx', 0, 0, tiled=True, axis_index_groups=groups)  26.5 us
    all_to_all x1, waiting for transfers between devices, exchange(): lax.all_to_all(value, 'ctx', 0, 0, tiled=True, axis_index_groups=groups)  12 us
    pallas_call x7, Pallas kernels, call(): pl.pallas_call(body, name=name, in_specs=[VMEM] * len(inputs), out_specs=...  9.04 us
    all_to_all x1, starting transfers between devices, exchange(): lax.all_to_all(value, 'ctx', 0, 0, tiled=True, axis_index_groups=groups)  6.32 us
    ppermute x3, starting transfers between devices, flip(): return lax.ppermute(value, axis, pairs)  5.75 us
    ppermute x1, waiting for transfers between devices, cross(): return lax.ppermute(value, ('ctx', 'dp'), pairs)  2.04 us
    ppermute x3, waiting for transfers between devices, flip(): return lax.ppermute(value, axis, pairs)  2.03 us
  transfers between devices with their start and end apart: 5, of which 3 were waited for; matrix products, arithmetic and copies ran while one was open for 1% of the time, Pallas kernels for 5%

profile of v3, /device:TPU:0, one launch (start us, length us, event | category | flops | bytes accessed | tf_op | source)
XLA Modules:
  0.0 67.2 jit_solution(4693392761098725176)
XLA Ops:
  0.6 0.0 copy-start
  0.6 2.6 %split.1 = bf16[8,4,128,128]{3,2,1,0:T(8,128)(2,1)} custom-call(bf16[1,128,1024]{2,1,0:T(8,128)(2,1)} %q_ref.1, bf16[1,128,1024]{2,1,0:T(8,128)(2,1)} %k_ref.1, bf16[1,128,1024]{2,1,0:T(8,128)(2,1)} %v_ref.1, bf16[1,128,1024]{2,1,0:T(8,128)(2,1)} %g_ref.1), custom_call_target="tpu_custom_call" | custom-call | bytes 2097152 | tf_op jit(solution)/shard_map/split/pallas_call | solution.py:390
  3.2 0.0 copy-start.1
  3.2 6.3 %all-to-all-start = ((bf16[8,4,128,128]{3,2,1,0:T(8,128)(2,1)}), bf16[8,4,128,128]{3,2,1,0:T(8,128)(2,1)S(1)}, u32[]{:S(2)}, u32[]{:S(2)}) async-start(bf16[8,4,128,128]{3,2,1,0:T(8,128)(2,1)} %split.1), calls=%async_computation | async-start | bytes 2097152 | tf_op jit(solution)/shard_map/all_to_all | solution.py:441
  9.6 0.0 copy-done.1
  9.6 0.2 fusion
  9.7 0.5 slice.3
  12.2 12.0 %all-to-all-done = bf16[8,4,128,128]{3,2,1,0:T(8,128)(2,1)S(1)} async-done(((bf16[8,4,128,128]{3,2,1,0:T(8,128)(2,1)}), bf16[8,4,128,128]{3,2,1,0:T(8,128)(2,1)S(1)}, u32[]{:S(2)}, u32[]{:S(2)}) %all-to-all-start) | async-done | bytes 1048608 | tf_op jit(solution)/shard_map/all_to_all | solution.py:441
  24.2 2.7 %collective-permute-start = (bf16[8,2,1,16,128]{4,3,2,1,0:T(8,128)(2,1)S(1)}, bf16[8,2,1,16,128]{4,3,2,1,0:T(8,128)(2,1)S(1)}, u32[]{:S(2)}, u32[]{:S(2)}) collective-permute-start(bf16[8,2,1,16,128]{4,3,2,1,0:T(8,128)(2,1)S(1)} %constant_dynamic-slice_fusion), channel_id=1, source_target_pairs={{0,16},{2,18},{4,20},{6,22},{8,24},{10,26},{12,28},{14,30},{16,0},... | collective-permute-start | bytes 196616 | tf_op jit(solution)/shard_map/ppermute | solution.py:404
  26.9 0.0 copy-done
  26.9 0.1 dynamic-slice_bitcast_fusion.gain_ref
  27.0 0.1 broadcast_in_dim.11.offs_ref
  27.0 1.6 %local_forward.1 = (f32[8,8,16,128]{3,2,1,0:T(8,128)S(1)}, f32[8,8,16,128]{3,2,1,0:T(8,128)S(1)}, f32[128,128]{1,0:T(8,128)S(1)}) custom-call(s32[3,128]{1,0:T(4,128)S(1)} %broadcast_in_dim.11.offs_ref, f32[1,128]{1,0:T(1,128)S(1)} %dynamic-slice_bitcast_fusion.gain_ref, bf16[8,4,8,16,128]{4,3,2,1,0:T(8,128)(2,1)S(1)} %bitcast.10), custom_call_target="tpu_custom_call" | custom-call | flops 100000000 | bytes 2164736 | tf_op jit(solution)/shard_map/local_forward/pallas_call | solution.py:390
  28.6 2.0 %collective-permute-done = bf16[8,2,1,16,128]{4,3,2,1,0:T(8,128)(2,1)S(1)} collective-permute-done((bf16[8,2,1,16,128]{4,3,2,1,0:T(8,128)(2,1)S(1)}, bf16[8,2,1,16,128]{4,3,2,1,0:T(8,128)(2,1)S(1)}, u32[]{:S(2)}, u32[]{:S(2)}) %collective-permute-start) | collective-permute-done | bytes 65568 | tf_op jit(solution)/shard_map/ppermute | solution.py:404
  30.6 0.7 %crossing_forward.1 = (bf16[8,8,16,128]{3,2,1,0:T(8,128)(2,1)S(1)}, f32[8,8,16,128]{3,2,1,0:T(8,128)S(1)}, f32[8,32,128]{2,1,0:T(8,128)S(1)}) custom-call(s32[3,128]{1,0:T(4,128)S(1)} %broadcast_in_dim.11.offs_ref, f32[1,128]{1,0:T(1,128)S(1)} %dynamic-slice_bitcast_fusion.gain_ref, bf16[8,4,8,16,128]{4,3,2,1,0:T(8,128)(2,1)S(1)} %bitcast.11, ...), custom_call_target="tpu_custom_call" | custom-call | bytes 3147776 | tf_op jit(solution)/shard_map/crossing_forward/pallas_call | solution.py:390
  31.3 8.5 %all_to_all.15.stats_ref = f32[8,32,128]{2,1,0:T(8,128)S(1)} all-to-all(f32[8,32,128]{2,1,0:T(8,128)S(1)} %get-tuple-element.29), channel_id=1, replica_groups={{0,2,4,6,8,10,12,14},{16,18,20,22,24,26,28,30},{1,3,5,7,9,11,13,15},{17..., dimensions={0} | all-to-all | bytes 262144 | tf_op jit(solution)/shard_map/all_to_all | solution.py:441
  39.8 1.2 %norm_and_crossing.1 = (bf16[8,8,16,128]{3,2,1,0:T(8,128)(2,1)S(1)}, bf16[8,8,16,128]{3,2,1,0:T(8,128)(2,1)S(1)}, f32[8,8,16,128]{3,2,1,0:T(8,128)S(1)}, f32[1,1...) custom-call(s32[3,128]{1,0:T(4,128)S(1)} %broadcast_in_dim.11.offs_ref, ...), custom_call_target="tpu_custom_call" | custom-call | flops 10000000 | bytes 3348992 | tf_op jit(solution)/shard_map/norm_and_crossing/pallas_call | solution.py:390
  41.0 2.8 %collective-permute-start.3 = (bf16[17,16,128]{2,1,0:T(8,128)(2,1)S(1)}, bf16[17,16,128]{2,1,0:T(8,128)(2,1)S(1)}, u32[]{:S(2)}, u32[]{:S(2)}) collective-permute-start(bf16[17,16,128]{2,1,0:T(8,128)(2,1)S(1)} %bitcast.16), channel_id=1, source_target_pairs={{0,16},{2,18},{4,20},{6,22},{8,24},{10,26},{12,28},{14,30},{16,0},... | collective-permute-start | bytes 208904 | tf_op jit(solution)/shard_map/ppermute | solution.py:404
  43.8 0.0 collective-permute-start.2
  43.9 0.3 collective-permute-start.1
  44.1 1.5 %local_backward.1 = (bf16[8,2,8,16,128]{4,3,2,1,0:T(8,128)(2,1)S(1)}, f32[2,8,8,16,128]{4,3,2,1,0:T(8,128)S(1)}) custom-call(s32[3,128]{1,0:T(4,128)S(1)} %broadcast_in_dim.11.offs_ref, bf16[8,4,8,16,128]{4,3,2,1,0:T(8,128)(2,1)S(1)} %bitcast.13, bf16[8,8,16,128]{3,2,1,0:T(8,128)(2,1)S(1)} %get-tuple-element.30.attended_ref, ...), custom_call_target="tpu_custom_call" | custom-call | flops 300000000 | bytes 4392448 | tf_op jit(solution)/shard_map/local_backward/pallas_call | solution.py:390
  45.7 2.0 %collective-permute-done.2.refs_2_ = f32[1,128]{1,0:T(1,128)S(1)} collective-permute-done((f32[1,128]{1,0:T(1,128)S(1)}, f32[1,128]{1,0:T(1,128)S(1)}, u32[]{:S(2)}, u32[]{:S(2)}) %collective-permute-start.2) | collective-permute-done | bytes 544 | tf_op jit(solution)/shard_map/ppermute | solution.py:412
  47.7 0.0 collective-permute-done.1.refs_1_
  47.7 0.0 collective-permute-done.3.refs_3_
  47.7 0.2 pack.1
  47.9 18.0 %all_to_all.16.in_ref = bf16[8,528,128]{2,1,0:T(8,128)(2,1)S(1)} all-to-all(bf16[8,528,128]{2,1,0:T(8,128)(2,1)S(1)} %pack.1), channel_id=1, replica_groups={{0,2,4,6,8,10,12,14},{16,18,20,22,24,26,28,30},{1,3,5,7,9,11,13,15},{17..., dimensions={0} | all-to-all | bytes 2162688 | tf_op jit(solution)/shard_map/all_to_all | solution.py:441
  65.9 1.3 %join.1 = (bf16[1,128,1024]{2,1,0:T(8,128)(2,1)}, bf16[1,128,1024]{2,1,0:T(8,128)(2,1)}, bf16[1,128,1024]{2,1,0:T(8,128)(2,1)}, bf16[1,128,1024]{2,1,0:T(8,128)(2,1)}, f32[1,1024]{1,0:T(1,128)}) custom-call(bf16[8,528,128]{2,1,0:T(8,128)(2,1)S(1)} %all_to_all.16.in_ref), custom_call_target="tpu_custom_call" | custom-call | bytes 2134016 | tf_op jit(solution)/shard_map/join/pallas_call | solution.py:390
  (1 shorter events, 0.0 us)
Async XLA Ops:
  0.6 26.3 %copy-start = (f32[1024]{0:T(1024)S(1)}, f32[1024]{0:T(1024)}, u32[]{:S(2)}) copy-start(f32[1024]{0:T(1024)} %param.10) | copy-start | bytes 12292
  3.2 6.3 %copy-start.1 = (s32[3,8]{1,0:T(4,128)S(1)}, s32[3,8]{1,0:T(4,128)}, u32[]{:S(2)}) copy-start(s32[3,8]{1,0:T(4,128)} %param.11) | copy-start | bytes 292
  3.2 21.0 %all-to-all-start = ((bf16[8,4,128,128]{3,2,1,0:T(8,128)(2,1)}), bf16[8,4,128,128]{3,2,1,0:T(8,128)(2,1)S(1)}, u32[]{:S(2)}, u32[]{:S(2)}) async-start(bf16[8,4,128,128]{3,2,1,0:T(8,128)(2,1)} %split.1), calls=%async_computation | async-start | bytes 2097152 | tf_op jit(solution)/shard_map/all_to_all | solution.py:441
  24.2 6.4 %collective-permute-start = (bf16[8,2,1,16,128]{4,3,2,1,0:T(8,128)(2,1)S(1)}, bf16[8,2,1,16,128]{4,3,2,1,0:T(8,128)(2,1)S(1)}, u32[]{:S(2)}, u32[]{:S(2)}) collective-permute-start(bf16[8,2,1,16,128]{4,3,2,1,0:T(8,128)(2,1)S(1)} %constant_dynamic-slice_fusion), channel_id=1, source_target_pairs={{0,16},{2,18},{4,20},{6,22},{8,24},{10,26},{12,28},{14,30},{16,0},... | collective-permute-start | bytes 196616 | tf_op jit(solution)/shard_map/ppermute | solution.py:404
  41.0 6.7 %collective-permute-start.3 = (bf16[17,16,128]{2,1,0:T(8,128)(2,1)S(1)}, bf16[17,16,128]{2,1,0:T(8,128)(2,1)S(1)}, u32[]{:S(2)}, u32[]{:S(2)}) collective-permute-start(bf16[17,16,128]{2,1,0:T(8,128)(2,1)S(1)} %bitcast.16), channel_id=1, source_target_pairs={{0,16},{2,18},{4,20},{6,22},{8,24},{10,26},{12,28},{14,30},{16,0},... | collective-permute-start | bytes 208904 | tf_op jit(solution)/shard_map/ppermute | solution.py:404
  43.8 3.9 %collective-permute-start.2 = (f32[1,128]{1,0:T(1,128)S(1)}, f32[1,128]{1,0:T(1,128)S(1)}, u32[]{:S(2)}, u32[]{:S(2)}) collective-permute-start(f32[1,128]{1,0:T(1,128)S(1)} %get-tuple-element.36.refs_0_), channel_id=1, source_target_pairs={{0,17},{1,16},{2,19},{3,18},{4,21},{5,20},{6,23},{7,22},{8,25},{9,... | collective-permute-start | bytes 1544 | tf_op jit(solution)/shard_map/ppermute | solution.py:412
  43.9 3.9 %collective-permute-start.1 = (f32[1,128]{1,0:T(1,128)S(1)}, f32[1,128]{1,0:T(1,128)S(1)}, u32[]{:S(2)}, u32[]{:S(2)}) collective-permute-start(f32[1,128]{1,0:T(1,128)S(1)} %get-tuple-element.36.refs_0_), channel_id=1, source_target_pairs={{0,1},{1,0},{2,3},{3,2},{4,5},{5,4},{6,7},{7,6},{8,9},{9,8},{10,11... | collective-permute-start | bytes 1544 | tf_op jit(solution)/shard_map/ppermute | solution.py:404

commit v4 on v3

--- a/solution.py
+++ b/solution.py
@@ -19,6 +19,7 @@
 LOG2E = math.log2(math.e)
 TILE = 16
 STAGED = 4
+ORDER = (0, 7, 2, 6, 1, 5, 4, 3)
 F32 = jnp.float32
 BF16 = jnp.bfloat16
 
@@ -63,7 +64,8 @@
 
 
 class Level:
-    def __init__(self, index, span, rate, top_rate, fold, group):
+    def __init__(self, index, span, rate, top_rate, fold, order):
+        group = len(order)
         self.index = index
         self.rate = rate
         self.count = top_rate // rate
@@ -71,6 +73,7 @@
         self.bits = span.bit_length() - group.bit_length()
         self.pieces = min(span, group) // fold
         self.segments = 1 if self.crossing else group // span
+        self.spots = [order.index(device) // fold for device in range(0, group, fold)]
 
     def starts(self, offs):
         first = 0 if self.index == 0 else offs[self.index - 1, 0]
@@ -78,7 +81,8 @@
 
     def places(self, offs_ref, segment):
         low = segment * self.pieces
-        return [(nb, b) for b in self.starts(offs_ref) for nb in range(low, low + self.pieces)]
+        spots = self.spots[low : low + self.pieces]
+        return [(nb, b) for b in self.starts(offs_ref) for nb in spots]
 
 
 def gather(read, places):
@@ -431,16 +435,18 @@
     fold = max(1, TILE // short)
     size = short * fold
     pieces = group // fold
-    levels = [Level(i, span, r, rate, fold, group) for i, (span, r) in enumerate(spans)]
+    order = list(ORDER) if group == len(ORDER) and fold == 1 else list(range(group))
+    levels = [Level(i, span, r, rate, fold, order) for i, (span, r) in enumerate(spans)]
     local = [level for level in levels if not level.crossing]
     crossing = [level for level in levels if level.crossing]
-    groups = [list(range(low, low + group)) for low in range(0, ctx_count, group)]
+    groups = [[low + device for device in order] for low in range(0, ctx_count, group)]
     low_bit = group.bit_length() - 1
 
     def exchange(value):
         return lax.all_to_all(value, "ctx", 0, 0, tiled=True, axis_index_groups=groups)
 
-    head = lax.axis_index("ctx") % group
+    place = lax.axis_index("ctx") % group
+    head = sum(order.index(device) * (place == device) for device in range(group))
     offs = lax.dynamic_slice(offsets, (0, head), (offsets.shape[0], 1))
     offs_rows = jnp.broadcast_to(offs, (offsets.shape[0], hd))
     gain = lax.dynamic_slice(norm_gain, (head * hd,), (hd,))[None]

time: 67.5 us -> 66.8 us (0.990)
  waiting for transfers between devices: 16.1 us -> 14.7 us
  blocking collectives: 26.5 us -> 27.2 us
    all_to_all x1, waiting for transfers between devices: 12 us -> 10.9 us  [exchange(): lax.all_to_all(value, 'ctx', 0, 0, tiled=True, axis_index_groups=groups)]
    all_to_all x2, blocking collectives: 26.5 us -> 27.2 us  [exchange(): lax.all_to_all(value, 'ctx', 0, 0, tiled=True, axis_index_groups=groups)]
where the time goes in v4:
time: 66.8 us; the launch traced here: 66.4 us
  blocking collectives  27.2 us (41%)
  waiting for transfers between devices  14.7 us (22%)
  starting transfers between devices  12.1 us (18%)
  Pallas kernels  9.03 us (14%)
  between operations  2.63 us (4%)
  local copies, waits for them, and re-layouts  0.87 us (1%)
    all_to_all x2, blocking collectives, exchange(): lax.all_to_all(value, 'ctx', 0, 0, tiled=True, axis_index_groups=groups)  27.2 us
    all_to_all x1, waiting for transfers between devices, exchange(): lax.all_to_all(value, 'ctx', 0, 0, tiled=True, axis_index_groups=groups)  10.9 us
    pallas_call x7, Pallas kernels, call(): pl.pallas_call(body, name=name, in_specs=[VMEM] * len(inputs), out_specs=...  9.03 us
    all_to_all x1, starting transfers between devices, exchange(): lax.all_to_all(value, 'ctx', 0, 0, tiled=True, axis_index_groups=groups)  6.32 us
    ppermute x3, starting transfers between devices, flip(): return lax.ppermute(value, axis, pairs)  5.79 us
    ppermute x1, waiting for transfers between devices, cross(): return lax.ppermute(value, ('ctx', 'dp'), pairs)  2.12 us
    ppermute x3, waiting for transfers between devices, flip(): return lax.ppermute(value, axis, pairs)  1.59 us
  transfers between devices with their start and end apart: 5, of which 3 were waited for; matrix products, arithmetic and copies ran while one was open for 1% of the time, Pallas kernels for 5%

profile of v4, /device:TPU:0, one launch (start us, length us, event | category | flops | bytes accessed | tf_op | source)
XLA Modules:
  0.0 66.4 jit_solution(10583029278248524741)
XLA Ops:
  0.6 0.0 copy-start
  0.6 2.6 %split.1 = bf16[8,4,128,128]{3,2,1,0:T(8,128)(2,1)} custom-call(bf16[1,128,1024]{2,1,0:T(8,128)(2,1)} %q_ref.1, bf16[1,128,1024]{2,1,0:T(8,128)(2,1)} %k_ref.1, bf16[1,128,1024]{2,1,0:T(8,128)(2,1)} %v_ref.1, bf16[1,128,1024]{2,1,0:T(8,128)(2,1)} %g_ref.1), custom_call_target="tpu_custom_call" | custom-call | bytes 2097152 | tf_op jit(solution)/shard_map/split/pallas_call | solution.py:394
  3.2 0.0 copy-start.1
  3.2 6.3 %all-to-all-start = ((bf16[8,4,128,128]{3,2,1,0:T(8,128)(2,1)}), bf16[8,4,128,128]{3,2,1,0:T(8,128)(2,1)S(1)}, u32[]{:S(2)}, u32[]{:S(2)}) async-start(bf16[8,4,128,128]{3,2,1,0:T(8,128)(2,1)} %split.1), calls=%async_computation | async-start | bytes 2097152 | tf_op jit(solution)/shard_map/all_to_all | solution.py:446
  9.6 0.0 copy-done.1
  9.6 0.2 fusion
  9.7 0.5 slice.3
  12.2 10.9 %all-to-all-done = bf16[8,4,128,128]{3,2,1,0:T(8,128)(2,1)S(1)} async-done(((bf16[8,4,128,128]{3,2,1,0:T(8,128)(2,1)}), bf16[8,4,128,128]{3,2,1,0:T(8,128)(2,1)S(1)}, u32[]{:S(2)}, u32[]{:S(2)}) %all-to-all-start) | async-done | bytes 1048608 | tf_op jit(solution)/shard_map/all_to_all | solution.py:446
  23.2 2.7 %collective-permute-start = (bf16[8,2,1,16,128]{4,3,2,1,0:T(8,128)(2,1)S(1)}, bf16[8,2,1,16,128]{4,3,2,1,0:T(8,128)(2,1)S(1)}, u32[]{:S(2)}, u32[]{:S(2)}) collective-permute-start(bf16[8,2,1,16,128]{4,3,2,1,0:T(8,128)(2,1)S(1)} %constant_dynamic-slice_fusion), channel_id=1, source_target_pairs={{0,16},{2,18},{4,20},{6,22},{8,24},{10,26},{12,28},{14,30},{16,0},... | collective-permute-start | bytes 196616 | tf_op jit(solution)/shard_map/ppermute | solution.py:408
  25.8 0.0 copy-done
  25.8 0.1 dynamic-slice_bitcast_fusion.gain_ref
  25.9 0.1 broadcast_in_dim.11.offs_ref
  26.0 1.5 %local_forward.1 = (f32[8,8,16,128]{3,2,1,0:T(8,128)S(1)}, f32[8,8,16,128]{3,2,1,0:T(8,128)S(1)}, f32[128,128]{1,0:T(8,128)S(1)}) custom-call(s32[3,128]{1,0:T(4,128)S(1)} %broadcast_in_dim.11.offs_ref, f32[1,128]{1,0:T(1,128)S(1)} %dynamic-slice_bitcast_fusion.gain_ref, bf16[8,4,8,16,128]{4,3,2,1,0:T(8,128)(2,1)S(1)} %bitcast.10), custom_call_target="tpu_custom_call" | custom-call | flops 100000000 | bytes 2164736 | tf_op jit(solution)/shard_map/local_forward/pallas_call | solution.py:394
  27.5 1.6 %collective-permute-done = bf16[8,2,1,16,128]{4,3,2,1,0:T(8,128)(2,1)S(1)} collective-permute-done((bf16[8,2,1,16,128]{4,3,2,1,0:T(8,128)(2,1)S(1)}, bf16[8,2,1,16,128]{4,3,2,1,0:T(8,128)(2,1)S(1)}, u32[]{:S(2)}, u32[]{:S(2)}) %collective-permute-start) | collective-permute-done | bytes 65568 | tf_op jit(solution)/shard_map/ppermute | solution.py:408
  29.1 0.7 %crossing_forward.1 = (bf16[8,8,16,128]{3,2,1,0:T(8,128)(2,1)S(1)}, f32[8,8,16,128]{3,2,1,0:T(8,128)S(1)}, f32[8,32,128]{2,1,0:T(8,128)S(1)}) custom-call(s32[3,128]{1,0:T(4,128)S(1)} %broadcast_in_dim.11.offs_ref, f32[1,128]{1,0:T(1,128)S(1)} %dynamic-slice_bitcast_fusion.gain_ref, bf16[8,4,8,16,128]{4,3,2,1,0:T(8,128)(2,1)S(1)} %bitcast.11, ...), custom_call_target="tpu_custom_call" | custom-call | bytes 3147776 | tf_op jit(solution)/shard_map/crossing_forward/pallas_call | solution.py:394
  29.8 9.4 %all_to_all.15.stats_ref = f32[8,32,128]{2,1,0:T(8,128)S(1)} all-to-all(f32[8,32,128]{2,1,0:T(8,128)S(1)} %get-tuple-element.29), channel_id=1, replica_groups={{0,14,4,12,2,10,8,6},{16,30,20,28,18,26,24,22},{1,15,5,13,3,11,9,7},{17..., dimensions={0} | all-to-all | bytes 262144 | tf_op jit(solution)/shard_map/all_to_all | solution.py:446
  39.2 1.2 %norm_and_crossing.1 = (bf16[8,8,16,128]{3,2,1,0:T(8,128)(2,1)S(1)}, bf16[8,8,16,128]{3,2,1,0:T(8,128)(2,1)S(1)}, f32[8,8,16,128]{3,2,1,0:T(8,128)S(1)}, f32[1,1...) custom-call(s32[3,128]{1,0:T(4,128)S(1)} %broadcast_in_dim.11.offs_ref, ...), custom_call_target="tpu_custom_call" | custom-call | flops 10000000 | bytes 3348992 | tf_op jit(solution)/shard_map/norm_and_crossing/pallas_call | solution.py:394
  40.4 3.0 %collective-permute-start.3 = (bf16[17,16,128]{2,1,0:T(8,128)(2,1)S(1)}, bf16[17,16,128]{2,1,0:T(8,128)(2,1)S(1)}, u32[]{:S(2)}, u32[]{:S(2)}) collective-permute-start(bf16[17,16,128]{2,1,0:T(8,128)(2,1)S(1)} %bitcast.16), channel_id=1, source_target_pairs={{0,16},{2,18},{4,20},{6,22},{8,24},{10,26},{12,28},{14,30},{16,0},... | collective-permute-start | bytes 208904 | tf_op jit(solution)/shard_map/ppermute | solution.py:408
  43.3 0.0 collective-permute-start.2
  43.4 0.2 collective-permute-start.1
  43.5 1.5 %local_backward.1 = (bf16[8,2,8,16,128]{4,3,2,1,0:T(8,128)(2,1)S(1)}, f32[2,8,8,16,128]{4,3,2,1,0:T(8,128)S(1)}) custom-call(s32[3,128]{1,0:T(4,128)S(1)} %broadcast_in_dim.11.offs_ref, bf16[8,4,8,16,128]{4,3,2,1,0:T(8,128)(2,1)S(1)} %bitcast.13, bf16[8,8,16,128]{3,2,1,0:T(8,128)(2,1)S(1)} %get-tuple-element.30.attended_ref, ...), custom_call_target="tpu_custom_call" | custom-call | flops 300000000 | bytes 4392448 | tf_op jit(solution)/shard_map/local_backward/pallas_call | solution.py:394
  45.1 2.1 %collective-permute-done.2.refs_2_ = f32[1,128]{1,0:T(1,128)S(1)} collective-permute-done((f32[1,128]{1,0:T(1,128)S(1)}, f32[1,128]{1,0:T(1,128)S(1)}, u32[]{:S(2)}, u32[]{:S(2)}) %collective-permute-start.2) | collective-permute-done | bytes 544 | tf_op jit(solution)/shard_map/ppermute | solution.py:416
  47.2 0.0 collective-permute-done.1.refs_1_
  47.2 0.0 collective-permute-done.3.refs_3_
  47.2 0.2 pack.1
  47.4 17.7 %all_to_all.16.in_ref = bf16[8,528,128]{2,1,0:T(8,128)(2,1)S(1)} all-to-all(bf16[8,528,128]{2,1,0:T(8,128)(2,1)S(1)} %pack.1), channel_id=1, replica_groups={{0,14,4,12,2,10,8,6},{16,30,20,28,18,26,24,22},{1,15,5,13,3,11,9,7},{17..., dimensions={0} | all-to-all | bytes 2162688 | tf_op jit(solution)/shard_map/all_to_all | solution.py:446
  65.1 1.3 %join.1 = (bf16[1,128,1024]{2,1,0:T(8,128)(2,1)}, bf16[1,128,1024]{2,1,0:T(8,128)(2,1)}, bf16[1,128,1024]{2,1,0:T(8,128)(2,1)}, bf16[1,128,1024]{2,1,0:T(8,128)(2,1)}, f32[1,1024]{1,0:T(1,128)}) custom-call(bf16[8,528,128]{2,1,0:T(8,128)(2,1)S(1)} %all_to_all.16.in_ref), custom_call_target="tpu_custom_call" | custom-call | bytes 2134016 | tf_op jit(solution)/shard_map/join/pallas_call | solution.py:394
  (1 shorter events, 0.0 us)
Async XLA Ops:
  0.6 25.2 %copy-start = (f32[1024]{0:T(1024)S(1)}, f32[1024]{0:T(1024)}, u32[]{:S(2)}) copy-start(f32[1024]{0:T(1024)} %param.10) | copy-start | bytes 12292
  3.2 6.3 %copy-start.1 = (s32[3,8]{1,0:T(4,128)S(1)}, s32[3,8]{1,0:T(4,128)}, u32[]{:S(2)}) copy-start(s32[3,8]{1,0:T(4,128)} %param.11) | copy-start | bytes 292
  3.2 19.9 %all-to-all-start = ((bf16[8,4,128,128]{3,2,1,0:T(8,128)(2,1)}), bf16[8,4,128,128]{3,2,1,0:T(8,128)(2,1)S(1)}, u32[]{:S(2)}, u32[]{:S(2)}) async-start(bf16[8,4,128,128]{3,2,1,0:T(8,128)(2,1)} %split.1), calls=%async_computation | async-start | bytes 2097152 | tf_op jit(solution)/shard_map/all_to_all | solution.py:446
  23.2 5.9 %collective-permute-start = (bf16[8,2,1,16,128]{4,3,2,1,0:T(8,128)(2,1)S(1)}, bf16[8,2,1,16,128]{4,3,2,1,0:T(8,128)(2,1)S(1)}, u32[]{:S(2)}, u32[]{:S(2)}) collective-permute-start(bf16[8,2,1,16,128]{4,3,2,1,0:T(8,128)(2,1)S(1)} %constant_dynamic-slice_fusion), channel_id=1, source_target_pairs={{0,16},{2,18},{4,20},{6,22},{8,24},{10,26},{12,28},{14,30},{16,0},... | collective-permute-start | bytes 196616 | tf_op jit(solution)/shard_map/ppermute | solution.py:408
  40.4 6.8 %collective-permute-start.3 = (bf16[17,16,128]{2,1,0:T(8,128)(2,1)S(1)}, bf16[17,16,128]{2,1,0:T(8,128)(2,1)S(1)}, u32[]{:S(2)}, u32[]{:S(2)}) collective-permute-start(bf16[17,16,128]{2,1,0:T(8,128)(2,1)S(1)} %bitcast.16), channel_id=1, source_target_pairs={{0,16},{2,18},{4,20},{6,22},{8,24},{10,26},{12,28},{14,30},{16,0},... | collective-permute-start | bytes 208904 | tf_op jit(solution)/shard_map/ppermute | solution.py:408
  43.3 3.9 %collective-permute-start.2 = (f32[1,128]{1,0:T(1,128)S(1)}, f32[1,128]{1,0:T(1,128)S(1)}, u32[]{:S(2)}, u32[]{:S(2)}) collective-permute-start(f32[1,128]{1,0:T(1,128)S(1)} %get-tuple-element.36.refs_0_), channel_id=1, source_target_pairs={{0,17},{1,16},{2,19},{3,18},{4,21},{5,20},{6,23},{7,22},{8,25},{9,... | collective-permute-start | bytes 1544 | tf_op jit(solution)/shard_map/ppermute | solution.py:416
  43.4 3.9 %collective-permute-start.1 = (f32[1,128]{1,0:T(1,128)S(1)}, f32[1,128]{1,0:T(1,128)S(1)}, u32[]{:S(2)}, u32[]{:S(2)}) collective-permute-start(f32[1,128]{1,0:T(1,128)S(1)} %get-tuple-element.36.refs_0_), channel_id=1, source_target_pairs={{0,1},{1,0},{2,3},{3,2},{4,5},{5,4},{6,7},{7,6},{8,9},{9,8},{10,11... | collective-permute-start | bytes 1544 | tf_op jit(solution)/shard_map/ppermute | solution.py:408

commit v5 on v4

--- a/solution.py
+++ b/solution.py
@@ -346,8 +346,8 @@
     out_ref[:, 1] = attended_ref[...]
 
 
-def pack_kernel(crossing, fold, sums, offs_ref, main_ref, kv_in, *refs):
-    gsum_refs, arrived_refs, (out_ref, kv_ref) = refs[:sums], refs[sums:-2], refs[-2:]
+def pack_kernel(crossing, fold, alone, offs_ref, main_ref, kv_in, gsum_ref, *refs):
+    arrived_refs, (out_ref, kv_ref) = refs[:-2], refs[-2:]
     pieces, _, rate, size, hd = main_ref.shape
     rows = rate * size
     kv_ref[...] = kv_in[...]
@@ -357,8 +357,8 @@
                 for t in range(2):
                     block = (nb * 2 + t) * level.count + i
                     kv_ref[t, nb, b] += arrived_ref[block].astype(F32)
-    total = functools.reduce(jnp.add, [ref[...] for ref in gsum_refs])
-    if sums > 1:
+    total = gsum_ref[...]
+    if alone:
         other = arrived_refs[0][arrived_refs[0].shape[0] - 1]
         total = total + jnp.sum(other.astype(F32), axis=0, keepdims=True)
     coded = three_parts(total)
@@ -372,7 +372,7 @@
             out_ref[nb, 4 * rows + f * TILE : 4 * rows + (f + 1) * TILE] = coded
 
 
-def join_kernel(rate, factor, in_ref, dq_ref, attended_ref, dk_ref, dv_ref, gain_ref):
+def join_kernel(rate, in_ref, dq_ref, attended_ref, dk_ref, dv_ref):
     group, _, hd = in_ref.shape
     tokens = dq_ref.shape[1]
     order = row_order(tokens, rate, True)
@@ -380,9 +380,6 @@
         for h in range(group):
             moved = dot(order, in_ref[h, t * tokens : (t + 1) * tokens, :], NN)
             ref[0, :, h * hd : (h + 1) * hd] = moved.astype(BF16)
-    for h in range(group):
-        coded = in_ref[h, 4 * tokens : 4 * tokens + TILE, :].astype(F32)
-        gain_ref[:, h * hd : (h + 1) * hd] = jnp.sum(coded, axis=0, keepdims=True) * factor
 
 
 VMEM = pl.BlockSpec(memory_space=pltpu.VMEM)
@@ -406,14 +403,6 @@
 def flip(value, axis, bit):
     pairs = [(source, source ^ (1 << bit)) for source in range(lax.axis_size(axis))]
     return lax.ppermute(value, axis, pairs)
-
-
-def cross(value):
-    ctx_count, dp_count = lax.axis_size("ctx"), lax.axis_size("dp")
-    count = ctx_count * dp_count
-    far = ctx_count // 2 * dp_count + dp_count // 2
-    pairs = [(source, source ^ far) for source in range(count)]
-    return lax.ppermute(value, ("ctx", "dp"), pairs)
 
 
 def shards(queries, key_rows, value_rows, out_grad, norm_gain, offsets):
@@ -519,13 +508,10 @@
             ]
         arrived.append(partial[0])
     alone = ctx_count == 2 * group and dp_count == 2 and size == TILE and len(crossing) == 1
-    gsums = [gsum]
-    if alone:
-        gsums += [flip(gsum, "dp", 0), cross(gsum)]
-    else:
+    if not alone:
         for axis, count, first in (("dp", dp_count, 0), ("ctx", ctx_count, low_bit)):
             for bit in range(first, count.bit_length() - 1):
-                gsums = [gsums[0] + flip(gsums[0], axis, bit)]
+                gsum = gsum + flip(gsum, axis, bit)
 
     main, kv = call(
         functools.partial(local_kernel, local, crossing, scale, score_scale),
@@ -536,9 +522,9 @@
         flops=3 * 10**8,
     )
     (packed,) = call(
-        functools.partial(pack_kernel, crossing, fold, len(gsums)),
+        functools.partial(pack_kernel, crossing, fold, alone),
         "pack",
-        [offs_rows, main, kv] + gsums + arrived,
+        [offs_rows, main, kv, gsum] + arrived,
         [((pieces, 4 * rate * size + TILE * fold, hd), BF16)],
         scratch=[((2,) + state, F32)],
     )
@@ -547,15 +533,19 @@
         rows = rows.transpose(0, 3, 1, 2, 4, 5).reshape(group, 4 * tokens, hd)
         packed = jnp.concatenate([rows, packed[:, 4 * rate * size :].reshape(group, TILE, hd)], 1)
     back = exchange(packed)
-    factor = 1.0 / math.sqrt(ctx_count * dp_count * tokens)
+    gains = jnp.sum(back[:, 4 * tokens :].astype(F32), axis=1)
+    if alone:
+        gains = gains + flip(gains, "dp", 0)
+    gain_grad = gains.reshape(width) / math.sqrt(ctx_count * dp_count * tokens)
     row = ((1, tokens, width), BF16)
-    dq, attended, dk, dv, gain_grad = call(
-        functools.partial(join_kernel, rate, factor),
+    dq, attended, dk, dv = call(
+        functools.partial(join_kernel, rate),
         "join",
         [back],
-        [row, row, row, row, ((1, width), F32)],
-    )
-    return attended, dq, dk, dv, gain_grad[0]
+        [row, row, row, row],
+        flops=10**8,
+    )
+    return attended, dq, dk, dv, gain_grad
 
 
 def solution(mesh):

time: 66.8 us -> 64.7 us (0.969)
  blocking collectives: 27.2 us -> 25.3 us
  waiting for transfers between devices: 14.7 us -> 14 us
    ppermute x1 -> x0, waiting for transfers between devices: 2.12 us -> none  [cross(): return lax.ppermute(value, ('ctx', 'dp'), pairs)]
    all_to_all x2, blocking collectives: 27.2 us -> 25.3 us  [exchange(): lax.all_to_all(value, 'ctx', 0, 0, tiled=True, axis_index_groups=groups)]
    ppermute x3, waiting for transfers between devices: 1.59 us -> 3.08 us  [flip(): return lax.ppermute(value, axis, pairs)]
  transfers between devices with their start and end apart: 5 -> 4, of which waited for: 3 -> 3; matrix products, arithmetic and copies ran while one was open for 1% -> 1% of each run, Pallas kernels for 5% -> 7%
where the time goes in v5:
time: 64.7 us; the launch traced here: 64.3 us
  blocking collectives  25.3 us (39%)
  waiting for transfers between devices  14 us (22%)
  starting transfers between devices  12 us (19%)
  Pallas kernels  8.93 us (14%)
  between operations  2.64 us (4%)
  local copies, waits for them, and re-layouts  0.87 us (1%)
    all_to_all x2, blocking collectives, exchange(): lax.all_to_all(value, 'ctx', 0, 0, tiled=True, axis_index_groups=groups)  25.3 us
    all_to_all x1, waiting for transfers between devices, exchange(): lax.all_to_all(value, 'ctx', 0, 0, tiled=True, axis_index_groups=groups)  10.9 us
    pallas_call x7, Pallas kernels, call(): pl.pallas_call(body, name=name, in_specs=[VMEM] * len(inputs), out_specs=...  8.93 us
    all_to_all x1, starting transfers between devices, exchange(): lax.all_to_all(value, 'ctx', 0, 0, tiled=True, axis_index_groups=groups)  6.32 us
    ppermute x3, starting transfers between devices, flip(): return lax.ppermute(value, axis, pairs)  5.68 us
    ppermute x3, waiting for transfers between devices, flip(): return lax.ppermute(value, axis, pairs)  3.08 us
  transfers between devices with their start and end apart: 4, of which 3 were waited for; matrix products, arithmetic and copies ran while one was open for 1% of the time, Pallas kernels for 7%

profile of v5, /device:TPU:0, one launch (start us, length us, event | category | flops | bytes accessed | tf_op | source)
XLA Modules:
  0.0 64.3 jit_solution(14607401406262583110)
XLA Ops:
  0.6 0.0 copy-start
  0.6 2.6 %split.1 = bf16[8,4,128,128]{3,2,1,0:T(8,128)(2,1)} custom-call(bf16[1,128,1024]{2,1,0:T(8,128)(2,1)} %q_ref.1, bf16[1,128,1024]{2,1,0:T(8,128)(2,1)} %k_ref.1, bf16[1,128,1024]{2,1,0:T(8,128)(2,1)} %v_ref.1, bf16[1,128,1024]{2,1,0:T(8,128)(2,1)} %g_ref.1), custom_call_target="tpu_custom_call" | custom-call | bytes 2097152 | tf_op jit(solution)/shard_map/split/pallas_call | solution.py:391
  3.2 0.0 copy-start.1
  3.2 6.3 %all-to-all-start = ((bf16[8,4,128,128]{3,2,1,0:T(8,128)(2,1)}), bf16[8,4,128,128]{3,2,1,0:T(8,128)(2,1)S(1)}, u32[]{:S(2)}, u32[]{:S(2)}) async-start(bf16[8,4,128,128]{3,2,1,0:T(8,128)(2,1)} %split.1), calls=%async_computation | async-start | bytes 2097152 | tf_op jit(solution)/shard_map/all_to_all | solution.py:435
  9.5 0.0 copy-done.1
  9.6 0.2 fusion
  9.7 0.5 slice.6
  12.2 10.9 %all-to-all-done = bf16[8,4,128,128]{3,2,1,0:T(8,128)(2,1)S(1)} async-done(((bf16[8,4,128,128]{3,2,1,0:T(8,128)(2,1)}), bf16[8,4,128,128]{3,2,1,0:T(8,128)(2,1)S(1)}, u32[]{:S(2)}, u32[]{:S(2)}) %all-to-all-start) | async-done | bytes 1048608 | tf_op jit(solution)/shard_map/all_to_all | solution.py:435
  23.2 2.7 %collective-permute-start = (bf16[8,2,1,16,128]{4,3,2,1,0:T(8,128)(2,1)S(1)}, bf16[8,2,1,16,128]{4,3,2,1,0:T(8,128)(2,1)S(1)}, u32[]{:S(2)}, u32[]{:S(2)}) collective-permute-start(bf16[8,2,1,16,128]{4,3,2,1,0:T(8,128)(2,1)S(1)} %constant_dynamic-slice_fusion), channel_id=1, source_target_pairs={{0,16},{2,18},{4,20},{6,22},{8,24},{10,26},{12,28},{14,30},{16,0},... | collective-permute-start | bytes 196616 | tf_op jit(solution)/shard_map/ppermute | solution.py:405
  25.8 0.0 copy-done
  25.8 0.1 dynamic-slice_bitcast_fusion.gain_ref
  25.9 0.1 broadcast_in_dim.11.offs_ref
  26.0 1.6 %local_forward.1 = (f32[8,8,16,128]{3,2,1,0:T(8,128)S(1)}, f32[8,8,16,128]{3,2,1,0:T(8,128)S(1)}, f32[128,128]{1,0:T(8,128)S(1)}) custom-call(s32[3,128]{1,0:T(4,128)S(1)} %broadcast_in_dim.11.offs_ref, f32[1,128]{1,0:T(1,128)S(1)} %dynamic-slice_bitcast_fusion.gain_ref, bf16[8,4,8,16,128]{4,3,2,1,0:T(8,128)(2,1)S(1)} %bitcast.11), custom_call_target="tpu_custom_call" | custom-call | flops 100000000 | bytes 2164736 | tf_op jit(solution)/shard_map/local_forward/pallas_call | solution.py:391
  27.5 1.6 %collective-permute-done = bf16[8,2,1,16,128]{4,3,2,1,0:T(8,128)(2,1)S(1)} collective-permute-done((bf16[8,2,1,16,128]{4,3,2,1,0:T(8,128)(2,1)S(1)}, bf16[8,2,1,16,128]{4,3,2,1,0:T(8,128)(2,1)S(1)}, u32[]{:S(2)}, u32[]{:S(2)}) %collective-permute-start) | collective-permute-done | bytes 65568 | tf_op jit(solution)/shard_map/ppermute | solution.py:405
  29.1 0.7 %crossing_forward.1 = (bf16[8,8,16,128]{3,2,1,0:T(8,128)(2,1)S(1)}, f32[8,8,16,128]{3,2,1,0:T(8,128)S(1)}, f32[8,32,128]{2,1,0:T(8,128)S(1)}) custom-call(s32[3,128]{1,0:T(4,128)S(1)} %broadcast_in_dim.11.offs_ref, f32[1,128]{1,0:T(1,128)S(1)} %dynamic-slice_bitcast_fusion.gain_ref, bf16[8,4,8,16,128]{4,3,2,1,0:T(8,128)(2,1)S(1)} %bitcast.12, ...), custom_call_target="tpu_custom_call" | custom-call | bytes 3147776 | tf_op jit(solution)/shard_map/crossing_forward/pallas_call | solution.py:391
  29.8 9.4 %all_to_all.15.stats_ref = f32[8,32,128]{2,1,0:T(8,128)S(1)} all-to-all(f32[8,32,128]{2,1,0:T(8,128)S(1)} %get-tuple-element.28), channel_id=1, replica_groups={{0,14,4,12,2,10,8,6},{16,30,20,28,18,26,24,22},{1,15,5,13,3,11,9,7},{17..., dimensions={0} | all-to-all | bytes 262144 | tf_op jit(solution)/shard_map/all_to_all | solution.py:435
  39.2 1.2 %norm_and_crossing.1 = (bf16[8,8,16,128]{3,2,1,0:T(8,128)(2,1)S(1)}, bf16[8,8,16,128]{3,2,1,0:T(8,128)(2,1)S(1)}, f32[8,8,16,128]{3,2,1,0:T(8,128)S(1)}, f32[1,1...) custom-call(s32[3,128]{1,0:T(4,128)S(1)} %broadcast_in_dim.11.offs_ref, ...), custom_call_target="tpu_custom_call" | custom-call | flops 10000000 | bytes 3348992 | tf_op jit(solution)/shard_map/norm_and_crossing/pallas_call | solution.py:391
  40.4 3.0 %collective-permute-start.1 = (bf16[17,16,128]{2,1,0:T(8,128)(2,1)S(1)}, bf16[17,16,128]{2,1,0:T(8,128)(2,1)S(1)}, u32[]{:S(2)}, u32[]{:S(2)}) collective-permute-start(bf16[17,16,128]{2,1,0:T(8,128)(2,1)S(1)} %bitcast.17), channel_id=1, source_target_pairs={{0,16},{2,18},{4,20},{6,22},{8,24},{10,26},{12,28},{14,30},{16,0},... | collective-permute-start | bytes 208904 | tf_op jit(solution)/shard_map/ppermute | solution.py:405
  43.3 1.6 %local_backward.1 = (bf16[8,2,8,16,128]{4,3,2,1,0:T(8,128)(2,1)S(1)}, f32[2,8,8,16,128]{4,3,2,1,0:T(8,128)S(1)}) custom-call(s32[3,128]{1,0:T(4,128)S(1)} %broadcast_in_dim.11.offs_ref, bf16[8,4,8,16,128]{4,3,2,1,0:T(8,128)(2,1)S(1)} %bitcast.14, bf16[8,8,16,128]{3,2,1,0:T(8,128)(2,1)S(1)} %get-tuple-element.29.attended_ref, ...), custom_call_target="tpu_custom_call" | custom-call | flops 300000000 | bytes 4392448 | tf_op jit(solution)/shard_map/local_backward/pallas_call | solution.py:391
  44.9 1.5 %collective-permute-done.1.refs_0_ = bf16[17,16,128]{2,1,0:T(8,128)(2,1)S(1)} collective-permute-done((bf16[17,16,128]{2,1,0:T(8,128)(2,1)S(1)}, bf16[17,16,128]{2,1,0:T(8,128)(2,1)S(1)}, u32[]{:S(2)}, u32[]{:S(2)}) %collective-permute-start.1) | collective-permute-done | bytes 69664 | tf_op jit(solution)/shard_map/ppermute | solution.py:405
  46.4 0.2 pack.1
  46.6 15.9 %all_to_all.16.in_ref = bf16[8,528,128]{2,1,0:T(8,128)(2,1)S(1)} all-to-all(bf16[8,528,128]{2,1,0:T(8,128)(2,1)S(1)} %pack.1), channel_id=1, replica_groups={{0,14,4,12,2,10,8,6},{16,30,20,28,18,26,24,22},{1,15,5,13,3,11,9,7},{17..., dimensions={0} | all-to-all | bytes 2162688 | tf_op jit(solution)/shard_map/all_to_all | solution.py:435
  62.5 0.1 collective-permute-start.2
  62.6 1.2 %join.1 = (bf16[1,128,1024]{2,1,0:T(8,128)(2,1)}, bf16[1,128,1024]{2,1,0:T(8,128)(2,1)}, bf16[1,128,1024]{2,1,0:T(8,128)(2,1)}, bf16[1,128,1024]{2,1,0:T(8,128)(2,1)}) custom-call(bf16[8,528,128]{2,1,0:T(8,128)(2,1)S(1)} %all_to_all.16.in_ref), custom_call_target="tpu_custom_call" | custom-call | flops 100000000 | bytes 2129920 | tf_op jit(solution)/shard_map/join/pallas_call | solution.py:391
  63.7 0.0 collective-permute-done.2
  63.7 0.6 multiply_bitcast_fusion
  (2 shorter events, 0.0 us)
Async XLA Ops:
  0.6 25.2 %copy-start = (f32[1024]{0:T(1024)S(1)}, f32[1024]{0:T(1024)}, u32[]{:S(2)}) copy-start(f32[1024]{0:T(1024)} %param.10) | copy-start | bytes 12292
  3.2 6.3 %copy-start.1 = (s32[3,8]{1,0:T(4,128)S(1)}, s32[3,8]{1,0:T(4,128)}, u32[]{:S(2)}) copy-start(s32[3,8]{1,0:T(4,128)} %param.11) | copy-start | bytes 292
  3.2 19.9 %all-to-all-start = ((bf16[8,4,128,128]{3,2,1,0:T(8,128)(2,1)}), bf16[8,4,128,128]{3,2,1,0:T(8,128)(2,1)S(1)}, u32[]{:S(2)}, u32[]{:S(2)}) async-start(bf16[8,4,128,128]{3,2,1,0:T(8,128)(2,1)} %split.1), calls=%async_computation | async-start | bytes 2097152 | tf_op jit(solution)/shard_map/all_to_all | solution.py:435
  23.2 5.9 %collective-permute-start = (bf16[8,2,1,16,128]{4,3,2,1,0:T(8,128)(2,1)S(1)}, bf16[8,2,1,16,128]{4,3,2,1,0:T(8,128)(2,1)S(1)}, u32[]{:S(2)}, u32[]{:S(2)}) collective-permute-start(bf16[8,2,1,16,128]{4,3,2,1,0:T(8,128)(2,1)S(1)} %constant_dynamic-slice_fusion), channel_id=1, source_target_pairs={{0,16},{2,18},{4,20},{6,22},{8,24},{10,26},{12,28},{14,30},{16,0},... | collective-permute-start | bytes 196616 | tf_op jit(solution)/shard_map/ppermute | solution.py:405
  40.4 6.0 %collective-permute-start.1 = (bf16[17,16,128]{2,1,0:T(8,128)(2,1)S(1)}, bf16[17,16,128]{2,1,0:T(8,128)(2,1)S(1)}, u32[]{:S(2)}, u32[]{:S(2)}) collective-permute-start(bf16[17,16,128]{2,1,0:T(8,128)(2,1)S(1)} %bitcast.17), channel_id=1, source_target_pairs={{0,16},{2,18},{4,20},{6,22},{8,24},{10,26},{12,28},{14,30},{16,0},... | collective-permute-start | bytes 208904 | tf_op jit(solution)/shard_map/ppermute | solution.py:405
  62.5 1.3 %collective-permute-start.2 = (f32[8,128]{1,0:T(8,128)S(1)}, f32[8,128]{1,0:T(8,128)S(1)}, u32[]{:S(2)}, u32[]{:S(2)}) collective-permute-start(f32[8,128]{1,0:T(8,128)S(1)} %convert_reduce_fusion), channel_id=1, source_target_pairs={{0,1},{1,0},{2,3},{3,2},{4,5},{5,4},{6,7},{7,6},{8,9},{9,8},{10,11... | collective-permute-start | bytes 12296 | tf_op jit(solution)/shard_map/ppermute | solution.py:405

commit v6 on v5

--- a/solution.py
+++ b/solution.py
@@ -20,6 +20,7 @@
 TILE = 16
 STAGED = 4
 ORDER = (0, 7, 2, 6, 1, 5, 4, 3)
+FAR_FIRST = (7, 6, 5, 3, 4, 2, 1)
 F32 = jnp.float32
 BF16 = jnp.bfloat16
 
@@ -61,6 +62,34 @@
         moved = dot(order, ref[0], NN).astype(BF16)
         for h in range(group):
             out_ref[h, t] = moved[:, h * hd : (h + 1) * hd]
+
+
+def head_at(order, apart):
+    place = lax.axis_index("ctx") % len(order) ^ apart
+    return sum(order.index(device) * (place == device) for device in range(len(order)))
+
+
+def split_apart_kernel(rate, order, q_ref, k_ref, v_ref, g_ref, *refs):
+    outs, moved_ref = refs[:-1], refs[-1]
+    group, _, tokens, hd = moved_ref.shape
+    change = row_order(tokens, rate, False)
+    for t, ref in enumerate((q_ref, k_ref, v_ref, g_ref)):
+        moved = dot(change, ref[0], NN).astype(BF16)
+        for h in range(group):
+            moved_ref[h, t] = moved[:, h * hd : (h + 1) * hd]
+    for apart, out_ref in enumerate(outs):
+        out_ref[...] = moved_ref[head_at(order, apart)]
+
+
+def collect_kernel(levels, order, offs_ref, *refs):
+    blocks, x_ref, own_refs = refs[: len(order)], refs[len(order)], refs[len(order) + 1 :]
+    for apart, block_ref in enumerate(blocks):
+        spot = head_at(order, apart)
+        x_ref[spot] = block_ref[...]
+        for level, own_ref in zip(levels, own_refs):
+            for i, b in enumerate(level.starts(offs_ref)):
+                for t in range(2):
+                    own_ref[spot, t, i] = block_ref[t + 1, b]
 
 
 class Level:
@@ -175,7 +204,7 @@
     )
 
 
-def forward_kernel(levels, scale, offs_ref, gain_ref, x_ref, o_ref, lse_ref, table_ref):
+def forward_kernel(levels, scale, offs_ref, gain_ref, x_ref, o_ref, attn_ref, lse_ref, table_ref):
     pieces, rate, size, hd = o_ref.shape
     for level, places, query, key, value in all_blocks(levels, offs_ref, x_ref, ()):
         mixed, lse = forward(query, key, value, scale)
@@ -189,7 +218,8 @@
     lane = lax.broadcasted_iota(jnp.int32, (hd, hd), 1)
     table = jnp.zeros((hd, hd), F32)
     for nb in range(pieces):
-        attn = o_ref[nb].reshape(rate * size, hd)
+        attn_ref[nb] = o_ref[nb].astype(BF16)
+        attn = attn_ref[nb].reshape(rate * size, hd)
         grad = x_ref[nb, 3].reshape(rate * size, hd)
         for part in range(per):
             rows = slice(part * hd, (part + 1) * hd)
@@ -198,19 +228,30 @@
     table_ref[...] = table
 
 
-def crossing_forward_kernel(levels, scale, offs_ref, gain_ref, x_ref, o_in, lse_in, table_ref, *refs):
+def crossing_forward_kernel(levels, scale, offs_ref, gain_ref, x_ref, o_in, attn_in, lse_in, table_ref, *refs):
     others, (attn_ref, lse_ref, stats_ref, o_ref, sums_ref) = refs[:-5], refs[-5:]
     pieces, rate, size, hd = o_ref.shape
     per = rate * size // hd
     chunks = pieces * per
     lane = lax.broadcasted_iota(jnp.int32, (size, hd), 1)
-    o_ref[...] = o_in[...]
+    if len(levels) > 1:
+        o_ref[...] = o_in[...]
+        o_in = o_ref
+    attn_ref[...] = attn_in[...]
     lse_ref[...] = lse_in[...]
     sums_ref[...] = table_ref[...]
     for level, places, query, key, value in all_blocks(levels, offs_ref, x_ref, others):
-        merge_into(o_ref, lse_ref, places, *forward(query, key, value, scale))
+        mixed, lse = merge(
+            gather(lambda nb, b: o_in[nb, b], places),
+            gather(lambda nb, b: lse_ref[nb, b], places),
+            *forward(query, key, value, scale),
+        )
+        if len(levels) > 1:
+            put(o_ref, places, mixed)
+        put(attn_ref, places, mixed.astype(BF16))
+        put(lse_ref, places, lse)
         sums = row_sums(
-            gather(lambda nb, b: o_ref[nb, b], places),
+            mixed,
             gather(lambda nb, b: x_ref[nb, 3, b], places),
             gain_ref[...],
         )
@@ -221,7 +262,6 @@
             for i, column in enumerate(sums):
                 table = jnp.where(lane == i * chunks + chunk, column[j * size : (j + 1) * size], table)
             sums_ref[rows, :] = table
-    attn_ref[...] = o_ref[...].astype(BF16)
     turned = sums_ref[...].T[: 4 * chunks]
     for peer in range(stats_ref.shape[0]):
         stats_ref[peer] = turned
@@ -230,8 +270,8 @@
 def norm_kernel(heads, levels, scale, score_scale, offs_ref, x_ref, attn_ref, lse_ref, gain_ref, stats_ref, *refs):
     count = len(levels)
     others, refs = refs[:count], refs[count:]
-    attended_ref, grad_ref, delta_ref, gsum_ref = refs[:4]
-    own_refs, sent_refs = refs[4 : 4 + count], refs[4 + count :]
+    attended_ref, grad_ref, gsum_ref = refs[:3]
+    own_refs, sent_refs = refs[3 : 3 + count], refs[3 + count :]
     pieces, rate, size, hd = attn_ref.shape
     chunks = pieces * rate * size // hd
     per = chunks // pieces
@@ -261,7 +301,6 @@
     picked = [jnp.where(lane == chunk, table, jnp.zeros_like(table)) for chunk in range(chunks)]
     columns = dot(jnp.concatenate(picked, axis=0), picker, NN)
     gsum = jnp.zeros((1, hd), F32)
-    products = []
     shape = (rate, size, hd)
     for nb in range(pieces):
         attn_all = attn_ref[nb].reshape(rate * size, hd).astype(F32)
@@ -278,17 +317,18 @@
             attended.append((normed * gain_ref[...]).astype(BF16))
             grad = (inv_c * (upstream * gain_ref[...] - first_c - normed * second_c)).astype(BF16)
             grads.append(grad)
-            products.append(two_parts(grad.astype(F32) * attn))
             gsum = gsum + jnp.sum(upstream * normed, axis=0, keepdims=True)
         attended_ref[nb] = jnp.concatenate(attended, axis=0).reshape(shape)
         grad_ref[nb] = jnp.concatenate(grads, axis=0).reshape(shape)
-    ones = jnp.ones((2 * hd, hd), BF16)
-    deltas = dot(jnp.concatenate(products, axis=0), ones, NN)
-    for nb in range(pieces):
-        delta_ref[nb] = deltas[nb * rate * size : (nb + 1) * rate * size].reshape(shape)
     gsum_ref[...] = gsum
     blocks = list(all_blocks(levels, offs_ref, x_ref, others))
-    results = backward(blocks, grad_ref, lse_ref, delta_ref, scale, score_scale)
+    deltas = []
+    for _, places, *_ in blocks:
+        grad = gather(lambda nb, b: grad_ref[nb, b], places).astype(F32)
+        attn = gather(lambda nb, b: attn_ref[nb, b], places).astype(F32)
+        delta = jnp.sum(grad * attn, axis=-1, keepdims=True)
+        deltas.append(jnp.broadcast_to(delta, grad.shape))
+    results = backward(blocks, grad_ref, lse_ref, deltas, scale, score_scale)
     for i, parts in enumerate(results):
         own = parts[0].shape[0]
         level, coded = levels[i], three_parts(gsum)
@@ -306,21 +346,20 @@
                     sent_refs[i][e, 2 * steps * level.pieces] = coded.astype(sent_refs[i].dtype)
 
 
-def backward(blocks, grad_ref, lse_ref, delta_ref, scale, score_scale):
-    def wide(ref, places, key):
-        column = gather(lambda nb, b: ref[nb, b], places)
+def backward(blocks, grad_ref, lse_ref, deltas, scale, score_scale):
+    def wide(column, key):
         return jnp.concatenate([column] * (key.shape[0] // column.shape[1]), axis=1)
 
     grads = [gather(lambda nb, b: grad_ref[nb, b], places) for _, places, _, _, _ in blocks]
     scores = [scores_of(query, key, score_scale) for _, _, query, key, _ in blocks]
     prob_grads = [dot(grad, block[4], NT) for grad, block in zip(grads, blocks)]
     probs = [
-        jnp.exp2(score - wide(lse_ref, places, key))
+        jnp.exp2(score - wide(gather(lambda nb, b: lse_ref[nb, b], places), key))
         for score, (_, places, _, key, _) in zip(scores, blocks)
     ]
     score_grads = [
-        (prob * (prob_grad - wide(delta_ref, places, key))).astype(BF16)
-        for prob, prob_grad, (_, places, _, key, _) in zip(probs, prob_grads, blocks)
+        (prob * (prob_grad - wide(delta, block[3]))).astype(BF16)
+        for prob, prob_grad, delta, block in zip(probs, prob_grads, deltas, blocks)
     ]
     queries = [dot(each, block[3], NN) * scale for each, block in zip(score_grads, blocks)]
     keys = [dot(each, block[2], TN) * scale for each, block in zip(score_grads, blocks)]
@@ -328,13 +367,21 @@
     return list(zip(queries, keys, values))
 
 
-def local_kernel(levels, crossing, scale, score_scale, offs_ref, x_ref, attended_ref, grad_ref, lse_ref, delta_ref, *refs):
-    own_refs, (out_ref, kv_ref, dq_ref) = refs[: len(crossing)], refs[len(crossing) :]
+def local_kernel(levels, crossing, scale, score_scale, offs_ref, x_ref, attended_ref, grad_ref, lse_ref, attn_ref, *refs):
+    own_refs, (out_ref, kv_ref, dq_ref, delta_ref) = refs[: len(crossing)], refs[len(crossing) :]
+    pieces, rate, size, hd = dq_ref.shape
+    products = [
+        two_parts((grad_ref[nb].astype(F32) * attn_ref[nb].astype(F32)).reshape(rate * size, hd))
+        for nb in range(pieces)
+    ]
+    sums = dot(jnp.concatenate(products, axis=0), jnp.ones((2 * hd, hd), BF16), NN)
+    delta_ref[...] = sums.reshape(delta_ref.shape)
     accumulators = (dq_ref, kv_ref.at[0], kv_ref.at[1])
     blocks = list(all_blocks(levels, offs_ref, x_ref, ()))
     for low in range(0, len(blocks), STAGED):
         some = blocks[low : low + STAGED]
-        results = backward(some, grad_ref, lse_ref, delta_ref, scale, score_scale)
+        deltas = [gather(lambda nb, b: delta_ref[nb, b], places) for _, places, *_ in some]
+        results = backward(some, grad_ref, lse_ref, deltas, scale, score_scale)
         for i, ref in enumerate(accumulators):
             for (level, places, *_), parts in zip(some, results):
                 (put if level.index == 0 else add)(ref, places, parts[i])
@@ -440,54 +487,79 @@
     offs_rows = jnp.broadcast_to(offs, (offsets.shape[0], hd))
     gain = lax.dynamic_slice(norm_gain, (head * hd,), (hd,))[None]
 
-    (sent,) = call(
-        functools.partial(split_kernel, rate),
-        "split",
-        [queries, key_rows, value_rows, out_grad],
-        [((group, 4, tokens, hd), BF16)],
-        limit=60,
-    )
-    x = exchange(sent)
-    if fold > 1:
-        x = x.reshape(pieces, fold, 4, rate, short, hd).transpose(0, 2, 3, 1, 4, 5)
-    x = x.reshape(pieces, 4, rate, size, hd)
+    alone = ctx_count == 2 * group and dp_count == 2 and size == TILE and len(crossing) == 1
+    alone = alone and group == len(ORDER)
+    if alone:
+        far = call(
+            functools.partial(split_apart_kernel, rate, order),
+            "split",
+            [queries, key_rows, value_rows, out_grad],
+            [((4, tokens, hd), BF16)] * group,
+            scratch=[((group, 4, tokens, hd), BF16)],
+            limit=60,
+        )
+        for apart in FAR_FIRST:
+            pairs = [(source, source ^ apart) for source in range(ctx_count)]
+            far[apart] = lax.ppermute(far[apart], "ctx", pairs)
+        x, *owns = call(
+            functools.partial(collect_kernel, crossing, order),
+            "collect",
+            [offs_rows] + [block.reshape(4, rate, size, hd) for block in far],
+            [((pieces, 4, rate, size, hd), BF16)]
+            + [((pieces, 2, level.count, size, hd), BF16) for level in crossing],
+        )
+    else:
+        (sent,) = call(
+            functools.partial(split_kernel, rate),
+            "split",
+            [queries, key_rows, value_rows, out_grad],
+            [((group, 4, tokens, hd), BF16)],
+            limit=60,
+        )
+        x = exchange(sent)
+        if fold > 1:
+            x = x.reshape(pieces, fold, 4, rate, short, hd).transpose(0, 2, 3, 1, 4, 5)
+        x = x.reshape(pieces, 4, rate, size, hd)
+        owns = []
+        for level in crossing:
+            own = [
+                lax.dynamic_slice(x, (0, 1, b, 0, 0), (pieces, 2, 1, size, hd))
+                for b in level.starts(offs)
+            ]
+            owns.append(jnp.concatenate(own, axis=2))
 
     others = []
-    for level in crossing:
-        own = [
-            lax.dynamic_slice(x, (0, 1, b, 0, 0), (pieces, 2, 1, size, hd))
-            for b in level.starts(offs)
-        ]
-        blocks = [jnp.concatenate(own, axis=2)]
+    for level, own in zip(crossing, owns):
+        blocks = [own]
         for bit in range(level.bits):
             blocks += [flip(block, "ctx", low_bit + bit) for block in blocks]
         others.append(jnp.stack(blocks[1:]))
 
     state = (pieces, rate, size, hd)
     chunks = group * tokens // hd
-    o, lse, table = call(
+    o, attn, lse, table = call(
         functools.partial(forward_kernel, local, score_scale),
         "local_forward",
         [offs_rows, gain, x],
-        [(state, F32), (state, F32), ((hd, hd), F32)],
+        [(state, F32), (state, BF16), (state, F32), ((hd, hd), F32)],
         flops=10**8,
     )
     attn, lse, stats = call(
         functools.partial(crossing_forward_kernel, crossing, score_scale),
         "crossing_forward",
-        [offs_rows, gain, x, o, lse, table] + others,
+        [offs_rows, gain, x, o, attn, lse, table] + others,
         [(state, BF16), (state, F32), ((group, 4 * chunks, hd), F32)],
         scratch=[(state, F32), ((hd, hd), F32)],
     )
     stats = exchange(stats)
-    outs = [(state, BF16), (state, BF16), (state, F32), ((1, hd), F32)]
+    outs = [(state, BF16), (state, BF16), ((1, hd), F32)]
     outs += [((3, pieces * level.count * size, hd), F32) for level in crossing]
     sent_types = [BF16 if level.bits == 1 else F32 for level in crossing]
     outs += [
         ((other.shape[0], 2 * level.pieces * level.count + 1, size, hd), kind)
         for level, other, kind in zip(crossing, others, sent_types)
     ]
-    attended, grad, delta, gsum, *rest = call(
+    attended, grad, gsum, *rest = call(
         functools.partial(norm_kernel, group, crossing, scale, score_scale),
         "norm_and_crossing",
         [offs_rows, x, attn, lse, gain, stats] + others,
@@ -507,7 +579,6 @@
                 for b, c in zip(partial[:half], came)
             ]
         arrived.append(partial[0])
-    alone = ctx_count == 2 * group and dp_count == 2 and size == TILE and len(crossing) == 1
     if not alone:
         for axis, count, first in (("dp", dp_count, 0), ("ctx", ctx_count, low_bit)):
             for bit in range(first, count.bit_length() - 1):
@@ -516,9 +587,9 @@
     main, kv = call(
         functools.partial(local_kernel, local, crossing, scale, score_scale),
         "local_backward",
-        [offs_rows, x, attended, grad, lse, delta] + owns,
+        [offs_rows, x, attended, grad, lse, attn] + owns,
         [((pieces, 2, rate, size, hd), BF16), ((2,) + state, F32)],
-        scratch=[(state, F32)],
+        scratch=[(state, F32)] * 2,
         flops=3 * 10**8,
     )
     (packed,) = call(

time: 64.7 us -> 61.9 us (0.957)
  starting transfers between devices: 12 us -> 17.5 us
  waiting for transfers between devices: 14 us -> 10.3 us
  blocking collectives: 25.3 us -> 22.4 us
  between operations: 2.64 us -> 0.72 us
    ppermute x0 -> x7, starting transfers between devices: none -> 11.9 us  [shards(): far[apart] = lax.ppermute(far[apart], 'ctx', pairs)]
    all_to_all x1 -> x0, waiting for transfers between devices: 10.9 us -> none  [exchange(): lax.all_to_all(value, 'ctx', 0, 0, tiled=True, axis_index_groups=groups)]
    ppermute x0 -> x7, waiting for transfers between devices: none -> 7.73 us  [shards(): far[apart] = lax.ppermute(far[apart], 'ctx', pairs)]
    all_to_all x1 -> x0, starting transfers between devices: 6.32 us -> none  [exchange(): lax.all_to_all(value, 'ctx', 0, 0, tiled=True, axis_index_groups=groups)]
    all_to_all x2, blocking collectives: 25.3 us -> 22.4 us  [exchange(): lax.all_to_all(value, 'ctx', 0, 0, tiled=True, axis_index_groups=groups)]
    unnamed x4 -> x6, local copies, waits for them, and re-layouts: 0.01 us -> 0.92 us
    pallas_call x7 -> x8, Pallas kernels: 8.93 us -> 8.85 us  [call(): pl.pallas_call(body, name=name, in_specs=[VMEM] * len(inputs), out_specs=...]
  transfers between devices with their start and end apart: 4 -> 10, of which waited for: 3 -> 5; matrix products, arithmetic and copies ran while one was open for 1% -> 0% of each run, Pallas kernels for 7% -> 7%
where the time goes in v6:
time: 61.9 us; the launch traced here: 61.6 us
  blocking collectives  22.4 us (36%)
  starting transfers between devices  17.5 us (28%)
  waiting for transfers between devices  10.3 us (17%)
  Pallas kernels  8.85 us (14%)
  local copies, waits for them, and re-layouts  1.24 us (2%)
  between operations  0.72 us (1%)
    all_to_all x2, blocking collectives, exchange(): lax.all_to_all(value, 'ctx', 0, 0, tiled=True, axis_index_groups=groups)  22.4 us
    ppermute x7, starting transfers between devices, shards(): far[apart] = lax.ppermute(far[apart], 'ctx', pairs)  11.9 us
    pallas_call x8, Pallas kernels, call(): pl.pallas_call(body, name=name, in_specs=[VMEM] * len(inputs), out_specs=...  8.85 us
    ppermute x7, waiting for transfers between devices, shards(): far[apart] = lax.ppermute(far[apart], 'ctx', pairs)  7.73 us
    ppermute x3, starting transfers between devices, flip(): return lax.ppermute(value, axis, pairs)  5.56 us
    ppermute x3, waiting for transfers between devices, flip(): return lax.ppermute(value, axis, pairs)  2.55 us
  transfers between devices with their start and end apart: 10, of which 5 were waited for; matrix products, arithmetic and copies ran while one was open for 0% of the time, Pallas kernels for 7%

profile of v6, /device:TPU:0, one launch (start us, length us, event | category | flops | bytes accessed | tf_op | source)
XLA Modules:
  0.0 61.6 jit_solution(13482706083525423138)
XLA Ops:
  0.6 0.0 copy-start
  0.6 0.0 copy-start.2
  0.7 2.6 %split.1 = (bf16[4,128,128]{2,1,0:T(8,128)(2,1)}, bf16[4,128,128]{2,1,0:T(8,128)(2,1)}, bf16[4,128,128]{2,1,0:T(8,128)(2,1)}, bf16[4,128,128]{2,1,0:T(8,128)(2,1...) custom-call(bf16[1,128,1024]{2,1,0:T(8,128)(2,1)} %q_ref.1, ...), custom_call_target="tpu_custom_call" | custom-call | bytes 2097152 | tf_op jit(solution)/shard_map/split/pallas_call | solution.py:438
  3.2 2.9 %collective-permute-start = (bf16[4,128,128]{2,1,0:T(8,128)(2,1)}, bf16[4,128,128]{2,1,0:T(8,128)(2,1)S(1)}, u32[]{:S(2)}, u32[]{:S(2)}) collective-permute-start(bf16[4,128,128]{2,1,0:T(8,128)(2,1)} %get-tuple-element.34), channel_id=1, source_target_pairs={{0,2},{2,0},{4,6},{6,4},{8,10},{10,8},{12,14},{14,12},{16,18},{18,... | collective-permute-start | bytes 393224 | tf_op jit(solution)/shard_map/ppermute | solution.py:503
  6.2 1.5 %collective-permute-start.1 = (bf16[4,128,128]{2,1,0:T(8,128)(2,1)}, bf16[4,128,128]{2,1,0:T(8,128)(2,1)S(1)}, u32[]{:S(2)}, u32[]{:S(2)}) collective-permute-start(bf16[4,128,128]{2,1,0:T(8,128)(2,1)} %get-tuple-element.35), channel_id=1, source_target_pairs={{0,4},{2,6},{4,0},{6,2},{8,12},{10,14},{12,8},{14,10},{16,20},{18,... | collective-permute-start | bytes 393224 | tf_op jit(solution)/shard_map/ppermute | solution.py:503
  7.7 0.0 collective-permute-start.2
  7.7 2.0 %collective-permute-start.3 = (bf16[4,128,128]{2,1,0:T(8,128)(2,1)}, bf16[4,128,128]{2,1,0:T(8,128)(2,1)S(1)}, u32[]{:S(2)}, u32[]{:S(2)}) collective-permute-start(bf16[4,128,128]{2,1,0:T(8,128)(2,1)} %get-tuple-element.37), channel_id=1, source_target_pairs={{0,8},{2,10},{4,12},{6,14},{8,0},{10,2},{12,4},{14,6},{16,24},{18,... | collective-permute-start | bytes 393224 | tf_op jit(solution)/shard_map/ppermute | solution.py:503
  9.7 1.4 %collective-permute-start.4 = (bf16[4,128,128]{2,1,0:T(8,128)(2,1)}, bf16[4,128,128]{2,1,0:T(8,128)(2,1)S(1)}, u32[]{:S(2)}, u32[]{:S(2)}) collective-permute-start(bf16[4,128,128]{2,1,0:T(8,128)(2,1)} %get-tuple-element.38), channel_id=1, source_target_pairs={{0,10},{2,8},{4,14},{6,12},{8,2},{10,0},{12,6},{14,4},{16,26},{18,... | collective-permute-start | bytes 393224 | tf_op jit(solution)/shard_map/ppermute | solution.py:503
  11.1 0.0 collective-permute-done
  11.1 2.5 %collective-permute-start.5 = (bf16[4,128,128]{2,1,0:T(8,128)(2,1)}, bf16[4,128,128]{2,1,0:T(8,128)(2,1)S(1)}, u32[]{:S(2)}, u32[]{:S(2)}) collective-permute-start(bf16[4,128,128]{2,1,0:T(8,128)(2,1)} %get-tuple-element.39), channel_id=1, source_target_pairs={{0,12},{2,14},{4,8},{6,10},{8,4},{10,6},{12,0},{14,2},{16,28},{18,... | collective-permute-start | bytes 393224 | tf_op jit(solution)/shard_map/ppermute | solution.py:503
  13.7 0.0 collective-permute-done.1
  13.7 1.5 %collective-permute-start.6 = (bf16[4,128,128]{2,1,0:T(8,128)(2,1)}, bf16[4,128,128]{2,1,0:T(8,128)(2,1)S(1)}, u32[]{:S(2)}, u32[]{:S(2)}) collective-permute-start(bf16[4,128,128]{2,1,0:T(8,128)(2,1)} %get-tuple-element.40), channel_id=1, source_target_pairs={{0,14},{2,12},{4,10},{6,8},{8,6},{10,4},{12,2},{14,0},{16,30},{18,... | collective-permute-start | bytes 393224 | tf_op jit(solution)/shard_map/ppermute | solution.py:503
  15.2 0.0 copy-done.2
  15.2 0.2 dynamic-slice_reduce_fusion
  15.4 0.0 collective-permute-done.2
  15.4 0.0 collective-permute-done.3
  15.4 3.2 %collective-permute-done.4 = bf16[4,128,128]{2,1,0:T(8,128)(2,1)S(1)} collective-permute-done((bf16[4,128,128]{2,1,0:T(8,128)(2,1)}, bf16[4,128,128]{2,1,0:T(8,128)(2,1)S(1)}, u32[]{:S(2)}, u32[]{:S(2)}) %collective-permute-start.4) | collective-permute-done | bytes 131104 | tf_op jit(solution)/shard_map/ppermute | solution.py:503
  18.6 2.8 %collective-permute-done.5 = bf16[4,128,128]{2,1,0:T(8,128)(2,1)S(1)} collective-permute-done((bf16[4,128,128]{2,1,0:T(8,128)(2,1)}, bf16[4,128,128]{2,1,0:T(8,128)(2,1)S(1)}, u32[]{:S(2)}, u32[]{:S(2)}) %collective-permute-start.5) | collective-permute-done | bytes 131104 | tf_op jit(solution)/shard_map/ppermute | solution.py:503
  21.3 1.8 %collective-permute-done.6 = bf16[4,128,128]{2,1,0:T(8,128)(2,1)S(1)} collective-permute-done((bf16[4,128,128]{2,1,0:T(8,128)(2,1)}, bf16[4,128,128]{2,1,0:T(8,128)(2,1)S(1)}, u32[]{:S(2)}, u32[]{:S(2)}) %collective-permute-start.6) | collective-permute-done | bytes 131104 | tf_op jit(solution)/shard_map/ppermute | solution.py:503
  23.1 0.1 broadcast_in_dim.11.offs_ref
  23.2 0.0 copy-start.1
  23.2 0.9 %copy-done.1 = bf16[4,128,128]{2,1,0:T(8,128)(2,1)S(1)} copy-done((bf16[4,128,128]{2,1,0:T(8,128)(2,1)S(1)}, bf16[4,128,128]{2,1,0:T(8,128)(2,1)}, u32[]{:S(2)}) %copy-start.1) | copy-done | bytes 131096
  24.1 0.1 collect.1
  24.2 2.7 %collective-permute-start.7 = (bf16[8,2,1,16,128]{4,3,1,0,2:T(8,128)(2,1)S(1)}, bf16[8,2,1,16,128]{4,3,1,0,2:T(8,128)(2,1)S(1)}, u32[]{:S(2)}, u32[]{:S(2)}) collective-permute-start(bf16[8,2,1,16,128]{4,3,1,0,2:T(8,128)(2,1)S(1)} %bitcast.26), channel_id=1, source_target_pairs={{0,16},{2,18},{4,20},{6,22},{8,24},{10,26},{12,28},{14,30},{16,0},... | collective-permute-start | bytes 196616 | tf_op jit(solution)/shard_map/ppermute | solution.py:452
  26.8 0.0 copy-done
  26.8 0.1 dynamic-slice_bitcast_fusion.gain_ref
  26.9 1.6 %local_forward.1 = (f32[8,8,16,128]{3,2,1,0:T(8,128)S(1)}, bf16[8,8,16,128]{3,2,1,0:T(8,128)(2,1)S(1)}, f32[8,8,16,128]{3,2,1,0:T(8,128)S(1)}, f32[128,128]{1,0:T(8,128)S(1)}) custom-call(s32[3,128]{1,0:T(4,128)S(1)} %broadcast_in_dim.11.offs_ref, f32[1,128]{1,0:T(1,128)S(1)} %dynamic-slice_bitcast_fusion.gain_ref, ...), custom_call_target="tpu_custom_call" | custom-call | flops 100000000 | bytes 2426880 | tf_op jit(solution)/shard_map/local_forward/pallas_call | solution.py:438
  28.5 0.9 %collective-permute-done.7 = bf16[8,2,1,16,128]{4,3,1,0,2:T(8,128)(2,1)S(1)} collective-permute-done((bf16[8,2,1,16,128]{4,3,1,0,2:T(8,128)(2,1)S(1)}, bf16[8,2,1,16,128]{4,3,1,0,2:T(8,128)(2,1)S(1)}, u32[]{:S(2)}, u32[]{:S(2)}) %collective-permute-start.7) | collective-permute-done | bytes 65568 | tf_op jit(solution)/shard_map/ppermute | solution.py:452
  29.4 0.7 %crossing_forward.1 = (bf16[8,8,16,128]{3,2,1,0:T(8,128)(2,1)S(1)}, f32[8,8,16,128]{3,2,1,0:T(8,128)S(1)}, f32[8,32,128]{2,1,0:T(8,128)S(1)}) custom-call(s32[3,128]{1,0:T(4,128)S(1)} %broadcast_in_dim.11.offs_ref, f32[1,128]{1,0:T(1,128)S(1)} %dynamic-slice_bitcast_fusion.gain_ref, bf16[8,4,8,16,128]{4,3,2,1,0:T(8,128)(2,1)S(1)} %get-tuple-element.41.x_ref, ...), custom_call_target="tpu_custom_call" | custom-call | bytes 3409920 | tf_op jit(solution)/shard_map/crossing_forward/pallas_call | solution.py:438
  30.1 8.8 %all_to_all.10.stats_ref = f32[8,32,128]{2,1,0:T(8,128)S(1)} all-to-all(f32[8,32,128]{2,1,0:T(8,128)S(1)} %get-tuple-element.49), channel_id=1, replica_groups={{0,14,4,12,2,10,8,6},{16,30,20,28,18,26,24,22},{1,15,5,13,3,11,9,7},{17..., dimensions={0} | all-to-all | bytes 262144 | tf_op jit(solution)/shard_map/all_to_all | solution.py:482
  38.9 0.9 %norm_and_crossing.1 = (bf16[8,8,16,128]{3,2,1,0:T(8,128)(2,1)S(1)}, bf16[8,8,16,128]{3,2,1,0:T(8,128)(2,1)S(1)}, f32[1,128]{1,0:T(1,128)S(1)}, f32[3,128,128]{2,1,0:T(8,128)S(1)}, bf16[1,17,16,128]{3,2,1,0:T(8,128)(2,1)S(1)}) custom-call(s32[3,128]{1,0:T(4,128)S(1)} %broadcast_in_dim.11.offs_ref, bf16[8,4,8,16,128]{4,3,2,1,0:T(8,128)(2,1)S(1)} %get-tuple-element.41.x_ref, ...), custom_call_target="tpu_custom_call" | custom-call | flops 10000000 | bytes 2824704 | tf_op jit(solution)/shard_map/norm_and_crossing/pallas_call | solution.py:438
  39.8 2.8 %collective-permute-start.8 = (bf16[17,16,128]{2,1,0:T(8,128)(2,1)S(1)}, bf16[17,16,128]{2,1,0:T(8,128)(2,1)S(1)}, u32[]{:S(2)}, u32[]{:S(2)}) collective-permute-start(bf16[17,16,128]{2,1,0:T(8,128)(2,1)S(1)} %bitcast.25), channel_id=1, source_target_pairs={{0,16},{2,18},{4,20},{6,22},{8,24},{10,26},{12,28},{14,30},{16,0},... | collective-permute-start | bytes 208904 | tf_op jit(solution)/shard_map/ppermute | solution.py:452
  42.6 1.7 %local_backward.1 = (bf16[8,2,8,16,128]{4,3,2,1,0:T(8,128)(2,1)S(1)}, f32[2,8,8,16,128]{4,3,2,1,0:T(8,128)S(1)}) custom-call(s32[3,128]{1,0:T(4,128)S(1)} %broadcast_in_dim.11.offs_ref, bf16[8,4,8,16,128]{4,3,2,1,0:T(8,128)(2,1)S(1)} %get-tuple-element.41.x_ref, bf16[8,8,16,128]{3,2,1,0:T(8,128)(2,1)S(1)} %get-tuple-element.50.attended_ref, ...), custom_call_target="tpu_custom_call" | custom-call | flops 300000000 | bytes 4130304 | tf_op jit(solution)/shard_map/local_backward/pallas_call | solution.py:438
  44.3 1.6 %collective-permute-done.8.refs_0_ = bf16[17,16,128]{2,1,0:T(8,128)(2,1)S(1)} collective-permute-done((bf16[17,16,128]{2,1,0:T(8,128)(2,1)S(1)}, bf16[17,16,128]{2,1,0:T(8,128)(2,1)S(1)}, u32[]{:S(2)}, u32[]{:S(2)}) %collective-permute-start.8) | collective-permute-done | bytes 69664 | tf_op jit(solution)/shard_map/ppermute | solution.py:452
  45.9 0.2 pack.1
  46.1 13.6 %all_to_all.11.in_ref = bf16[8,528,128]{2,1,0:T(8,128)(2,1)S(1)} all-to-all(bf16[8,528,128]{2,1,0:T(8,128)(2,1)S(1)} %pack.1), channel_id=1, replica_groups={{0,14,4,12,2,10,8,6},{16,30,20,28,18,26,24,22},{1,15,5,13,3,11,9,7},{17..., dimensions={0} | all-to-all | bytes 2162688 | tf_op jit(solution)/shard_map/all_to_all | solution.py:482
  59.7 0.1 collective-permute-start.9
  59.8 1.2 %join.1 = (bf16[1,128,1024]{2,1,0:T(8,128)(2,1)}, bf16[1,128,1024]{2,1,0:T(8,128)(2,1)}, bf16[1,128,1024]{2,1,0:T(8,128)(2,1)}, bf16[1,128,1024]{2,1,0:T(8,128)(2,1)}) custom-call(bf16[8,528,128]{2,1,0:T(8,128)(2,1)S(1)} %all_to_all.11.in_ref), custom_call_target="tpu_custom_call" | custom-call | flops 100000000 | bytes 2129920 | tf_op jit(solution)/shard_map/join/pallas_call | solution.py:438
  61.0 0.0 collective-permute-done.9
  61.0 0.6 multiply_bitcast_fusion
  (1 shorter events, 0.0 us)
Async XLA Ops:
  0.6 26.2 %copy-start = (f32[1024]{0:T(1024)S(1)}, f32[1024]{0:T(1024)}, u32[]{:S(2)}) copy-start(f32[1024]{0:T(1024)} %param.10) | copy-start | bytes 12292
  0.6 14.5 %copy-start.2 = (s32[3,8]{1,0:T(4,128)S(1)}, s32[3,8]{1,0:T(4,128)}, u32[]{:S(2)}) copy-start(s32[3,8]{1,0:T(4,128)} %param.11) | copy-start | bytes 292
  3.2 7.9 %collective-permute-start = (bf16[4,128,128]{2,1,0:T(8,128)(2,1)}, bf16[4,128,128]{2,1,0:T(8,128)(2,1)S(1)}, u32[]{:S(2)}, u32[]{:S(2)}) collective-permute-start(bf16[4,128,128]{2,1,0:T(8,128)(2,1)} %get-tuple-element.34), channel_id=1, source_target_pairs={{0,2},{2,0},{4,6},{6,4},{8,10},{10,8},{12,14},{14,12},{16,18},{18,... | collective-permute-start | bytes 393224 | tf_op jit(solution)/shard_map/ppermute | solution.py:503
  6.2 7.5 %collective-permute-start.1 = (bf16[4,128,128]{2,1,0:T(8,128)(2,1)}, bf16[4,128,128]{2,1,0:T(8,128)(2,1)S(1)}, u32[]{:S(2)}, u32[]{:S(2)}) collective-permute-start(bf16[4,128,128]{2,1,0:T(8,128)(2,1)} %get-tuple-element.35), channel_id=1, source_target_pairs={{0,4},{2,6},{4,0},{6,2},{8,12},{10,14},{12,8},{14,10},{16,20},{18,... | collective-permute-start | bytes 393224 | tf_op jit(solution)/shard_map/ppermute | solution.py:503
  7.7 7.7 %collective-permute-start.2 = (bf16[4,128,128]{2,1,0:T(8,128)(2,1)}, bf16[4,128,128]{2,1,0:T(8,128)(2,1)S(1)}, u32[]{:S(2)}, u32[]{:S(2)}) collective-permute-start(bf16[4,128,128]{2,1,0:T(8,128)(2,1)} %get-tuple-element.36), channel_id=1, source_target_pairs={{0,6},{2,4},{4,2},{6,0},{8,14},{10,12},{12,10},{14,8},{16,22},{18,... | collective-permute-start | bytes 393224 | tf_op jit(solution)/shard_map/ppermute | solution.py:503
  7.7 7.7 %collective-permute-start.3 = (bf16[4,128,128]{2,1,0:T(8,128)(2,1)}, bf16[4,128,128]{2,1,0:T(8,128)(2,1)S(1)}, u32[]{:S(2)}, u32[]{:S(2)}) collective-permute-start(bf16[4,128,128]{2,1,0:T(8,128)(2,1)} %get-tuple-element.37), channel_id=1, source_target_pairs={{0,8},{2,10},{4,12},{6,14},{8,0},{10,2},{12,4},{14,6},{16,24},{18,... | collective-permute-start | bytes 393224 | tf_op jit(solution)/shard_map/ppermute | solution.py:503
  9.7 8.8 %collective-permute-start.4 = (bf16[4,128,128]{2,1,0:T(8,128)(2,1)}, bf16[4,128,128]{2,1,0:T(8,128)(2,1)S(1)}, u32[]{:S(2)}, u32[]{:S(2)}) collective-permute-start(bf16[4,128,128]{2,1,0:T(8,128)(2,1)} %get-tuple-element.38), channel_id=1, source_target_pairs={{0,10},{2,8},{4,14},{6,12},{8,2},{10,0},{12,6},{14,4},{16,26},{18,... | collective-permute-start | bytes 393224 | tf_op jit(solution)/shard_map/ppermute | solution.py:503
  11.1 10.2 %collective-permute-start.5 = (bf16[4,128,128]{2,1,0:T(8,128)(2,1)}, bf16[4,128,128]{2,1,0:T(8,128)(2,1)S(1)}, u32[]{:S(2)}, u32[]{:S(2)}) collective-permute-start(bf16[4,128,128]{2,1,0:T(8,128)(2,1)} %get-tuple-element.39), channel_id=1, source_target_pairs={{0,12},{2,14},{4,8},{6,10},{8,4},{10,6},{12,0},{14,2},{16,28},{18,... | collective-permute-start | bytes 393224 | tf_op jit(solution)/shard_map/ppermute | solution.py:503
  13.7 9.4 %collective-permute-start.6 = (bf16[4,128,128]{2,1,0:T(8,128)(2,1)}, bf16[4,128,128]{2,1,0:T(8,128)(2,1)S(1)}, u32[]{:S(2)}, u32[]{:S(2)}) collective-permute-start(bf16[4,128,128]{2,1,0:T(8,128)(2,1)} %get-tuple-element.40), channel_id=1, source_target_pairs={{0,14},{2,12},{4,10},{6,8},{8,6},{10,4},{12,2},{14,0},{16,30},{18,... | collective-permute-start | bytes 393224 | tf_op jit(solution)/shard_map/ppermute | solution.py:503
  23.2 0.9 %copy-start.1 = (bf16[4,128,128]{2,1,0:T(8,128)(2,1)S(1)}, bf16[4,128,128]{2,1,0:T(8,128)(2,1)}, u32[]{:S(2)}) copy-start(bf16[4,128,128]{2,1,0:T(8,128)(2,1)} %get-tuple-element.33) | copy-start | bytes 393220
  24.2 5.2 %collective-permute-start.7 = (bf16[8,2,1,16,128]{4,3,1,0,2:T(8,128)(2,1)S(1)}, bf16[8,2,1,16,128]{4,3,1,0,2:T(8,128)(2,1)S(1)}, u32[]{:S(2)}, u32[]{:S(2)}) collective-permute-start(bf16[8,2,1,16,128]{4,3,1,0,2:T(8,128)(2,1)S(1)} %bitcast.26), channel_id=1, source_target_pairs={{0,16},{2,18},{4,20},{6,22},{8,24},{10,26},{12,28},{14,30},{16,0},... | collective-permute-start | bytes 196616 | tf_op jit(solution)/shard_map/ppermute | solution.py:452
  39.8 6.1 %collective-permute-start.8 = (bf16[17,16,128]{2,1,0:T(8,128)(2,1)S(1)}, bf16[17,16,128]{2,1,0:T(8,128)(2,1)S(1)}, u32[]{:S(2)}, u32[]{:S(2)}) collective-permute-start(bf16[17,16,128]{2,1,0:T(8,128)(2,1)S(1)} %bitcast.25), channel_id=1, source_target_pairs={{0,16},{2,18},{4,20},{6,22},{8,24},{10,26},{12,28},{14,30},{16,0},... | collective-permute-start | bytes 208904 | tf_op jit(solution)/shard_map/ppermute | solution.py:452
  59.7 1.3 %collective-permute-start.9 = (f32[8,128]{1,0:T(8,128)S(1)}, f32[8,128]{1,0:T(8,128)S(1)}, u32[]{:S(2)}, u32[]{:S(2)}) collective-permute-start(f32[8,128]{1,0:T(8,128)S(1)} %convert_reduce_fusion), channel_id=1, source_target_pairs={{0,1},{1,0},{2,3},{3,2},{4,5},{5,4},{6,7},{7,6},{8,9},{9,8},{10,11... | collective-permute-start | bytes 12296 | tf_op jit(solution)/shard_map/ppermute | solution.py:452

commit v7 on v6

--- a/solution.py
+++ b/solution.py
@@ -69,12 +69,12 @@
     return sum(order.index(device) * (place == device) for device in range(len(order)))
 
 
-def split_apart_kernel(rate, order, q_ref, k_ref, v_ref, g_ref, *refs):
+def split_apart_kernel(rate, order, rows_ref, *refs):
     outs, moved_ref = refs[:-1], refs[-1]
     group, _, tokens, hd = moved_ref.shape
     change = row_order(tokens, rate, False)
-    for t, ref in enumerate((q_ref, k_ref, v_ref, g_ref)):
-        moved = dot(change, ref[0], NN).astype(BF16)
+    for t in range(4):
+        moved = dot(change, rows_ref[t], NN).astype(BF16)
         for h in range(group):
             moved_ref[h, t] = moved[:, h * hd : (h + 1) * hd]
     for apart, out_ref in enumerate(outs):
@@ -493,10 +493,9 @@
         far = call(
             functools.partial(split_apart_kernel, rate, order),
             "split",
-            [queries, key_rows, value_rows, out_grad],
+            [jnp.concatenate([queries, key_rows, value_rows, out_grad], axis=0)],
             [((4, tokens, hd), BF16)] * group,
             scratch=[((group, 4, tokens, hd), BF16)],
-            limit=60,
         )
         for apart in FAR_FIRST:
             pairs = [(source, source ^ apart) for source in range(ctx_count)]

time: 61.9 us -> 60.1 us (0.971)
  Pallas kernels: 8.85 us -> 6.77 us
  other arithmetic: 0.61 us -> 1.94 us
  local copies, waits for them, and re-layouts: 1.24 us -> 0.34 us
    pallas_call x8, Pallas kernels: 8.85 us -> 6.77 us  [call(): pl.pallas_call(body, name=name, in_specs=[VMEM] * len(inputs), out_specs=...]
    concatenate x0 -> x1, other arithmetic: none -> 1.32 us  [shards(): jnp.concatenate([queries, key_rows, value_rows, out_grad], axis=0)]
    unnamed x6 -> x4, local copies, waits for them, and re-layouts: 0.92 us -> 0.02 us
where the time goes in v7:
time: 60.1 us; the launch traced here: 59.8 us
  blocking collectives  22.4 us (37%)
  starting transfers between devices  17.3 us (29%)
  waiting for transfers between devices  10.3 us (17%)
  Pallas kernels  6.77 us (11%)
  other arithmetic  1.94 us (3%)
  between operations  0.73 us (1%)
    all_to_all x2, blocking collectives, exchange(): lax.all_to_all(value, 'ctx', 0, 0, tiled=True, axis_index_groups=groups)  22.4 us
    ppermute x7, starting transfers between devices, shards(): far[apart] = lax.ppermute(far[apart], 'ctx', pairs)  11.8 us
    ppermute x7, waiting for transfers between devices, shards(): far[apart] = lax.ppermute(far[apart], 'ctx', pairs)  7.74 us
    pallas_call x8, Pallas kernels, call(): pl.pallas_call(body, name=name, in_specs=[VMEM] * len(inputs), out_specs=...  6.77 us
    ppermute x3, starting transfers between devices, flip(): return lax.ppermute(value, axis, pairs)  5.56 us
    ppermute x3, waiting for transfers between devices, flip(): return lax.ppermute(value, axis, pairs)  2.55 us
    concatenate x1, other arithmetic, shards(): jnp.concatenate([queries, key_rows, value_rows, out_grad], axis=0)  1.32 us
  transfers between devices with their start and end apart: 10, of which 5 were waited for; matrix products, arithmetic and copies ran while one was open for 0% of the time, Pallas kernels for 7%

profile of v7, /device:TPU:0, one launch (start us, length us, event | category | flops | bytes accessed | tf_op | source)
XLA Modules:
  0.0 59.8 jit_solution(10754955413097592637)
XLA Ops:
  0.6 0.0 copy-start
  0.6 1.3 %pad_maximum_fusion.rows_ref = bf16[4,128,1024]{2,1,0:T(8,128)(2,1)S(1)} fusion(bf16[1,128,1024]{2,1,0:T(8,128)(2,1)} %param.9, bf16[1,128,1024]{2,1,0:T(8,128)(2,1)} %param.8, bf16[1,128,1024]{2,1,0:T(8,128)(2,1)} %param.7, bf16[1,128,1024]{2,1,0:T(8,128)(2,1)} %param.6), kind=kLoop, calls=%fused_computation | loop fusion | flops 1572864 | bytes 2097152 | tf_op jit(solution)/shard_map/concatenate | solution.py:496
  2.0 0.0 copy-start.1
  2.0 0.5 split.1
  2.5 3.0 %collective-permute-start = (bf16[4,128,128]{2,1,0:T(8,128)(2,1)S(1)}, bf16[4,128,128]{2,1,0:T(8,128)(2,1)S(1)}, u32[]{:S(2)}, u32[]{:S(2)}) collective-permute-start(bf16[4,128,128]{2,1,0:T(8,128)(2,1)S(1)} %get-tuple-element.34), channel_id=1, source_target_pairs={{0,2},{2,0},{4,6},{6,4},{8,10},{10,8},{12,14},{14,12},{16,18},{18,... | collective-permute-start | bytes 393224 | tf_op jit(solution)/shard_map/ppermute | solution.py:502
  5.5 1.5 %collective-permute-start.1 = (bf16[4,128,128]{2,1,0:T(8,128)(2,1)S(1)}, bf16[4,128,128]{2,1,0:T(8,128)(2,1)S(1)}, u32[]{:S(2)}, u32[]{:S(2)}) collective-permute-start(bf16[4,128,128]{2,1,0:T(8,128)(2,1)S(1)} %get-tuple-element.35), channel_id=1, source_target_pairs={{0,4},{2,6},{4,0},{6,2},{8,12},{10,14},{12,8},{14,10},{16,20},{18,... | collective-permute-start | bytes 393224 | tf_op jit(solution)/shard_map/ppermute | solution.py:502
  7.0 0.0 collective-permute-start.2
  7.0 2.0 %collective-permute-start.3 = (bf16[4,128,128]{2,1,0:T(8,128)(2,1)S(1)}, bf16[4,128,128]{2,1,0:T(8,128)(2,1)S(1)}, u32[]{:S(2)}, u32[]{:S(2)}) collective-permute-start(bf16[4,128,128]{2,1,0:T(8,128)(2,1)S(1)} %get-tuple-element.37), channel_id=1, source_target_pairs={{0,8},{2,10},{4,12},{6,14},{8,0},{10,2},{12,4},{14,6},{16,24},{18,... | collective-permute-start | bytes 393224 | tf_op jit(solution)/shard_map/ppermute | solution.py:502
  9.1 1.4 %collective-permute-start.4 = (bf16[4,128,128]{2,1,0:T(8,128)(2,1)S(1)}, bf16[4,128,128]{2,1,0:T(8,128)(2,1)S(1)}, u32[]{:S(2)}, u32[]{:S(2)}) collective-permute-start(bf16[4,128,128]{2,1,0:T(8,128)(2,1)S(1)} %get-tuple-element.38), channel_id=1, source_target_pairs={{0,10},{2,8},{4,14},{6,12},{8,2},{10,0},{12,6},{14,4},{16,26},{18,... | collective-permute-start | bytes 393224 | tf_op jit(solution)/shard_map/ppermute | solution.py:502
  10.5 0.0 collective-permute-done
  10.5 2.5 %collective-permute-start.5 = (bf16[4,128,128]{2,1,0:T(8,128)(2,1)S(1)}, bf16[4,128,128]{2,1,0:T(8,128)(2,1)S(1)}, u32[]{:S(2)}, u32[]{:S(2)}) collective-permute-start(bf16[4,128,128]{2,1,0:T(8,128)(2,1)S(1)} %get-tuple-element.39), channel_id=1, source_target_pairs={{0,12},{2,14},{4,8},{6,10},{8,4},{10,6},{12,0},{14,2},{16,28},{18,... | collective-permute-start | bytes 393224 | tf_op jit(solution)/shard_map/ppermute | solution.py:502
  13.0 0.0 collective-permute-done.1
  13.0 1.3 %collective-permute-start.6 = (bf16[4,128,128]{2,1,0:T(8,128)(2,1)S(1)}, bf16[4,128,128]{2,1,0:T(8,128)(2,1)S(1)}, u32[]{:S(2)}, u32[]{:S(2)}) collective-permute-start(bf16[4,128,128]{2,1,0:T(8,128)(2,1)S(1)} %get-tuple-element.40), channel_id=1, source_target_pairs={{0,14},{2,12},{4,10},{6,8},{8,6},{10,4},{12,2},{14,0},{16,30},{18,... | collective-permute-start | bytes 393224 | tf_op jit(solution)/shard_map/ppermute | solution.py:502
  14.3 0.0 copy-done.1
  14.3 0.2 dynamic-slice_reduce_fusion
  14.5 0.0 collective-permute-done.2
  14.5 0.0 collective-permute-done.3
  14.5 3.2 %collective-permute-done.4 = bf16[4,128,128]{2,1,0:T(8,128)(2,1)S(1)} collective-permute-done((bf16[4,128,128]{2,1,0:T(8,128)(2,1)S(1)}, bf16[4,128,128]{2,1,0:T(8,128)(2,1)S(1)}, u32[]{:S(2)}, u32[]{:S(2)}) %collective-permute-start.4) | collective-permute-done | bytes 131104 | tf_op jit(solution)/shard_map/ppermute | solution.py:502
  17.7 2.8 %collective-permute-done.5 = bf16[4,128,128]{2,1,0:T(8,128)(2,1)S(1)} collective-permute-done((bf16[4,128,128]{2,1,0:T(8,128)(2,1)S(1)}, bf16[4,128,128]{2,1,0:T(8,128)(2,1)S(1)}, u32[]{:S(2)}, u32[]{:S(2)}) %collective-permute-start.5) | collective-permute-done | bytes 131104 | tf_op jit(solution)/shard_map/ppermute | solution.py:502
  20.4 1.8 %collective-permute-done.6 = bf16[4,128,128]{2,1,0:T(8,128)(2,1)S(1)} collective-permute-done((bf16[4,128,128]{2,1,0:T(8,128)(2,1)S(1)}, bf16[4,128,128]{2,1,0:T(8,128)(2,1)S(1)}, u32[]{:S(2)}, u32[]{:S(2)}) %collective-permute-start.6) | collective-permute-done | bytes 131104 | tf_op jit(solution)/shard_map/ppermute | solution.py:502
  22.2 0.1 broadcast_in_dim.11.offs_ref
  22.3 0.1 collect.1
  22.4 2.7 %collective-permute-start.7 = (bf16[8,2,1,16,128]{4,3,1,0,2:T(8,128)(2,1)S(1)}, bf16[8,2,1,16,128]{4,3,1,0,2:T(8,128)(2,1)S(1)}, u32[]{:S(2)}, u32[]{:S(2)}) collective-permute-start(bf16[8,2,1,16,128]{4,3,1,0,2:T(8,128)(2,1)S(1)} %bitcast.26), channel_id=1, source_target_pairs={{0,16},{2,18},{4,20},{6,22},{8,24},{10,26},{12,28},{14,30},{16,0},... | collective-permute-start | bytes 196616 | tf_op jit(solution)/shard_map/ppermute | solution.py:452
  25.0 0.0 copy-done
  25.1 0.1 dynamic-slice_bitcast_fusion.gain_ref
  25.1 1.6 %local_forward.1 = (f32[8,8,16,128]{3,2,1,0:T(8,128)S(1)}, bf16[8,8,16,128]{3,2,1,0:T(8,128)(2,1)S(1)}, f32[8,8,16,128]{3,2,1,0:T(8,128)S(1)}, f32[128,128]{1,0:T(8,128)S(1)}) custom-call(s32[3,128]{1,0:T(4,128)S(1)} %broadcast_in_dim.11.offs_ref, f32[1,128]{1,0:T(1,128)S(1)} %dynamic-slice_bitcast_fusion.gain_ref, ...), custom_call_target="tpu_custom_call" | custom-call | flops 100000000 | bytes 2426880 | tf_op jit(solution)/shard_map/local_forward/pallas_call | solution.py:438
  26.7 0.9 %collective-permute-done.7 = bf16[8,2,1,16,128]{4,3,1,0,2:T(8,128)(2,1)S(1)} collective-permute-done((bf16[8,2,1,16,128]{4,3,1,0,2:T(8,128)(2,1)S(1)}, bf16[8,2,1,16,128]{4,3,1,0,2:T(8,128)(2,1)S(1)}, u32[]{:S(2)}, u32[]{:S(2)}) %collective-permute-start.7) | collective-permute-done | bytes 65568 | tf_op jit(solution)/shard_map/ppermute | solution.py:452
  27.6 0.7 %crossing_forward.1 = (bf16[8,8,16,128]{3,2,1,0:T(8,128)(2,1)S(1)}, f32[8,8,16,128]{3,2,1,0:T(8,128)S(1)}, f32[8,32,128]{2,1,0:T(8,128)S(1)}) custom-call(s32[3,128]{1,0:T(4,128)S(1)} %broadcast_in_dim.11.offs_ref, f32[1,128]{1,0:T(1,128)S(1)} %dynamic-slice_bitcast_fusion.gain_ref, bf16[8,4,8,16,128]{4,3,2,1,0:T(8,128)(2,1)S(1)} %get-tuple-element.41.x_ref, ...), custom_call_target="tpu_custom_call" | custom-call | bytes 3409920 | tf_op jit(solution)/shard_map/crossing_forward/pallas_call | solution.py:438
  28.3 8.8 %all_to_all.10.stats_ref = f32[8,32,128]{2,1,0:T(8,128)S(1)} all-to-all(f32[8,32,128]{2,1,0:T(8,128)S(1)} %get-tuple-element.49), channel_id=1, replica_groups={{0,14,4,12,2,10,8,6},{16,30,20,28,18,26,24,22},{1,15,5,13,3,11,9,7},{17..., dimensions={0} | all-to-all | bytes 262144 | tf_op jit(solution)/shard_map/all_to_all | solution.py:482
  37.1 0.9 %norm_and_crossing.1 = (bf16[8,8,16,128]{3,2,1,0:T(8,128)(2,1)S(1)}, bf16[8,8,16,128]{3,2,1,0:T(8,128)(2,1)S(1)}, f32[1,128]{1,0:T(1,128)S(1)}, f32[3,128,128]{2,1,0:T(8,128)S(1)}, bf16[1,17,16,128]{3,2,1,0:T(8,128)(2,1)S(1)}) custom-call(s32[3,128]{1,0:T(4,128)S(1)} %broadcast_in_dim.11.offs_ref, bf16[8,4,8,16,128]{4,3,2,1,0:T(8,128)(2,1)S(1)} %get-tuple-element.41.x_ref, ...), custom_call_target="tpu_custom_call" | custom-call | flops 10000000 | bytes 2824704 | tf_op jit(solution)/shard_map/norm_and_crossing/pallas_call | solution.py:438
  38.0 2.8 %collective-permute-start.8 = (bf16[17,16,128]{2,1,0:T(8,128)(2,1)S(1)}, bf16[17,16,128]{2,1,0:T(8,128)(2,1)S(1)}, u32[]{:S(2)}, u32[]{:S(2)}) collective-permute-start(bf16[17,16,128]{2,1,0:T(8,128)(2,1)S(1)} %bitcast.25), channel_id=1, source_target_pairs={{0,16},{2,18},{4,20},{6,22},{8,24},{10,26},{12,28},{14,30},{16,0},... | collective-permute-start | bytes 208904 | tf_op jit(solution)/shard_map/ppermute | solution.py:452
  40.8 1.7 %local_backward.1 = (bf16[8,2,8,16,128]{4,3,2,1,0:T(8,128)(2,1)S(1)}, f32[2,8,8,16,128]{4,3,2,1,0:T(8,128)S(1)}) custom-call(s32[3,128]{1,0:T(4,128)S(1)} %broadcast_in_dim.11.offs_ref, bf16[8,4,8,16,128]{4,3,2,1,0:T(8,128)(2,1)S(1)} %get-tuple-element.41.x_ref, bf16[8,8,16,128]{3,2,1,0:T(8,128)(2,1)S(1)} %get-tuple-element.50.attended_ref, ...), custom_call_target="tpu_custom_call" | custom-call | flops 300000000 | bytes 4130304 | tf_op jit(solution)/shard_map/local_backward/pallas_call | solution.py:438
  42.5 1.6 %collective-permute-done.8.refs_0_ = bf16[17,16,128]{2,1,0:T(8,128)(2,1)S(1)} collective-permute-done((bf16[17,16,128]{2,1,0:T(8,128)(2,1)S(1)}, bf16[17,16,128]{2,1,0:T(8,128)(2,1)S(1)}, u32[]{:S(2)}, u32[]{:S(2)}) %collective-permute-start.8) | collective-permute-done | bytes 69664 | tf_op jit(solution)/shard_map/ppermute | solution.py:452
  44.1 0.2 pack.1
  44.3 13.6 %all_to_all.11.in_ref = bf16[8,528,128]{2,1,0:T(8,128)(2,1)S(1)} all-to-all(bf16[8,528,128]{2,1,0:T(8,128)(2,1)S(1)} %pack.1), channel_id=1, replica_groups={{0,14,4,12,2,10,8,6},{16,30,20,28,18,26,24,22},{1,15,5,13,3,11,9,7},{17..., dimensions={0} | all-to-all | bytes 2162688 | tf_op jit(solution)/shard_map/all_to_all | solution.py:482
  57.9 0.1 collective-permute-start.9
  58.0 1.2 %join.1 = (bf16[1,128,1024]{2,1,0:T(8,128)(2,1)}, bf16[1,128,1024]{2,1,0:T(8,128)(2,1)}, bf16[1,128,1024]{2,1,0:T(8,128)(2,1)}, bf16[1,128,1024]{2,1,0:T(8,128)(2,1)}) custom-call(bf16[8,528,128]{2,1,0:T(8,128)(2,1)S(1)} %all_to_all.11.in_ref), custom_call_target="tpu_custom_call" | custom-call | flops 100000000 | bytes 2129920 | tf_op jit(solution)/shard_map/join/pallas_call | solution.py:438
  59.2 0.0 collective-permute-done.9
  59.2 0.6 multiply_bitcast_fusion
  (1 shorter events, 0.0 us)
Async XLA Ops:
  0.6 24.4 %copy-start = (f32[1024]{0:T(1024)S(1)}, f32[1024]{0:T(1024)}, u32[]{:S(2)}) copy-start(f32[1024]{0:T(1024)} %param.10) | copy-start | bytes 12292
  2.0 12.3 %copy-start.1 = (s32[3,8]{1,0:T(4,128)S(1)}, s32[3,8]{1,0:T(4,128)}, u32[]{:S(2)}) copy-start(s32[3,8]{1,0:T(4,128)} %param.11) | copy-start | bytes 292
  2.5 8.0 %collective-permute-start = (bf16[4,128,128]{2,1,0:T(8,128)(2,1)S(1)}, bf16[4,128,128]{2,1,0:T(8,128)(2,1)S(1)}, u32[]{:S(2)}, u32[]{:S(2)}) collective-permute-start(bf16[4,128,128]{2,1,0:T(8,128)(2,1)S(1)} %get-tuple-element.34), channel_id=1, source_target_pairs={{0,2},{2,0},{4,6},{6,4},{8,10},{10,8},{12,14},{14,12},{16,18},{18,... | collective-permute-start | bytes 393224 | tf_op jit(solution)/shard_map/ppermute | solution.py:502
  5.5 7.5 %collective-permute-start.1 = (bf16[4,128,128]{2,1,0:T(8,128)(2,1)S(1)}, bf16[4,128,128]{2,1,0:T(8,128)(2,1)S(1)}, u32[]{:S(2)}, u32[]{:S(2)}) collective-permute-start(bf16[4,128,128]{2,1,0:T(8,128)(2,1)S(1)} %get-tuple-element.35), channel_id=1, source_target_pairs={{0,4},{2,6},{4,0},{6,2},{8,12},{10,14},{12,8},{14,10},{16,20},{18,... | collective-permute-start | bytes 393224 | tf_op jit(solution)/shard_map/ppermute | solution.py:502
  7.0 7.4 %collective-permute-start.2 = (bf16[4,128,128]{2,1,0:T(8,128)(2,1)S(1)}, bf16[4,128,128]{2,1,0:T(8,128)(2,1)S(1)}, u32[]{:S(2)}, u32[]{:S(2)}) collective-permute-start(bf16[4,128,128]{2,1,0:T(8,128)(2,1)S(1)} %get-tuple-element.36), channel_id=1, source_target_pairs={{0,6},{2,4},{4,2},{6,0},{8,14},{10,12},{12,10},{14,8},{16,22},{18,... | collective-permute-start | bytes 393224 | tf_op jit(solution)/shard_map/ppermute | solution.py:502
  7.0 7.4 %collective-permute-start.3 = (bf16[4,128,128]{2,1,0:T(8,128)(2,1)S(1)}, bf16[4,128,128]{2,1,0:T(8,128)(2,1)S(1)}, u32[]{:S(2)}, u32[]{:S(2)}) collective-permute-start(bf16[4,128,128]{2,1,0:T(8,128)(2,1)S(1)} %get-tuple-element.37), channel_id=1, source_target_pairs={{0,8},{2,10},{4,12},{6,14},{8,0},{10,2},{12,4},{14,6},{16,24},{18,... | collective-permute-start | bytes 393224 | tf_op jit(solution)/shard_map/ppermute | solution.py:502
  9.1 8.6 %collective-permute-start.4 = (bf16[4,128,128]{2,1,0:T(8,128)(2,1)S(1)}, bf16[4,128,128]{2,1,0:T(8,128)(2,1)S(1)}, u32[]{:S(2)}, u32[]{:S(2)}) collective-permute-start(bf16[4,128,128]{2,1,0:T(8,128)(2,1)S(1)} %get-tuple-element.38), channel_id=1, source_target_pairs={{0,10},{2,8},{4,14},{6,12},{8,2},{10,0},{12,6},{14,4},{16,26},{18,... | collective-permute-start | bytes 393224 | tf_op jit(solution)/shard_map/ppermute | solution.py:502
  10.5 10.0 %collective-permute-start.5 = (bf16[4,128,128]{2,1,0:T(8,128)(2,1)S(1)}, bf16[4,128,128]{2,1,0:T(8,128)(2,1)S(1)}, u32[]{:S(2)}, u32[]{:S(2)}) collective-permute-start(bf16[4,128,128]{2,1,0:T(8,128)(2,1)S(1)} %get-tuple-element.39), channel_id=1, source_target_pairs={{0,12},{2,14},{4,8},{6,10},{8,4},{10,6},{12,0},{14,2},{16,28},{18,... | collective-permute-start | bytes 393224 | tf_op jit(solution)/shard_map/ppermute | solution.py:502
  13.0 9.2 %collective-permute-start.6 = (bf16[4,128,128]{2,1,0:T(8,128)(2,1)S(1)}, bf16[4,128,128]{2,1,0:T(8,128)(2,1)S(1)}, u32[]{:S(2)}, u32[]{:S(2)}) collective-permute-start(bf16[4,128,128]{2,1,0:T(8,128)(2,1)S(1)} %get-tuple-element.40), channel_id=1, source_target_pairs={{0,14},{2,12},{4,10},{6,8},{8,6},{10,4},{12,2},{14,0},{16,30},{18,... | collective-permute-start | bytes 393224 | tf_op jit(solution)/shard_map/ppermute | solution.py:502
  22.4 5.2 %collective-permute-start.7 = (bf16[8,2,1,16,128]{4,3,1,0,2:T(8,128)(2,1)S(1)}, bf16[8,2,1,16,128]{4,3,1,0,2:T(8,128)(2,1)S(1)}, u32[]{:S(2)}, u32[]{:S(2)}) collective-permute-start(bf16[8,2,1,16,128]{4,3,1,0,2:T(8,128)(2,1)S(1)} %bitcast.26), channel_id=1, source_target_pairs={{0,16},{2,18},{4,20},{6,22},{8,24},{10,26},{12,28},{14,30},{16,0},... | collective-permute-start | bytes 196616 | tf_op jit(solution)/shard_map/ppermute | solution.py:452
  38.0 6.1 %collective-permute-start.8 = (bf16[17,16,128]{2,1,0:T(8,128)(2,1)S(1)}, bf16[17,16,128]{2,1,0:T(8,128)(2,1)S(1)}, u32[]{:S(2)}, u32[]{:S(2)}) collective-permute-start(bf16[17,16,128]{2,1,0:T(8,128)(2,1)S(1)} %bitcast.25), channel_id=1, source_target_pairs={{0,16},{2,18},{4,20},{6,22},{8,24},{10,26},{12,28},{14,30},{16,0},... | collective-permute-start | bytes 208904 | tf_op jit(solution)/shard_map/ppermute | solution.py:452
  57.9 1.3 %collective-permute-start.9 = (f32[8,128]{1,0:T(8,128)S(1)}, f32[8,128]{1,0:T(8,128)S(1)}, u32[]{:S(2)}, u32[]{:S(2)}) collective-permute-start(f32[8,128]{1,0:T(8,128)S(1)} %convert_reduce_fusion), channel_id=1, source_target_pairs={{0,1},{1,0},{2,3},{3,2},{4,5},{5,4},{6,7},{7,6},{8,9},{9,8},{10,11... | collective-permute-start | bytes 12296 | tf_op jit(solution)/shard_map/ppermute | solution.py:452

commit v8 on v7

--- a/solution.py
+++ b/solution.py
@@ -69,16 +69,13 @@
     return sum(order.index(device) * (place == device) for device in range(len(order)))
 
 
-def split_apart_kernel(rate, order, rows_ref, *refs):
-    outs, moved_ref = refs[:-1], refs[-1]
-    group, _, tokens, hd = moved_ref.shape
+def split_apart_kernel(rate, order, aparts, rows_ref, *outs):
+    _, tokens, hd = outs[0].shape
     change = row_order(tokens, rate, False)
-    for t in range(4):
-        moved = dot(change, rows_ref[t], NN).astype(BF16)
-        for h in range(group):
-            moved_ref[h, t] = moved[:, h * hd : (h + 1) * hd]
-    for apart, out_ref in enumerate(outs):
-        out_ref[...] = moved_ref[head_at(order, apart)]
+    for apart, out_ref in zip(aparts, outs):
+        columns = pl.ds(pl.multiple_of(head_at(order, apart) * hd, hd), hd)
+        for t in range(4):
+            out_ref[t] = dot(change, rows_ref[t, :, columns], NN).astype(BF16)
 
 
 def collect_kernel(levels, order, offs_ref, *refs):
@@ -490,13 +487,17 @@
     alone = ctx_count == 2 * group and dp_count == 2 and size == TILE and len(crossing) == 1
     alone = alone and group == len(ORDER)
     if alone:
-        far = call(
-            functools.partial(split_apart_kernel, rate, order),
-            "split",
-            [jnp.concatenate([queries, key_rows, value_rows, out_grad], axis=0)],
-            [((4, tokens, hd), BF16)] * group,
-            scratch=[((group, 4, tokens, hd), BF16)],
-        )
+        whole = jnp.concatenate([queries, key_rows, value_rows, out_grad], axis=0)
+        far = [None] * group
+        for aparts in (FAR_FIRST + (0,),):
+            made = call(
+                functools.partial(split_apart_kernel, rate, order, aparts),
+                "split",
+                [whole],
+                [((4, tokens, hd), BF16)] * len(aparts),
+            )
+            for apart, block in zip(aparts, made):
+                far[apart] = block
         for apart in FAR_FIRST:
             pairs = [(source, source ^ apart) for source in range(ctx_count)]
             far[apart] = lax.ppermute(far[apart], "ctx", pairs)

time: 60.1 us -> 60 us (level)
  no operation moved by 1% of the time
where the time goes in v8:
time: 60 us; the launch traced here: 59.8 us
  blocking collectives  22.4 us (37%)
  starting transfers between devices  17.3 us (29%)
  waiting for transfers between devices  10.3 us (17%)
  Pallas kernels  6.74 us (11%)
  other arithmetic  1.94 us (3%)
  between operations  0.73 us (1%)
    all_to_all x2, blocking collectives, exchange(): lax.all_to_all(value, 'ctx', 0, 0, tiled=True, axis_index_groups=groups)  22.4 us
    ppermute x7, starting transfers between devices, shards(): far[apart] = lax.ppermute(far[apart], 'ctx', pairs)  11.8 us
    ppermute x7, waiting for transfers between devices, shards(): far[apart] = lax.ppermute(far[apart], 'ctx', pairs)  7.74 us
    pallas_call x8, Pallas kernels, call(): pl.pallas_call(body, name=name, in_specs=[VMEM] * len(inputs), out_specs=...  6.74 us
    ppermute x3, starting transfers between devices, flip(): return lax.ppermute(value, axis, pairs)  5.55 us
    ppermute x3, waiting for transfers between devices, flip(): return lax.ppermute(value, axis, pairs)  2.57 us
    concatenate x1, other arithmetic, shards(): whole = jnp.concatenate([queries, key_rows, value_rows, out_grad], axis=0)  1.32 us
  transfers between devices with their start and end apart: 10, of which 5 were waited for; matrix products, arithmetic and copies ran while one was open for 0% of the time, Pallas kernels for 7%

profile of v8, /device:TPU:0, one launch (start us, length us, event | category | flops | bytes accessed | tf_op | source)
XLA Modules:
  0.0 59.8 jit_solution(3514011253733926561)
XLA Ops:
  0.6 0.0 copy-start
  0.6 1.3 %pad_maximum_fusion.rows_ref = bf16[4,128,1024]{2,1,0:T(8,128)(2,1)S(1)} fusion(bf16[1,128,1024]{2,1,0:T(8,128)(2,1)} %param.9, bf16[1,128,1024]{2,1,0:T(8,128)(2,1)} %param.8, bf16[1,128,1024]{2,1,0:T(8,128)(2,1)} %param.7, bf16[1,128,1024]{2,1,0:T(8,128)(2,1)} %param.6), kind=kLoop, calls=%fused_computation | loop fusion | flops 1572864 | bytes 2097152 | tf_op jit(solution)/shard_map/concatenate | solution.py:490
  2.0 0.0 copy-start.1
  2.0 0.5 split.1
  2.5 3.0 %collective-permute-start = (bf16[4,128,128]{2,1,0:T(8,128)(2,1)S(1)}, bf16[4,128,128]{2,1,0:T(8,128)(2,1)S(1)}, u32[]{:S(2)}, u32[]{:S(2)}) collective-permute-start(bf16[4,128,128]{2,1,0:T(8,128)(2,1)S(1)} %get-tuple-element.34), channel_id=1, source_target_pairs={{0,2},{2,0},{4,6},{6,4},{8,10},{10,8},{12,14},{14,12},{16,18},{18,... | collective-permute-start | bytes 393224 | tf_op jit(solution)/shard_map/ppermute | solution.py:503
  5.5 1.5 %collective-permute-start.1 = (bf16[4,128,128]{2,1,0:T(8,128)(2,1)S(1)}, bf16[4,128,128]{2,1,0:T(8,128)(2,1)S(1)}, u32[]{:S(2)}, u32[]{:S(2)}) collective-permute-start(bf16[4,128,128]{2,1,0:T(8,128)(2,1)S(1)} %get-tuple-element.35), channel_id=1, source_target_pairs={{0,4},{2,6},{4,0},{6,2},{8,12},{10,14},{12,8},{14,10},{16,20},{18,... | collective-permute-start | bytes 393224 | tf_op jit(solution)/shard_map/ppermute | solution.py:503
  7.0 0.0 collective-permute-start.2
  7.0 2.0 %collective-permute-start.3 = (bf16[4,128,128]{2,1,0:T(8,128)(2,1)S(1)}, bf16[4,128,128]{2,1,0:T(8,128)(2,1)S(1)}, u32[]{:S(2)}, u32[]{:S(2)}) collective-permute-start(bf16[4,128,128]{2,1,0:T(8,128)(2,1)S(1)} %get-tuple-element.37), channel_id=1, source_target_pairs={{0,8},{2,10},{4,12},{6,14},{8,0},{10,2},{12,4},{14,6},{16,24},{18,... | collective-permute-start | bytes 393224 | tf_op jit(solution)/shard_map/ppermute | solution.py:503
  9.0 1.4 %collective-permute-start.4 = (bf16[4,128,128]{2,1,0:T(8,128)(2,1)S(1)}, bf16[4,128,128]{2,1,0:T(8,128)(2,1)S(1)}, u32[]{:S(2)}, u32[]{:S(2)}) collective-permute-start(bf16[4,128,128]{2,1,0:T(8,128)(2,1)S(1)} %get-tuple-element.38), channel_id=1, source_target_pairs={{0,10},{2,8},{4,14},{6,12},{8,2},{10,0},{12,6},{14,4},{16,26},{18,... | collective-permute-start | bytes 393224 | tf_op jit(solution)/shard_map/ppermute | solution.py:503
  10.4 0.0 collective-permute-done
  10.4 2.5 %collective-permute-start.5 = (bf16[4,128,128]{2,1,0:T(8,128)(2,1)S(1)}, bf16[4,128,128]{2,1,0:T(8,128)(2,1)S(1)}, u32[]{:S(2)}, u32[]{:S(2)}) collective-permute-start(bf16[4,128,128]{2,1,0:T(8,128)(2,1)S(1)} %get-tuple-element.39), channel_id=1, source_target_pairs={{0,12},{2,14},{4,8},{6,10},{8,4},{10,6},{12,0},{14,2},{16,28},{18,... | collective-permute-start | bytes 393224 | tf_op jit(solution)/shard_map/ppermute | solution.py:503
  13.0 0.0 collective-permute-done.1
  13.0 1.3 %collective-permute-start.6 = (bf16[4,128,128]{2,1,0:T(8,128)(2,1)S(1)}, bf16[4,128,128]{2,1,0:T(8,128)(2,1)S(1)}, u32[]{:S(2)}, u32[]{:S(2)}) collective-permute-start(bf16[4,128,128]{2,1,0:T(8,128)(2,1)S(1)} %get-tuple-element.40), channel_id=1, source_target_pairs={{0,14},{2,12},{4,10},{6,8},{8,6},{10,4},{12,2},{14,0},{16,30},{18,... | collective-permute-start | bytes 393224 | tf_op jit(solution)/shard_map/ppermute | solution.py:503
  14.2 0.0 copy-done.1
  14.2 0.2 dynamic-slice_reduce_fusion
  14.4 0.0 collective-permute-done.2
  14.4 0.0 collective-permute-done.3
  14.4 3.2 %collective-permute-done.4 = bf16[4,128,128]{2,1,0:T(8,128)(2,1)S(1)} collective-permute-done((bf16[4,128,128]{2,1,0:T(8,128)(2,1)S(1)}, bf16[4,128,128]{2,1,0:T(8,128)(2,1)S(1)}, u32[]{:S(2)}, u32[]{:S(2)}) %collective-permute-start.4) | collective-permute-done | bytes 131104 | tf_op jit(solution)/shard_map/ppermute | solution.py:503
  17.6 2.8 %collective-permute-done.5 = bf16[4,128,128]{2,1,0:T(8,128)(2,1)S(1)} collective-permute-done((bf16[4,128,128]{2,1,0:T(8,128)(2,1)S(1)}, bf16[4,128,128]{2,1,0:T(8,128)(2,1)S(1)}, u32[]{:S(2)}, u32[]{:S(2)}) %collective-permute-start.5) | collective-permute-done | bytes 131104 | tf_op jit(solution)/shard_map/ppermute | solution.py:503
  20.4 1.8 %collective-permute-done.6 = bf16[4,128,128]{2,1,0:T(8,128)(2,1)S(1)} collective-permute-done((bf16[4,128,128]{2,1,0:T(8,128)(2,1)S(1)}, bf16[4,128,128]{2,1,0:T(8,128)(2,1)S(1)}, u32[]{:S(2)}, u32[]{:S(2)}) %collective-permute-start.6) | collective-permute-done | bytes 131104 | tf_op jit(solution)/shard_map/ppermute | solution.py:503
  22.2 0.1 broadcast_in_dim.11.offs_ref
  22.2 0.1 collect.1
  22.4 2.6 %collective-permute-start.7 = (bf16[8,2,1,16,128]{4,3,1,0,2:T(8,128)(2,1)S(1)}, bf16[8,2,1,16,128]{4,3,1,0,2:T(8,128)(2,1)S(1)}, u32[]{:S(2)}, u32[]{:S(2)}) collective-permute-start(bf16[8,2,1,16,128]{4,3,1,0,2:T(8,128)(2,1)S(1)} %bitcast.26), channel_id=1, source_target_pairs={{0,16},{2,18},{4,20},{6,22},{8,24},{10,26},{12,28},{14,30},{16,0},... | collective-permute-start | bytes 196616 | tf_op jit(solution)/shard_map/ppermute | solution.py:449
  25.0 0.0 copy-done
  25.0 0.1 dynamic-slice_bitcast_fusion.gain_ref
  25.1 1.6 %local_forward.1 = (f32[8,8,16,128]{3,2,1,0:T(8,128)S(1)}, bf16[8,8,16,128]{3,2,1,0:T(8,128)(2,1)S(1)}, f32[8,8,16,128]{3,2,1,0:T(8,128)S(1)}, f32[128,128]{1,0:T(8,128)S(1)}) custom-call(s32[3,128]{1,0:T(4,128)S(1)} %broadcast_in_dim.11.offs_ref, f32[1,128]{1,0:T(1,128)S(1)} %dynamic-slice_bitcast_fusion.gain_ref, ...), custom_call_target="tpu_custom_call" | custom-call | flops 100000000 | bytes 2426880 | tf_op jit(solution)/shard_map/local_forward/pallas_call | solution.py:435
  26.7 0.9 %collective-permute-done.7 = bf16[8,2,1,16,128]{4,3,1,0,2:T(8,128)(2,1)S(1)} collective-permute-done((bf16[8,2,1,16,128]{4,3,1,0,2:T(8,128)(2,1)S(1)}, bf16[8,2,1,16,128]{4,3,1,0,2:T(8,128)(2,1)S(1)}, u32[]{:S(2)}, u32[]{:S(2)}) %collective-permute-start.7) | collective-permute-done | bytes 65568 | tf_op jit(solution)/shard_map/ppermute | solution.py:449
  27.6 0.7 %crossing_forward.1 = (bf16[8,8,16,128]{3,2,1,0:T(8,128)(2,1)S(1)}, f32[8,8,16,128]{3,2,1,0:T(8,128)S(1)}, f32[8,32,128]{2,1,0:T(8,128)S(1)}) custom-call(s32[3,128]{1,0:T(4,128)S(1)} %broadcast_in_dim.11.offs_ref, f32[1,128]{1,0:T(1,128)S(1)} %dynamic-slice_bitcast_fusion.gain_ref, bf16[8,4,8,16,128]{4,3,2,1,0:T(8,128)(2,1)S(1)} %get-tuple-element.41.x_ref, ...), custom_call_target="tpu_custom_call" | custom-call | bytes 3409920 | tf_op jit(solution)/shard_map/crossing_forward/pallas_call | solution.py:435
  28.3 8.8 %all_to_all.10.stats_ref = f32[8,32,128]{2,1,0:T(8,128)S(1)} all-to-all(f32[8,32,128]{2,1,0:T(8,128)S(1)} %get-tuple-element.49), channel_id=1, replica_groups={{0,14,4,12,2,10,8,6},{16,30,20,28,18,26,24,22},{1,15,5,13,3,11,9,7},{17..., dimensions={0} | all-to-all | bytes 262144 | tf_op jit(solution)/shard_map/all_to_all | solution.py:479
  37.1 0.9 %norm_and_crossing.1 = (bf16[8,8,16,128]{3,2,1,0:T(8,128)(2,1)S(1)}, bf16[8,8,16,128]{3,2,1,0:T(8,128)(2,1)S(1)}, f32[1,128]{1,0:T(1,128)S(1)}, f32[3,128,128]{2,1,0:T(8,128)S(1)}, bf16[1,17,16,128]{3,2,1,0:T(8,128)(2,1)S(1)}) custom-call(s32[3,128]{1,0:T(4,128)S(1)} %broadcast_in_dim.11.offs_ref, bf16[8,4,8,16,128]{4,3,2,1,0:T(8,128)(2,1)S(1)} %get-tuple-element.41.x_ref, ...), custom_call_target="tpu_custom_call" | custom-call | flops 10000000 | bytes 2824704 | tf_op jit(solution)/shard_map/norm_and_crossing/pallas_call | solution.py:435
  38.0 2.8 %collective-permute-start.8 = (bf16[17,16,128]{2,1,0:T(8,128)(2,1)S(1)}, bf16[17,16,128]{2,1,0:T(8,128)(2,1)S(1)}, u32[]{:S(2)}, u32[]{:S(2)}) collective-permute-start(bf16[17,16,128]{2,1,0:T(8,128)(2,1)S(1)} %bitcast.25), channel_id=1, source_target_pairs={{0,16},{2,18},{4,20},{6,22},{8,24},{10,26},{12,28},{14,30},{16,0},... | collective-permute-start | bytes 208904 | tf_op jit(solution)/shard_map/ppermute | solution.py:449
  40.8 1.7 %local_backward.1 = (bf16[8,2,8,16,128]{4,3,2,1,0:T(8,128)(2,1)S(1)}, f32[2,8,8,16,128]{4,3,2,1,0:T(8,128)S(1)}) custom-call(s32[3,128]{1,0:T(4,128)S(1)} %broadcast_in_dim.11.offs_ref, bf16[8,4,8,16,128]{4,3,2,1,0:T(8,128)(2,1)S(1)} %get-tuple-element.41.x_ref, bf16[8,8,16,128]{3,2,1,0:T(8,128)(2,1)S(1)} %get-tuple-element.50.attended_ref, ...), custom_call_target="tpu_custom_call" | custom-call | flops 300000000 | bytes 4130304 | tf_op jit(solution)/shard_map/local_backward/pallas_call | solution.py:435
  42.5 1.6 %collective-permute-done.8.refs_0_ = bf16[17,16,128]{2,1,0:T(8,128)(2,1)S(1)} collective-permute-done((bf16[17,16,128]{2,1,0:T(8,128)(2,1)S(1)}, bf16[17,16,128]{2,1,0:T(8,128)(2,1)S(1)}, u32[]{:S(2)}, u32[]{:S(2)}) %collective-permute-start.8) | collective-permute-done | bytes 69664 | tf_op jit(solution)/shard_map/ppermute | solution.py:449
  44.1 0.2 pack.1
  44.3 13.6 %all_to_all.11.in_ref = bf16[8,528,128]{2,1,0:T(8,128)(2,1)S(1)} all-to-all(bf16[8,528,128]{2,1,0:T(8,128)(2,1)S(1)} %pack.1), channel_id=1, replica_groups={{0,14,4,12,2,10,8,6},{16,30,20,28,18,26,24,22},{1,15,5,13,3,11,9,7},{17..., dimensions={0} | all-to-all | bytes 2162688 | tf_op jit(solution)/shard_map/all_to_all | solution.py:479
  57.9 0.1 collective-permute-start.9
  58.0 1.2 %join.1 = (bf16[1,128,1024]{2,1,0:T(8,128)(2,1)}, bf16[1,128,1024]{2,1,0:T(8,128)(2,1)}, bf16[1,128,1024]{2,1,0:T(8,128)(2,1)}, bf16[1,128,1024]{2,1,0:T(8,128)(2,1)}) custom-call(bf16[8,528,128]{2,1,0:T(8,128)(2,1)S(1)} %all_to_all.11.in_ref), custom_call_target="tpu_custom_call" | custom-call | flops 100000000 | bytes 2129920 | tf_op jit(solution)/shard_map/join/pallas_call | solution.py:435
  59.2 0.0 collective-permute-done.9
  59.2 0.6 multiply_bitcast_fusion
  (1 shorter events, 0.0 us)
Async XLA Ops:
  0.6 24.4 %copy-start = (f32[1024]{0:T(1024)S(1)}, f32[1024]{0:T(1024)}, u32[]{:S(2)}) copy-start(f32[1024]{0:T(1024)} %param.10) | copy-start | bytes 12292
  2.0 12.3 %copy-start.1 = (s32[3,8]{1,0:T(4,128)S(1)}, s32[3,8]{1,0:T(4,128)}, u32[]{:S(2)}) copy-start(s32[3,8]{1,0:T(4,128)} %param.11) | copy-start | bytes 292
  2.5 8.0 %collective-permute-start = (bf16[4,128,128]{2,1,0:T(8,128)(2,1)S(1)}, bf16[4,128,128]{2,1,0:T(8,128)(2,1)S(1)}, u32[]{:S(2)}, u32[]{:S(2)}) collective-permute-start(bf16[4,128,128]{2,1,0:T(8,128)(2,1)S(1)} %get-tuple-element.34), channel_id=1, source_target_pairs={{0,2},{2,0},{4,6},{6,4},{8,10},{10,8},{12,14},{14,12},{16,18},{18,... | collective-permute-start | bytes 393224 | tf_op jit(solution)/shard_map/ppermute | solution.py:503
  5.5 7.5 %collective-permute-start.1 = (bf16[4,128,128]{2,1,0:T(8,128)(2,1)S(1)}, bf16[4,128,128]{2,1,0:T(8,128)(2,1)S(1)}, u32[]{:S(2)}, u32[]{:S(2)}) collective-permute-start(bf16[4,128,128]{2,1,0:T(8,128)(2,1)S(1)} %get-tuple-element.35), channel_id=1, source_target_pairs={{0,4},{2,6},{4,0},{6,2},{8,12},{10,14},{12,8},{14,10},{16,20},{18,... | collective-permute-start | bytes 393224 | tf_op jit(solution)/shard_map/ppermute | solution.py:503
  7.0 7.4 %collective-permute-start.2 = (bf16[4,128,128]{2,1,0:T(8,128)(2,1)S(1)}, bf16[4,128,128]{2,1,0:T(8,128)(2,1)S(1)}, u32[]{:S(2)}, u32[]{:S(2)}) collective-permute-start(bf16[4,128,128]{2,1,0:T(8,128)(2,1)S(1)} %get-tuple-element.36), channel_id=1, source_target_pairs={{0,6},{2,4},{4,2},{6,0},{8,14},{10,12},{12,10},{14,8},{16,22},{18,... | collective-permute-start | bytes 393224 | tf_op jit(solution)/shard_map/ppermute | solution.py:503
  7.0 7.4 %collective-permute-start.3 = (bf16[4,128,128]{2,1,0:T(8,128)(2,1)S(1)}, bf16[4,128,128]{2,1,0:T(8,128)(2,1)S(1)}, u32[]{:S(2)}, u32[]{:S(2)}) collective-permute-start(bf16[4,128,128]{2,1,0:T(8,128)(2,1)S(1)} %get-tuple-element.37), channel_id=1, source_target_pairs={{0,8},{2,10},{4,12},{6,14},{8,0},{10,2},{12,4},{14,6},{16,24},{18,... | collective-permute-start | bytes 393224 | tf_op jit(solution)/shard_map/ppermute | solution.py:503
  9.0 8.6 %collective-permute-start.4 = (bf16[4,128,128]{2,1,0:T(8,128)(2,1)S(1)}, bf16[4,128,128]{2,1,0:T(8,128)(2,1)S(1)}, u32[]{:S(2)}, u32[]{:S(2)}) collective-permute-start(bf16[4,128,128]{2,1,0:T(8,128)(2,1)S(1)} %get-tuple-element.38), channel_id=1, source_target_pairs={{0,10},{2,8},{4,14},{6,12},{8,2},{10,0},{12,6},{14,4},{16,26},{18,... | collective-permute-start | bytes 393224 | tf_op jit(solution)/shard_map/ppermute | solution.py:503
  10.4 10.0 %collective-permute-start.5 = (bf16[4,128,128]{2,1,0:T(8,128)(2,1)S(1)}, bf16[4,128,128]{2,1,0:T(8,128)(2,1)S(1)}, u32[]{:S(2)}, u32[]{:S(2)}) collective-permute-start(bf16[4,128,128]{2,1,0:T(8,128)(2,1)S(1)} %get-tuple-element.39), channel_id=1, source_target_pairs={{0,12},{2,14},{4,8},{6,10},{8,4},{10,6},{12,0},{14,2},{16,28},{18,... | collective-permute-start | bytes 393224 | tf_op jit(solution)/shard_map/ppermute | solution.py:503
  13.0 9.2 %collective-permute-start.6 = (bf16[4,128,128]{2,1,0:T(8,128)(2,1)S(1)}, bf16[4,128,128]{2,1,0:T(8,128)(2,1)S(1)}, u32[]{:S(2)}, u32[]{:S(2)}) collective-permute-start(bf16[4,128,128]{2,1,0:T(8,128)(2,1)S(1)} %get-tuple-element.40), channel_id=1, source_target_pairs={{0,14},{2,12},{4,10},{6,8},{8,6},{10,4},{12,2},{14,0},{16,30},{18,... | collective-permute-start | bytes 393224 | tf_op jit(solution)/shard_map/ppermute | solution.py:503
  22.4 5.2 %collective-permute-start.7 = (bf16[8,2,1,16,128]{4,3,1,0,2:T(8,128)(2,1)S(1)}, bf16[8,2,1,16,128]{4,3,1,0,2:T(8,128)(2,1)S(1)}, u32[]{:S(2)}, u32[]{:S(2)}) collective-permute-start(bf16[8,2,1,16,128]{4,3,1,0,2:T(8,128)(2,1)S(1)} %bitcast.26), channel_id=1, source_target_pairs={{0,16},{2,18},{4,20},{6,22},{8,24},{10,26},{12,28},{14,30},{16,0},... | collective-permute-start | bytes 196616 | tf_op jit(solution)/shard_map/ppermute | solution.py:449
  38.0 6.1 %collective-permute-start.8 = (bf16[17,16,128]{2,1,0:T(8,128)(2,1)S(1)}, bf16[17,16,128]{2,1,0:T(8,128)(2,1)S(1)}, u32[]{:S(2)}, u32[]{:S(2)}) collective-permute-start(bf16[17,16,128]{2,1,0:T(8,128)(2,1)S(1)} %bitcast.25), channel_id=1, source_target_pairs={{0,16},{2,18},{4,20},{6,22},{8,24},{10,26},{12,28},{14,30},{16,0},... | collective-permute-start | bytes 208904 | tf_op jit(solution)/shard_map/ppermute | solution.py:449
  57.9 1.3 %collective-permute-start.9 = (f32[8,128]{1,0:T(8,128)S(1)}, f32[8,128]{1,0:T(8,128)S(1)}, u32[]{:S(2)}, u32[]{:S(2)}) collective-permute-start(f32[8,128]{1,0:T(8,128)S(1)} %convert_reduce_fusion), channel_id=1, source_target_pairs={{0,1},{1,0},{2,3},{3,2},{4,5},{5,4},{6,7},{7,6},{8,9},{9,8},{10,11... | collective-permute-start | bytes 12296 | tf_op jit(solution)/shard_map/ppermute | solution.py:449

commit v9 on v8

--- a/solution.py
+++ b/solution.py
@@ -20,7 +20,7 @@
 TILE = 16
 STAGED = 4
 ORDER = (0, 7, 2, 6, 1, 5, 4, 3)
-FAR_FIRST = (7, 6, 5, 3, 4, 2, 1)
+FAR_FIRST = (4, 7, 6, 5, 3, 2, 1)
 F32 = jnp.float32
 BF16 = jnp.bfloat16
 

time: 60 us -> 60 us (level)
  no operation moved by 1% of the time
where the time goes in v9:
time: 60 us; the launch traced here: 59.8 us
  blocking collectives  22.4 us (37%)
  starting transfers between devices  17.3 us (29%)
  waiting for transfers between devices  10.3 us (17%)
  Pallas kernels  6.71 us (11%)
  other arithmetic  1.94 us (3%)
  between operations  0.73 us (1%)
    all_to_all x2, blocking collectives, exchange(): lax.all_to_all(value, 'ctx', 0, 0, tiled=True, axis_index_groups=groups)  22.4 us
    ppermute x7, starting transfers between devices, shards(): far[apart] = lax.ppermute(far[apart], 'ctx', pairs)  11.8 us
    ppermute x7, waiting for transfers between devices, shards(): far[apart] = lax.ppermute(far[apart], 'ctx', pairs)  7.74 us
    pallas_call x8, Pallas kernels, call(): pl.pallas_call(body, name=name, in_specs=[VMEM] * len(inputs), out_specs=...  6.71 us
    ppermute x3, starting transfers between devices, flip(): return lax.ppermute(value, axis, pairs)  5.55 us
    ppermute x3, waiting for transfers between devices, flip(): return lax.ppermute(value, axis, pairs)  2.58 us
    concatenate x1, other arithmetic, shards(): whole = jnp.concatenate([queries, key_rows, value_rows, out_grad], axis=0)  1.32 us
  transfers between devices with their start and end apart: 10, of which 5 were waited for; matrix products, arithmetic and copies ran while one was open for 0% of the time, Pallas kernels for 7%

profile of v9, /device:TPU:0, one launch (start us, length us, event | category | flops | bytes accessed | tf_op | source)
XLA Modules:
  0.0 59.8 jit_solution(5514011598024977725)
XLA Ops:
  0.6 0.0 copy-start
  0.6 1.3 %pad_maximum_fusion.rows_ref = bf16[4,128,1024]{2,1,0:T(8,128)(2,1)S(1)} fusion(bf16[1,128,1024]{2,1,0:T(8,128)(2,1)} %param.9, bf16[1,128,1024]{2,1,0:T(8,128)(2,1)} %param.8, bf16[1,128,1024]{2,1,0:T(8,128)(2,1)} %param.7, bf16[1,128,1024]{2,1,0:T(8,128)(2,1)} %param.6), kind=kLoop, calls=%fused_computation | loop fusion | flops 1572864 | bytes 2097152 | tf_op jit(solution)/shard_map/concatenate | solution.py:490
  2.0 0.0 copy-start.1
  2.0 0.5 split.1
  2.5 3.0 %collective-permute-start = (bf16[4,128,128]{2,1,0:T(8,128)(2,1)S(1)}, bf16[4,128,128]{2,1,0:T(8,128)(2,1)S(1)}, u32[]{:S(2)}, u32[]{:S(2)}) collective-permute-start(bf16[4,128,128]{2,1,0:T(8,128)(2,1)S(1)} %get-tuple-element.34), channel_id=1, source_target_pairs={{0,2},{2,0},{4,6},{6,4},{8,10},{10,8},{12,14},{14,12},{16,18},{18,... | collective-permute-start | bytes 393224 | tf_op jit(solution)/shard_map/ppermute | solution.py:503
  5.5 1.5 %collective-permute-start.1 = (bf16[4,128,128]{2,1,0:T(8,128)(2,1)S(1)}, bf16[4,128,128]{2,1,0:T(8,128)(2,1)S(1)}, u32[]{:S(2)}, u32[]{:S(2)}) collective-permute-start(bf16[4,128,128]{2,1,0:T(8,128)(2,1)S(1)} %get-tuple-element.35), channel_id=1, source_target_pairs={{0,4},{2,6},{4,0},{6,2},{8,12},{10,14},{12,8},{14,10},{16,20},{18,... | collective-permute-start | bytes 393224 | tf_op jit(solution)/shard_map/ppermute | solution.py:503
  7.0 0.0 collective-permute-start.2
  7.0 2.0 %collective-permute-start.3 = (bf16[4,128,128]{2,1,0:T(8,128)(2,1)S(1)}, bf16[4,128,128]{2,1,0:T(8,128)(2,1)S(1)}, u32[]{:S(2)}, u32[]{:S(2)}) collective-permute-start(bf16[4,128,128]{2,1,0:T(8,128)(2,1)S(1)} %get-tuple-element.37), channel_id=1, source_target_pairs={{0,8},{2,10},{4,12},{6,14},{8,0},{10,2},{12,4},{14,6},{16,24},{18,... | collective-permute-start | bytes 393224 | tf_op jit(solution)/shard_map/ppermute | solution.py:503
  9.0 1.4 %collective-permute-start.4 = (bf16[4,128,128]{2,1,0:T(8,128)(2,1)S(1)}, bf16[4,128,128]{2,1,0:T(8,128)(2,1)S(1)}, u32[]{:S(2)}, u32[]{:S(2)}) collective-permute-start(bf16[4,128,128]{2,1,0:T(8,128)(2,1)S(1)} %get-tuple-element.38), channel_id=1, source_target_pairs={{0,10},{2,8},{4,14},{6,12},{8,2},{10,0},{12,6},{14,4},{16,26},{18,... | collective-permute-start | bytes 393224 | tf_op jit(solution)/shard_map/ppermute | solution.py:503
  10.4 0.0 collective-permute-done
  10.4 2.5 %collective-permute-start.5 = (bf16[4,128,128]{2,1,0:T(8,128)(2,1)S(1)}, bf16[4,128,128]{2,1,0:T(8,128)(2,1)S(1)}, u32[]{:S(2)}, u32[]{:S(2)}) collective-permute-start(bf16[4,128,128]{2,1,0:T(8,128)(2,1)S(1)} %get-tuple-element.39), channel_id=1, source_target_pairs={{0,12},{2,14},{4,8},{6,10},{8,4},{10,6},{12,0},{14,2},{16,28},{18,... | collective-permute-start | bytes 393224 | tf_op jit(solution)/shard_map/ppermute | solution.py:503
  13.0 0.0 collective-permute-done.1
  13.0 1.3 %collective-permute-start.6 = (bf16[4,128,128]{2,1,0:T(8,128)(2,1)S(1)}, bf16[4,128,128]{2,1,0:T(8,128)(2,1)S(1)}, u32[]{:S(2)}, u32[]{:S(2)}) collective-permute-start(bf16[4,128,128]{2,1,0:T(8,128)(2,1)S(1)} %get-tuple-element.40), channel_id=1, source_target_pairs={{0,14},{2,12},{4,10},{6,8},{8,6},{10,4},{12,2},{14,0},{16,30},{18,... | collective-permute-start | bytes 393224 | tf_op jit(solution)/shard_map/ppermute | solution.py:503
  14.2 0.0 copy-done.1
  14.2 0.2 dynamic-slice_reduce_fusion
  14.4 0.0 collective-permute-done.2
  14.4 0.0 collective-permute-done.3
  14.4 3.2 %collective-permute-done.4 = bf16[4,128,128]{2,1,0:T(8,128)(2,1)S(1)} collective-permute-done((bf16[4,128,128]{2,1,0:T(8,128)(2,1)S(1)}, bf16[4,128,128]{2,1,0:T(8,128)(2,1)S(1)}, u32[]{:S(2)}, u32[]{:S(2)}) %collective-permute-start.4) | collective-permute-done | bytes 131104 | tf_op jit(solution)/shard_map/ppermute | solution.py:503
  17.6 2.8 %collective-permute-done.5 = bf16[4,128,128]{2,1,0:T(8,128)(2,1)S(1)} collective-permute-done((bf16[4,128,128]{2,1,0:T(8,128)(2,1)S(1)}, bf16[4,128,128]{2,1,0:T(8,128)(2,1)S(1)}, u32[]{:S(2)}, u32[]{:S(2)}) %collective-permute-start.5) | collective-permute-done | bytes 131104 | tf_op jit(solution)/shard_map/ppermute | solution.py:503
  20.4 1.8 %collective-permute-done.6 = bf16[4,128,128]{2,1,0:T(8,128)(2,1)S(1)} collective-permute-done((bf16[4,128,128]{2,1,0:T(8,128)(2,1)S(1)}, bf16[4,128,128]{2,1,0:T(8,128)(2,1)S(1)}, u32[]{:S(2)}, u32[]{:S(2)}) %collective-permute-start.6) | collective-permute-done | bytes 131104 | tf_op jit(solution)/shard_map/ppermute | solution.py:503
  22.2 0.1 broadcast_in_dim.11.offs_ref
  22.2 0.1 collect.1
  22.4 2.6 %collective-permute-start.7 = (bf16[8,2,1,16,128]{4,3,1,0,2:T(8,128)(2,1)S(1)}, bf16[8,2,1,16,128]{4,3,1,0,2:T(8,128)(2,1)S(1)}, u32[]{:S(2)}, u32[]{:S(2)}) collective-permute-start(bf16[8,2,1,16,128]{4,3,1,0,2:T(8,128)(2,1)S(1)} %bitcast.26), channel_id=1, source_target_pairs={{0,16},{2,18},{4,20},{6,22},{8,24},{10,26},{12,28},{14,30},{16,0},... | collective-permute-start | bytes 196616 | tf_op jit(solution)/shard_map/ppermute | solution.py:449
  25.0 0.0 copy-done
  25.0 0.1 dynamic-slice_bitcast_fusion.gain_ref
  25.1 1.6 %local_forward.1 = (f32[8,8,16,128]{3,2,1,0:T(8,128)S(1)}, bf16[8,8,16,128]{3,2,1,0:T(8,128)(2,1)S(1)}, f32[8,8,16,128]{3,2,1,0:T(8,128)S(1)}, f32[128,128]{1,0:T(8,128)S(1)}) custom-call(s32[3,128]{1,0:T(4,128)S(1)} %broadcast_in_dim.11.offs_ref, f32[1,128]{1,0:T(1,128)S(1)} %dynamic-slice_bitcast_fusion.gain_ref, ...), custom_call_target="tpu_custom_call" | custom-call | flops 100000000 | bytes 2426880 | tf_op jit(solution)/shard_map/local_forward/pallas_call | solution.py:435
  26.7 0.9 %collective-permute-done.7 = bf16[8,2,1,16,128]{4,3,1,0,2:T(8,128)(2,1)S(1)} collective-permute-done((bf16[8,2,1,16,128]{4,3,1,0,2:T(8,128)(2,1)S(1)}, bf16[8,2,1,16,128]{4,3,1,0,2:T(8,128)(2,1)S(1)}, u32[]{:S(2)}, u32[]{:S(2)}) %collective-permute-start.7) | collective-permute-done | bytes 65568 | tf_op jit(solution)/shard_map/ppermute | solution.py:449
  27.6 0.7 %crossing_forward.1 = (bf16[8,8,16,128]{3,2,1,0:T(8,128)(2,1)S(1)}, f32[8,8,16,128]{3,2,1,0:T(8,128)S(1)}, f32[8,32,128]{2,1,0:T(8,128)S(1)}) custom-call(s32[3,128]{1,0:T(4,128)S(1)} %broadcast_in_dim.11.offs_ref, f32[1,128]{1,0:T(1,128)S(1)} %dynamic-slice_bitcast_fusion.gain_ref, bf16[8,4,8,16,128]{4,3,2,1,0:T(8,128)(2,1)S(1)} %get-tuple-element.41.x_ref, ...), custom_call_target="tpu_custom_call" | custom-call | bytes 3409920 | tf_op jit(solution)/shard_map/crossing_forward/pallas_call | solution.py:435
  28.3 8.8 %all_to_all.10.stats_ref = f32[8,32,128]{2,1,0:T(8,128)S(1)} all-to-all(f32[8,32,128]{2,1,0:T(8,128)S(1)} %get-tuple-element.49), channel_id=1, replica_groups={{0,14,4,12,2,10,8,6},{16,30,20,28,18,26,24,22},{1,15,5,13,3,11,9,7},{17..., dimensions={0} | all-to-all | bytes 262144 | tf_op jit(solution)/shard_map/all_to_all | solution.py:479
  37.1 0.9 %norm_and_crossing.1 = (bf16[8,8,16,128]{3,2,1,0:T(8,128)(2,1)S(1)}, bf16[8,8,16,128]{3,2,1,0:T(8,128)(2,1)S(1)}, f32[1,128]{1,0:T(1,128)S(1)}, f32[3,128,128]{2,1,0:T(8,128)S(1)}, bf16[1,17,16,128]{3,2,1,0:T(8,128)(2,1)S(1)}) custom-call(s32[3,128]{1,0:T(4,128)S(1)} %broadcast_in_dim.11.offs_ref, bf16[8,4,8,16,128]{4,3,2,1,0:T(8,128)(2,1)S(1)} %get-tuple-element.41.x_ref, ...), custom_call_target="tpu_custom_call" | custom-call | flops 10000000 | bytes 2824704 | tf_op jit(solution)/shard_map/norm_and_crossing/pallas_call | solution.py:435
  38.0 2.8 %collective-permute-start.8 = (bf16[17,16,128]{2,1,0:T(8,128)(2,1)S(1)}, bf16[17,16,128]{2,1,0:T(8,128)(2,1)S(1)}, u32[]{:S(2)}, u32[]{:S(2)}) collective-permute-start(bf16[17,16,128]{2,1,0:T(8,128)(2,1)S(1)} %bitcast.25), channel_id=1, source_target_pairs={{0,16},{2,18},{4,20},{6,22},{8,24},{10,26},{12,28},{14,30},{16,0},... | collective-permute-start | bytes 208904 | tf_op jit(solution)/shard_map/ppermute | solution.py:449
  40.8 1.7 %local_backward.1 = (bf16[8,2,8,16,128]{4,3,2,1,0:T(8,128)(2,1)S(1)}, f32[2,8,8,16,128]{4,3,2,1,0:T(8,128)S(1)}) custom-call(s32[3,128]{1,0:T(4,128)S(1)} %broadcast_in_dim.11.offs_ref, bf16[8,4,8,16,128]{4,3,2,1,0:T(8,128)(2,1)S(1)} %get-tuple-element.41.x_ref, bf16[8,8,16,128]{3,2,1,0:T(8,128)(2,1)S(1)} %get-tuple-element.50.attended_ref, ...), custom_call_target="tpu_custom_call" | custom-call | flops 300000000 | bytes 4130304 | tf_op jit(solution)/shard_map/local_backward/pallas_call | solution.py:435
  42.5 1.6 %collective-permute-done.8.refs_0_ = bf16[17,16,128]{2,1,0:T(8,128)(2,1)S(1)} collective-permute-done((bf16[17,16,128]{2,1,0:T(8,128)(2,1)S(1)}, bf16[17,16,128]{2,1,0:T(8,128)(2,1)S(1)}, u32[]{:S(2)}, u32[]{:S(2)}) %collective-permute-start.8) | collective-permute-done | bytes 69664 | tf_op jit(solution)/shard_map/ppermute | solution.py:449
  44.1 0.2 pack.1
  44.3 13.6 %all_to_all.11.in_ref = bf16[8,528,128]{2,1,0:T(8,128)(2,1)S(1)} all-to-all(bf16[8,528,128]{2,1,0:T(8,128)(2,1)S(1)} %pack.1), channel_id=1, replica_groups={{0,14,4,12,2,10,8,6},{16,30,20,28,18,26,24,22},{1,15,5,13,3,11,9,7},{17..., dimensions={0} | all-to-all | bytes 2162688 | tf_op jit(solution)/shard_map/all_to_all | solution.py:479
  57.9 0.1 collective-permute-start.9
  58.0 1.2 %join.1 = (bf16[1,128,1024]{2,1,0:T(8,128)(2,1)}, bf16[1,128,1024]{2,1,0:T(8,128)(2,1)}, bf16[1,128,1024]{2,1,0:T(8,128)(2,1)}, bf16[1,128,1024]{2,1,0:T(8,128)(2,1)}) custom-call(bf16[8,528,128]{2,1,0:T(8,128)(2,1)S(1)} %all_to_all.11.in_ref), custom_call_target="tpu_custom_call" | custom-call | flops 100000000 | bytes 2129920 | tf_op jit(solution)/shard_map/join/pallas_call | solution.py:435
  59.2 0.0 collective-permute-done.9
  59.2 0.6 multiply_bitcast_fusion
  (1 shorter events, 0.0 us)
Async XLA Ops:
  0.6 24.4 %copy-start = (f32[1024]{0:T(1024)S(1)}, f32[1024]{0:T(1024)}, u32[]{:S(2)}) copy-start(f32[1024]{0:T(1024)} %param.10) | copy-start | bytes 12292
  2.0 12.3 %copy-start.1 = (s32[3,8]{1,0:T(4,128)S(1)}, s32[3,8]{1,0:T(4,128)}, u32[]{:S(2)}) copy-start(s32[3,8]{1,0:T(4,128)} %param.11) | copy-start | bytes 292
  2.5 8.0 %collective-permute-start = (bf16[4,128,128]{2,1,0:T(8,128)(2,1)S(1)}, bf16[4,128,128]{2,1,0:T(8,128)(2,1)S(1)}, u32[]{:S(2)}, u32[]{:S(2)}) collective-permute-start(bf16[4,128,128]{2,1,0:T(8,128)(2,1)S(1)} %get-tuple-element.34), channel_id=1, source_target_pairs={{0,2},{2,0},{4,6},{6,4},{8,10},{10,8},{12,14},{14,12},{16,18},{18,... | collective-permute-start | bytes 393224 | tf_op jit(solution)/shard_map/ppermute | solution.py:503
  5.5 7.5 %collective-permute-start.1 = (bf16[4,128,128]{2,1,0:T(8,128)(2,1)S(1)}, bf16[4,128,128]{2,1,0:T(8,128)(2,1)S(1)}, u32[]{:S(2)}, u32[]{:S(2)}) collective-permute-start(bf16[4,128,128]{2,1,0:T(8,128)(2,1)S(1)} %get-tuple-element.35), channel_id=1, source_target_pairs={{0,4},{2,6},{4,0},{6,2},{8,12},{10,14},{12,8},{14,10},{16,20},{18,... | collective-permute-start | bytes 393224 | tf_op jit(solution)/shard_map/ppermute | solution.py:503
  7.0 7.4 %collective-permute-start.2 = (bf16[4,128,128]{2,1,0:T(8,128)(2,1)S(1)}, bf16[4,128,128]{2,1,0:T(8,128)(2,1)S(1)}, u32[]{:S(2)}, u32[]{:S(2)}) collective-permute-start(bf16[4,128,128]{2,1,0:T(8,128)(2,1)S(1)} %get-tuple-element.36), channel_id=1, source_target_pairs={{0,6},{2,4},{4,2},{6,0},{8,14},{10,12},{12,10},{14,8},{16,22},{18,... | collective-permute-start | bytes 393224 | tf_op jit(solution)/shard_map/ppermute | solution.py:503
  7.0 7.4 %collective-permute-start.3 = (bf16[4,128,128]{2,1,0:T(8,128)(2,1)S(1)}, bf16[4,128,128]{2,1,0:T(8,128)(2,1)S(1)}, u32[]{:S(2)}, u32[]{:S(2)}) collective-permute-start(bf16[4,128,128]{2,1,0:T(8,128)(2,1)S(1)} %get-tuple-element.37), channel_id=1, source_target_pairs={{0,8},{2,10},{4,12},{6,14},{8,0},{10,2},{12,4},{14,6},{16,24},{18,... | collective-permute-start | bytes 393224 | tf_op jit(solution)/shard_map/ppermute | solution.py:503
  9.0 8.6 %collective-permute-start.4 = (bf16[4,128,128]{2,1,0:T(8,128)(2,1)S(1)}, bf16[4,128,128]{2,1,0:T(8,128)(2,1)S(1)}, u32[]{:S(2)}, u32[]{:S(2)}) collective-permute-start(bf16[4,128,128]{2,1,0:T(8,128)(2,1)S(1)} %get-tuple-element.38), channel_id=1, source_target_pairs={{0,10},{2,8},{4,14},{6,12},{8,2},{10,0},{12,6},{14,4},{16,26},{18,... | collective-permute-start | bytes 393224 | tf_op jit(solution)/shard_map/ppermute | solution.py:503
  10.4 10.0 %collective-permute-start.5 = (bf16[4,128,128]{2,1,0:T(8,128)(2,1)S(1)}, bf16[4,128,128]{2,1,0:T(8,128)(2,1)S(1)}, u32[]{:S(2)}, u32[]{:S(2)}) collective-permute-start(bf16[4,128,128]{2,1,0:T(8,128)(2,1)S(1)} %get-tuple-element.39), channel_id=1, source_target_pairs={{0,12},{2,14},{4,8},{6,10},{8,4},{10,6},{12,0},{14,2},{16,28},{18,... | collective-permute-start | bytes 393224 | tf_op jit(solution)/shard_map/ppermute | solution.py:503
  13.0 9.2 %collective-permute-start.6 = (bf16[4,128,128]{2,1,0:T(8,128)(2,1)S(1)}, bf16[4,128,128]{2,1,0:T(8,128)(2,1)S(1)}, u32[]{:S(2)}, u32[]{:S(2)}) collective-permute-start(bf16[4,128,128]{2,1,0:T(8,128)(2,1)S(1)} %get-tuple-element.40), channel_id=1, source_target_pairs={{0,14},{2,12},{4,10},{6,8},{8,6},{10,4},{12,2},{14,0},{16,30},{18,... | collective-permute-start | bytes 393224 | tf_op jit(solution)/shard_map/ppermute | solution.py:503
  22.4 5.2 %collective-permute-start.7 = (bf16[8,2,1,16,128]{4,3,1,0,2:T(8,128)(2,1)S(1)}, bf16[8,2,1,16,128]{4,3,1,0,2:T(8,128)(2,1)S(1)}, u32[]{:S(2)}, u32[]{:S(2)}) collective-permute-start(bf16[8,2,1,16,128]{4,3,1,0,2:T(8,128)(2,1)S(1)} %bitcast.26), channel_id=1, source_target_pairs={{0,16},{2,18},{4,20},{6,22},{8,24},{10,26},{12,28},{14,30},{16,0},... | collective-permute-start | bytes 196616 | tf_op jit(solution)/shard_map/ppermute | solution.py:449
  38.0 6.1 %collective-permute-start.8 = (bf16[17,16,128]{2,1,0:T(8,128)(2,1)S(1)}, bf16[17,16,128]{2,1,0:T(8,128)(2,1)S(1)}, u32[]{:S(2)}, u32[]{:S(2)}) collective-permute-start(bf16[17,16,128]{2,1,0:T(8,128)(2,1)S(1)} %bitcast.25), channel_id=1, source_target_pairs={{0,16},{2,18},{4,20},{6,22},{8,24},{10,26},{12,28},{14,30},{16,0},... | collective-permute-start | bytes 208904 | tf_op jit(solution)/shard_map/ppermute | solution.py:449
  57.9 1.3 %collective-permute-start.9 = (f32[8,128]{1,0:T(8,128)S(1)}, f32[8,128]{1,0:T(8,128)S(1)}, u32[]{:S(2)}, u32[]{:S(2)}) collective-permute-start(f32[8,128]{1,0:T(8,128)S(1)} %convert_reduce_fusion), channel_id=1, source_target_pairs={{0,1},{1,0},{2,3},{3,2},{4,5},{5,4},{6,7},{7,6},{8,9},{9,8},{10,11... | collective-permute-start | bytes 12296 | tf_op jit(solution)/shard_map/ppermute | solution.py:449
